TPU v7x, 256 devices: a whole 4x4x8 slice. The times are simulated.
256 devices in a mesh: dp: 32 (over y, z_lo, x), mp: 8 (over z_hi, core).
Axes of the slice: x: 4, y: 4, z: 8 (z_hi: 4, z_lo: 2; z = z_hi * 2 + z_lo), core: 2. Of those that a mesh axis runs over, the one named last changes fastest.
Arguments:
- enc_resid: bfloat16 [32, 256, 4096], P(None, 'dp', 'mp'), may hold values from -420 to 420
- enc_gain: float32 [4096], P('mp'), may hold values from 0.5 to 2
- text_in_w: bfloat16 [4096, 3072], P('mp'), may hold values from -0.09375 to 0.09375
- key_w: bfloat16 [3072, 3072], P('dp', 'mp'), may hold values from -0.109375 to 0.109375
- value_w: bfloat16 [3072, 3072], P('dp', 'mp'), may hold values from -0.109375 to 0.109375
- key_gain: float32 [128], replicated, may hold values from 0.5 to 2
- img_query: bfloat16 [24576, 3072], P('dp', 'mp'), may hold values from -24 to 24
- img_keys: bfloat16 [131072, 3072], P('dp', 'mp'), may hold values from -9 to 9
- img_values: bfloat16 [131072, 3072], P('dp', 'mp'), may hold values from -6 to 6
- out_grad: bfloat16 [24576, 3072], P('dp', 'mp'), may hold values from -6 to 6
- cap_lengths: int32 [32], replicated, may hold values from 32 to 256, as said below
- assignment: int32 [32], replicated, may hold values from 0 to 31, each once
Outputs:
- attn_out: float32 [24576, 3072], P('dp', 'mp')
- grad_key: float32 [3072, 3072], P('dp', 'mp')
- grad_value: float32 [3072, 3072], P('dp', 'mp')
Inputs may be any that keep to these rules, and one draw needn't show every extreme that they name: `cap_lengths`: the longest caption fills all 256 positions in every draw.
All inputs are finite; a program needn't handle non-finite values.
Results may differ from a plain program's by a relative error of at most 0.017.
Values may be sent and summed in bfloat16 or wider, within the bound.
No kernel may reach another device: no remote copies, remote signals or barrier semaphores. Data moves between devices by JAX's collectives and lax.ppermute only.
A program may use at most 128 MiB of HBM per device.

v0:
```python
import jax
import jax.numpy as jnp
from jax import lax
from jax.sharding import PartitionSpec as P

D_ENC = 4096


def head_attend(key_pre, value_pre, queries, image_keys, image_values, keep, key_gain):
    scale = queries.shape[-1] ** (-0.5)
    mean_sq = jnp.mean(key_pre * key_pre, axis=-1, keepdims=True)
    text_keys = (key_pre * lax.rsqrt(mean_sq + 1e-06) * key_gain).astype(jnp.bfloat16)
    text_values = value_pre.astype(jnp.bfloat16)
    text_scores = jnp.dot(queries, text_keys.T, preferred_element_type=jnp.float32) * scale
    text_scores = jnp.where(keep[None, :], text_scores, -1e30)
    image_scores = jnp.dot(queries, image_keys.T, preferred_element_type=jnp.float32) * scale
    highest = jnp.maximum(
        jnp.max(text_scores, axis=-1, keepdims=True), jnp.max(image_scores, axis=-1, keepdims=True)
    )
    highest = lax.stop_gradient(highest)
    text_exp = jnp.exp(text_scores - highest)
    image_exp = jnp.exp(image_scores - highest)
    totals = jnp.sum(text_exp, axis=-1, keepdims=True) + jnp.sum(image_exp, axis=-1, keepdims=True)
    text_probs = (text_exp / totals).astype(jnp.bfloat16)
    image_probs = (image_exp / totals).astype(jnp.bfloat16)
    joined = jnp.dot(text_probs, text_values, preferred_element_type=jnp.float32)
    return joined + jnp.dot(image_probs, image_values, preferred_element_type=jnp.float32)


def split_heads(matrix, size):
    return matrix.reshape(matrix.shape[0], -1, size).transpose(1, 0, 2)


def join_heads(stack):
    return stack.transpose(1, 0, 2).reshape(stack.shape[1], -1)


def heads_backward(
    key_pre, value_pre, queries, image_keys, image_values, cotangent, keep, key_gain
):
    size = key_gain.shape[0]

    def one_head(items):
        head_key, head_value, head_query, head_ikeys, head_ivalues, head_cot = items

        def attend(first, second):
            return head_attend(first, second, head_query, head_ikeys, head_ivalues, keep, key_gain)

        joined, pullback = jax.vjp(attend, head_key, head_value)
        key_cot, value_cot = pullback(head_cot.astype(jnp.float32))
        return (joined, key_cot.astype(jnp.bfloat16), value_cot.astype(jnp.bfloat16))

    stacked = (
        split_heads(key_pre, size),
        split_heads(value_pre, size),
        split_heads(queries, size),
        split_heads(image_keys, size),
        split_heads(image_values, size),
        split_heads(cotangent, size),
    )
    outs, key_cots, value_cots = lax.map(one_head, stacked)
    return (join_heads(outs), join_heads(key_cots), join_heads(value_cots))


def reorder(target, blocks):
    moved = jnp.einsum("dc,ctf->dtf", target, blocks, preferred_element_type=jnp.float32)
    return moved.astype(jnp.bfloat16)


def text_features(enc_rows, text_in_w):
    partial_sums = jnp.dot(enc_rows, text_in_w, preferred_element_type=jnp.float32)
    return lax.psum(partial_sums, "mp").astype(jnp.bfloat16)


def body(
    enc_resid,
    enc_gain,
    text_in_w,
    key_w,
    value_w,
    key_gain,
    img_query,
    img_keys,
    img_values,
    out_grad,
    cap_lengths,
    assignment,
):
    values32 = enc_resid.astype(jnp.float32)
    squares = lax.psum(jnp.sum(values32 * values32, axis=-1), "mp")
    scaled = lax.rsqrt(squares / D_ENC + 1e-06)
    normed = (values32 * scaled[..., None] * enc_gain).astype(jnp.bfloat16)
    samples = assignment.shape[0]
    target = (assignment[None, :] == jnp.arange(samples, dtype=jnp.int32)[:, None]).astype(
        jnp.bfloat16
    )
    arrived = lax.all_to_all(reorder(target, normed), "dp", split_axis=0, concat_axis=1, tiled=True)
    text_rows = text_features(arrived[0], text_in_w)
    position = lax.axis_index("dp")
    length = jnp.sum(jnp.where(assignment == position, cap_lengths, 0))
    keep = jnp.arange(text_rows.shape[0], dtype=jnp.int32) < length
    key_piece = lax.all_gather(key_w, "dp", axis=0, tiled=True)
    value_piece = lax.all_gather(value_w, "dp", axis=0, tiled=True)
    columns = text_rows
    key_acc = jnp.dot(columns, key_piece, preferred_element_type=jnp.float32)
    value_acc = jnp.dot(columns, value_piece, preferred_element_type=jnp.float32)
    attn_out, key_cot, value_cot = heads_backward(
        key_acc, value_acc, img_query, img_keys, img_values, out_grad, keep, key_gain
    )
    both_cots = jnp.concatenate([key_cot, value_cot], axis=1)
    columns = text_rows
    summed = lax.psum_scatter(
        lax.dot_general(
            columns, both_cots, (((0,), (0,)), ((), ())), preferred_element_type=jnp.float32
        ),
        "dp",
        scatter_dimension=0,
        tiled=True,
    )
    width = key_w.shape[1]
    return (attn_out, summed[:, :width], summed[:, width:])


def solution(mesh):
    return jax.shard_map(
        body,
        mesh=mesh,
        in_specs=(
            P(None, "dp", "mp"),
            P("mp"),
            P("mp", None),
            P("dp", "mp"),
            P("dp", "mp"),
            P(),
            P("dp", "mp"),
            P("dp", "mp"),
            P("dp", "mp"),
            P("dp", "mp"),
            P(),
            P(),
        ),
        out_specs=(P("dp", "mp"), P("dp", "mp"), P("dp", "mp")),
        check_vma=False,
    )
```

profile of v0, /device:TPU:64, one launch (start us, length us, event | category | flops | bytes accessed | tf_op | source)
XLA Modules:
  0.0 638.9 jit_solution(14650782059511907080)
XLA Ops:
  9.7 28.1 %psum.14 = f32[32,8]{1,0:T(8,128)S(1)} all-reduce(f32[32,8]{1,0:T(8,128)S(1)} %fusion.65), channel_id=1, replica_groups=mesh['dp'=32,'mp'=8] {'mp'}, use_global_device_ids=true, to_apply=%region_1.0 | all-reduce | flops 256 | bytes 2048 | tf_op jit(solution)/shard_map/psum | solution.py:90
  40.7 8.0 %all-to-all-start = ((bf16[32,8,512]{2,1,0:T(8,128)(2,1)}), bf16[32,8,512]{2,1,0:T(8,128)(2,1)S(1)}, u32[]{:S(2)}, u32[]{:S(2)}) async-start(bf16[32,8,512]{2,1,0:T(8,128)(2,1)} %copy.39), calls=%async_computation | async-start | bytes 524288 | tf_op jit(solution)/shard_map/all_to_all | solution.py:97
  48.8 2.1 copy.37
  51.0 2.1 copy.44
  53.1 4.7 copy.41
  57.8 4.8 copy.43
  63.3 2.7 fusion.72
  66.0 87.8 %all-reduce.1 = bf16[256,3072]{1,0:T(8,128)(2,1)} all-reduce(f32[256,3072]{1,0:T(8,128)} %fusion.72), channel_id=1, replica_groups=mesh['dp'=32,'mp'=8] {'mp'}, use_global_device_ids=true, to_apply=%region_2.0 | all-reduce | flops 786432 | bytes 4718592 | tf_op jit(solution)/shard_map/psum | solution.py:72
  153.8 21.6 %all-gather.5.cloned.1.call-done = bf16[3072,384]{1,0:T(8,128)(2,1)} async-done(((bf16[96,384]{1,0:T(8,128)(2,1)}), bf16[3072,384]{1,0:T(8,128)(2,1)}) %all-gather.5.cloned.1.call-update) | async-done | bytes 2359312 | tf_op jit(solution)/shard_map/all_gather | solution.py:103
  175.4 3.9 fusion.87
  179.3 153.6 %all-gather.3.cloned.1.call-done = bf16[3072,384]{1,0:T(8,128)(2,1)} async-done(((bf16[96,384]{1,0:T(8,128)(2,1)}), bf16[3072,384]{1,0:T(8,128)(2,1)}) %all-gather.3.cloned.1.call-update) | async-done | bytes 2359312 | tf_op jit(solution)/shard_map/all_gather | solution.py:102
  332.9 3.9 fusion.88
  336.8 103.3 %while.15 = (s32[]{:T(128)}, f32[3,768,128]{1,2,0:T(8,128)}, bf16[3,256,128]{1,2,0:T(8,128)(2,1)}, bf16[3,256,128]{1,2,0:T(8,128)(2,1)}, bf16[3,768,128]{1,2,0:T...) while((s32[]{:T(128)}, f32[3,768,128]{1,2,0:T(8,128)}, ...), condition=%wide.region_13.14_spmd.clone, body=%wide.region_4.13_spmd.clone.sunk | while | flops 2722269696 | bytes 68405520 | solution.py:61
  341.5 3.5 multiply_reduce_fusion.6
  345.0 2.2 fusion.125
  347.3 5.0 multiply_reduce_fusion.8
  352.3 3.9 fusion.126
  356.2 2.7 multiply_reduce_fusion.7
  359.9 1.9 copy.72
  362.5 2.5 fusion.128
  365.1 1.8 fusion.129
  367.9 1.6 fusion.130
  369.5 1.8 constant_dynamic-update-slice_fusion.3
  374.5 1.4 fusion.123
  375.9 3.5 multiply_reduce_fusion.6
  379.4 2.2 fusion.125
  381.8 5.0 multiply_reduce_fusion.8
  386.7 3.9 fusion.126
  390.6 2.7 multiply_reduce_fusion.7
  394.4 1.9 copy.72
  397.0 2.5 fusion.128
  399.5 1.8 fusion.129
  402.3 1.6 fusion.130
  403.9 1.8 constant_dynamic-update-slice_fusion.3
  410.3 3.5 multiply_reduce_fusion.6
  413.9 2.2 fusion.125
  416.2 5.0 multiply_reduce_fusion.8
  421.2 3.9 fusion.126
  425.1 2.7 multiply_reduce_fusion.7
  428.8 1.9 copy.72
  431.4 2.5 fusion.128
  434.0 1.8 fusion.129
  436.7 1.7 fusion.130
  438.4 1.8 constant_dynamic-update-slice_fusion.3
  440.2 6.5 %fusion.68 = f32[3072,768]{1,0:T(8,128)} fusion(bf16[256,384]{0,1:T(8,128)(2,1)} %bitcast.161, bf16[256,384]{0,1:T(8,128)(2,1)} %bitcast.162, bf16[256,3072]{1,0:T(8,128)(2,1)} %all-reduce.1), kind=kOutput, calls=%fused_computation.95 | convolution fusion | flops 1208745984 | bytes 11403264 | tf_op jit(solution)/shard_map/dot_general | solution.py:113
  446.7 2.7 copy.53
  449.4 181.3 %reduce-scatter.2.cloned.1.call-done = f32[96,768]{1,0:T(8,128)} async-done(((f32[3072,768]{1,0:T(8,128)}), f32[96,768]{1,0:T(8,128)}) %reduce-scatter.2.cloned.1.call-update) | async-done | bytes 294928 | tf_op jit(solution)/shard_map/reduce_scatter | solution.py:112
  630.7 1.7 fusion.86
  (84 shorter events, 27.1 us)
Async XLA Ops:
  7.2 56.1 %copy-start = (bf16[512,3072]{1,0:T(8,128)(2,1)S(1)}, bf16[512,3072]{1,0:T(8,128)(2,1)}, u32[]{:S(2)}) copy-start(bf16[512,3072]{1,0:T(8,128)(2,1)} %param.16) | copy-start | bytes 9437188
  7.2 168.2 %all-gather.5.cloned.1.call-start = ((), (), s32[]{:S(2)}) async-start(), calls=%async_computation.3 | async-start | bytes 2433024 | tf_op jit(solution)/shard_map/all_gather | solution.py:103
  7.9 325.0 %all-gather.3.cloned.1.call-start = ((), (), s32[]{:S(2)}) async-start(), calls=%async_computation.2 | async-start | bytes 2433024 | tf_op jit(solution)/shard_map/all_gather | solution.py:102
  40.7 22.5 %all-to-all-start = ((bf16[32,8,512]{2,1,0:T(8,128)(2,1)}), bf16[32,8,512]{2,1,0:T(8,128)(2,1)S(1)}, u32[]{:S(2)}, u32[]{:S(2)}) async-start(bf16[32,8,512]{2,1,0:T(8,128)(2,1)} %copy.39), calls=%async_computation | async-start | bytes 524288 | tf_op jit(solution)/shard_map/all_to_all | solution.py:97
  48.8 581.9 %reduce-scatter.2.cloned.1.call-start = ((), (), s32[]{:S(2)}) async-start(), calls=%async_computation.4 | async-start | bytes 9732096 | tf_op jit(solution)/shard_map/reduce_scatter | solution.py:112
  57.8 4.8 copy-start.5
  57.8 4.8 copy-start.6
  337.5 7.4 %copy-start.4 = (pred[256]{0:T(512)(128)(4,1)}, pred[256]{0:T(512)(128)(4,1)S(1)}, u32[]{:S(2)}) copy-start(pred[256]{0:T(512)(128)(4,1)S(1)} %iota_compare_fusion.3) | copy-start | bytes 772 | tf_op jit(solution)/shard_map/while
  341.4 14.7 %copy-start.1 = (f32[768,256]{0,1:T(8,128)}, f32[768,256]{0,1:T(8,128)S(1)}, u32[]{:S(2)}) copy-start(f32[768,256]{0,1:T(8,128)S(1)} %get-tuple-element.265) | copy-start | bytes 2359300 | tf_op jit(solution)/shard_map/while
  347.3 8.9 %copy-start.3 = (f32[768]{0:T(1024)}, f32[768]{0:T(1024)S(1)}, u32[]{:S(2)}) copy-start(f32[768]{0:T(1024)S(1)} %get-tuple-element.268) | copy-start | bytes 9220 | tf_op jit(solution)/shard_map/while
  352.3 3.9 copy-start.2
  372.0 7.4 %copy-start.4 = (pred[256]{0:T(512)(128)(4,1)}, pred[256]{0:T(512)(128)(4,1)S(1)}, u32[]{:S(2)}) copy-start(pred[256]{0:T(512)(128)(4,1)S(1)} %iota_compare_fusion.3) | copy-start | bytes 772 | tf_op jit(solution)/shard_map/while
  375.9 14.7 %copy-start.1 = (f32[768,256]{0,1:T(8,128)}, f32[768,256]{0,1:T(8,128)S(1)}, u32[]{:S(2)}) copy-start(f32[768,256]{0,1:T(8,128)S(1)} %get-tuple-element.265) | copy-start | bytes 2359300 | tf_op jit(solution)/shard_map/while
  381.8 8.9 %copy-start.3 = (f32[768]{0:T(1024)}, f32[768]{0:T(1024)S(1)}, u32[]{:S(2)}) copy-start(f32[768]{0:T(1024)S(1)} %get-tuple-element.268) | copy-start | bytes 9220 | tf_op jit(solution)/shard_map/while
  386.7 3.9 copy-start.2
  406.4 7.4 %copy-start.4 = (pred[256]{0:T(512)(128)(4,1)}, pred[256]{0:T(512)(128)(4,1)S(1)}, u32[]{:S(2)}) copy-start(pred[256]{0:T(512)(128)(4,1)S(1)} %iota_compare_fusion.3) | copy-start | bytes 772 | tf_op jit(solution)/shard_map/while
  410.3 14.7 %copy-start.1 = (f32[768,256]{0,1:T(8,128)}, f32[768,256]{0,1:T(8,128)S(1)}, u32[]{:S(2)}) copy-start(f32[768,256]{0,1:T(8,128)S(1)} %get-tuple-element.265) | copy-start | bytes 2359300 | tf_op jit(solution)/shard_map/while
  416.2 8.9 %copy-start.3 = (f32[768]{0:T(1024)}, f32[768]{0:T(1024)S(1)}, u32[]{:S(2)}) copy-start(f32[768]{0:T(1024)S(1)} %get-tuple-element.268) | copy-start | bytes 9220 | tf_op jit(solution)/shard_map/while
  421.2 3.9 copy-start.2
Sparse Core Ops, SparseCore 0:
  9.8 165.5 all-gather.4
  177.2 155.6 all-gather.2
  446.9 183.7 reduce-scatter.1
where the time goes:
time: 641 us; the launch traced here: 639 us
  waiting for transfers between devices  358 us (56%)
  blocking collectives  116 us (18%)
  matrix products  83.3 us (13%)
  local copies, waits for them, and re-layouts  37.6 us (6%)
  other arithmetic  21.8 us (3%)
  between operations  13.8 us (2%)
  starting transfers between devices  8.14 us (1%)
    reduce_scatter x1, waiting for transfers between devices, body(): lax.psum_scatter(lax.dot_general(columns, both_cots, (((0,), (0,)), ((),...  181 us
    all_gather x1, waiting for transfers between devices, body(): key_piece = lax.all_gather(key_w, 'dp', axis=0, tiled=True)  154 us
    psum x1, blocking collectives, text_features(): return lax.psum(partial_sums, 'mp').astype(jnp.bfloat16)  87.8 us
    psum x1, blocking collectives, body(): squares = lax.psum(jnp.sum(values32 * values32, axis=-1), 'mp')  28.1 us
    dot_general x6, matrix products, head_attend(): jnp.dot(image_probs, image_values, preferred_element_type=jnp.float32)  26.5 us
    all_gather x1, waiting for transfers between devices, body(): value_piece = lax.all_gather(value_w, 'dp', axis=0, tiled=True)  21.6 us
    dot_general x9, matrix products, head_attend(): jnp.dot(text_probs, text_values, preferred_element_type=jnp.float32)  16.7 us
    unnamed x11, local copies, waits for them, and re-layouts  16.4 us
  transfers between devices with their start and end apart: 4, of which 3 were waited for; matrix products, arithmetic and copies ran while one was open for 4% of the time, Pallas kernels for 0%

commit v1 on v0

v1 whole, which is shorter than its diff:
```python
import functools
import math

import jax
import jax.numpy as jnp
from jax import lax
from jax.experimental import pallas as pl
from jax.experimental.pallas import tpu as pltpu
from jax.sharding import Mesh, PartitionSpec as P

BF16 = jnp.bfloat16
F32 = jnp.float32

D_ENC = 4096
D = 3072
HD = 128
CT = 256
IQ = 768
IK = 4096
SAMPLES = 32
NY, NZL, NX, NZH, NC = 4, 2, 4, 4, 2
TOK = CT // SAMPLES
FEAT = D_ENC // (NZH * NC)
COLS = D // (NZH * NC)
HEADS = COLS // HD
CHUNK = D // NY
HALF = CHUNK // NC
GROUP = NZL * NX
EXTRA = 128
WIDE = NY * HALF + EXTRA
SCALE = HD ** (-0.5)
LOG2E = math.log2(math.e)
NT = (((1,), (1,)), ((), ()))
TN = (((0,), (0,)), ((), ()))
VMEM_LIMIT = 56 * 2**20


def params():
    return pltpu.CompilerParams(vmem_limit_bytes=VMEM_LIMIT)


def dot(a, b, dims=(((1,), (0,)), ((), ()))):
    return lax.dot_general(a, b, dims, preferred_element_type=F32)


def hi_lo(total, width):
    hi = total.astype(BF16)
    lo = (total - hi.astype(F32)).astype(BF16)
    lane = lax.broadcasted_iota(jnp.int32, (total.shape[0], width), 1)
    wide_hi = jnp.broadcast_to(hi.astype(F32), lane.shape)
    wide_lo = jnp.broadcast_to(lo.astype(F32), lane.shape)
    return jnp.where(lane == 0, wide_hi, jnp.where(lane == 1, wide_lo, 0.0)).astype(BF16)


def front_kernel(core_ref, assign_ref, x_ref, gain_ref, w_ref, send_ref, keep_ref, rows):
    step = pl.program_id(0)

    @pl.when(step == 0)
    def _():
        gain = gain_ref[...]
        for c in range(SAMPLES):
            start = pl.multiple_of(assign_ref[c] * TOK, TOK)
            values = x_ref[c].astype(F32)
            squares = jnp.sum(values * values, axis=1, keepdims=True)
            rows[pl.ds(start, TOK), :FEAT] = values * gain
            rows[pl.ds(start, TOK), FEAT:] = jnp.broadcast_to(squares, (TOK, EXTRA))
        total = rows[:, FEAT : FEAT + 1]
        send_ref[:, NY * HALF :] = hi_lo(total, EXTRA)
        lane = lax.broadcasted_iota(jnp.int32, (CT, EXTRA), 1)
        keep_ref[:, NY * HALF :] = jnp.where(lane == 0, rows[:, FEAT:], 0.0)

    part = dot(rows[:, :FEAT].astype(BF16), w_ref[...])
    for j in range(NY):

        @pl.when(step == j)
        def _():
            send_ref[:, j * HALF : (j + 1) * HALF] = part.astype(BF16)

        @pl.when(step == NY + j)
        def _():
            keep_ref[:, j * HALF : (j + 1) * HALF] = part


def front(core, assignment, x, gain, w):
    def column(i, core_ref, assign_ref):
        half = jnp.where(i < NY, 1 - core_ref[0], core_ref[0])
        return (0, (i % NY) * NC + half)

    whole = lambda *zeros: lambda i, *_: zeros
    return pl.pallas_call(
        front_kernel,
        grid_spec=pltpu.PrefetchScalarGridSpec(
            num_scalar_prefetch=2,
            grid=(NY * NC,),
            in_specs=[
                pl.BlockSpec((SAMPLES, TOK, FEAT), whole(0, 0, 0)),
                pl.BlockSpec((1, FEAT), whole(0, 0)),
                pl.BlockSpec((FEAT, HALF), column),
            ],
            out_specs=[
                pl.BlockSpec((CT, WIDE), whole(0, 0)),
                pl.BlockSpec((CT, WIDE), whole(0, 0)),
            ],
            scratch_shapes=[pltpu.VMEM((CT, FEAT + EXTRA), F32)],
        ),
        out_shape=[
            jax.ShapeDtypeStruct((CT, WIDE), BF16),
            jax.ShapeDtypeStruct((CT, WIDE), F32),
        ],
        compiler_params=params(),
        name="text_partial",
    )(core, assignment, x, gain, w)


def core_sum_kernel(keep_ref, got_ref, out_ref):
    total = keep_ref[...] + got_ref[...].astype(F32)
    edge = NY * HALF
    squares = jnp.sum(total[:, edge:], axis=1, keepdims=True)
    out_ref[:, :edge] = total[:, :edge].astype(BF16)
    out_ref[:, edge:] = hi_lo(squares, EXTRA)


def core_sum(keep, got):
    return pl.pallas_call(
        core_sum_kernel,
        out_shape=jax.ShapeDtypeStruct((CT, WIDE), BF16),
        compiler_params=params(),
        name="core_sum",
    )(keep, got)


def text_kernel(got_ref, out_ref):
    total = got_ref[0].astype(F32)
    for i in range(1, NZH):
        total = total + got_ref[i].astype(F32)
    edge = NY * HALF
    squares = jnp.sum(total[:, edge:], axis=1, keepdims=True)
    scale = lax.rsqrt(squares / D_ENC + 1e-06)
    for j in range(NY):
        out_ref[j] = (total[:, j * HALF : (j + 1) * HALF] * scale).astype(BF16)


def finish_text(got):
    rows = CT // NZH
    return pl.pallas_call(
        text_kernel,
        out_shape=jax.ShapeDtypeStruct((NY, rows, HALF), BF16),
        compiler_params=params(),
        name="finish_text",
    )(got)


def project_kernel(core_ref, own_ref, other_ref, w_ref, out_ref):
    core = core_ref[0]
    own_w = w_ref[pl.ds(pl.multiple_of(core * HALF, HALF), HALF), :]
    other_w = w_ref[pl.ds(pl.multiple_of((1 - core) * HALF, HALF), HALF), :]
    out_ref[...] = (dot(own_ref[...], own_w) + dot(other_ref[...], other_w)).astype(BF16)


def project(core, own, other, w):
    return pl.pallas_call(
        project_kernel,
        grid_spec=pltpu.PrefetchScalarGridSpec(
            num_scalar_prefetch=1,
            grid=(NY,),
            in_specs=[
                pl.BlockSpec((CT, HALF), lambda i, _: (i, 0)),
                pl.BlockSpec((CT, HALF), lambda i, _: (i, 0)),
                pl.BlockSpec((CHUNK, 2 * COLS), lambda i, _: (0, 0)),
            ],
            out_specs=pl.BlockSpec((CT, 2 * COLS), lambda i, _: (i, 0)),
        ),
        out_shape=jax.ShapeDtypeStruct((NY * CT, 2 * COLS), BF16),
        compiler_params=params(),
        name="project",
    )(core, own, other, w)


def image_kernel(q_ref, k_ref, v_ref, o_ref, m_ref, l_ref, wide, *, block, rows):
    factor = SCALE * LOG2E
    wide[:, :HD] = v_ref[...]
    wide[:, HD:] = jnp.ones((IK, HD), BF16)
    for r in range(IQ // rows):
        part = pl.ds(r * rows, rows)
        q = q_ref[part, :]
        top = None
        for j in range(IK // block):
            cols = pl.ds(j * block, block)
            s = dot(q, k_ref[cols, :], NT)
            here = jnp.max(s, axis=1, keepdims=True) * factor
            new = here if top is None else jnp.maximum(top, here)
            p = jnp.exp2(s * factor - new).astype(BF16)
            add = dot(p, wide[cols, :])
            acc = add if top is None else acc * jnp.exp2(top - new) + add
            top = new
        o_ref[part, :] = acc[:, :HD]
        l_ref[part, :] = acc[:, HD:]
        m_ref[part, :] = jnp.broadcast_to(top, (rows, HD))


def image_attention(q, k, v, head):
    out = jax.ShapeDtypeStruct((IQ, HD), F32)
    return pl.pallas_call(
        functools.partial(image_kernel, block=512, rows=256),
        grid=(1,),
        in_specs=[
            pl.BlockSpec((IQ, HD), lambda i: (0, head)),
            pl.BlockSpec((IK, HD), lambda i: (0, head)),
            pl.BlockSpec((IK, HD), lambda i: (0, head)),
        ],
        out_specs=[pl.BlockSpec((IQ, HD), lambda i: (0, 0))] * 3,
        out_shape=[out] * 3,
        scratch_shapes=[pltpu.VMEM((IK, 2 * HD), BF16)],
        compiler_params=params(),
        name="image_attention",
    )(q, k, v)


def text_attention_kernel(
    length_ref, kv_ref, q_ref, g_ref, gain_ref, *refs
):
    parts, (out_ref, cot_ref) = refs[: 3 * HEADS], refs[3 * HEADS :]
    length = length_ref[0]
    gain = gain_ref[...]
    factor = SCALE * LOG2E
    keep = lax.broadcasted_iota(jnp.int32, (1, CT), 1) < length
    kv = kv_ref[0].astype(F32)
    for i in range(1, NY):
        kv = kv + kv_ref[i].astype(F32)
    for h in range(HEADS):
        cols = slice(h * HD, (h + 1) * HD)
        o, m, l = parts[3 * h][...], parts[3 * h + 1][:, :1], parts[3 * h + 2][:, :1]
        key_pre = kv[:, cols]
        value = kv[:, COLS + h * HD : COLS + (h + 1) * HD].astype(BF16)
        root = lax.rsqrt(jnp.mean(key_pre * key_pre, axis=1, keepdims=True) + 1e-06)
        key = (key_pre * root * gain).astype(BF16)
        q = q_ref[:, cols]
        g = g_ref[:, cols]
        s = jnp.where(keep, dot(q, key, NT) * factor, -1e30)
        top = jnp.maximum(m, jnp.max(s, axis=1, keepdims=True))
        e = jnp.exp2(s - top)
        fade = jnp.exp2(m - top)
        inverse = 1.0 / (l * fade + jnp.sum(e, axis=1, keepdims=True))
        p = e * inverse
        probs = p.astype(BF16)
        joint = o * (fade * inverse) + dot(probs, value)
        out_ref[:, cols] = joint
        mean = jnp.sum(g.astype(F32) * joint, axis=1, keepdims=True)
        dp = dot(g, value, NT)
        ds = (p * (dp - mean) * SCALE).astype(BF16)
        d_value = dot(probs, g, TN).astype(BF16)
        d_key = dot(ds, q, TN).astype(BF16).astype(F32) * gain
        along = jnp.mean(d_key * key_pre, axis=1, keepdims=True)
        d_pre = (root * d_key - key_pre * (root * root * root * along)).astype(BF16)
        for i in range(NY):
            cot_ref[i, :, cols] = d_pre
            cot_ref[i, :, COLS + h * HD : COLS + (h + 1) * HD] = d_value


def text_attention(length, kv, q, g, gain, parts):
    vmem = pl.BlockSpec(memory_space=pltpu.VMEM)
    return pl.pallas_call(
        text_attention_kernel,
        in_specs=[pl.BlockSpec(memory_space=pltpu.SMEM)] + [vmem] * (4 + 3 * HEADS),
        out_specs=[vmem, vmem],
        out_shape=[
            jax.ShapeDtypeStruct((IQ, COLS), F32),
            jax.ShapeDtypeStruct((NY, CT, 2 * COLS), BF16),
        ],
        compiler_params=params(),
        name="text_attention",
    )(length, kv, q, g, gain, *parts)


def gradient_kernel(core_ref, own_ref, other_ref, cot_ref, out_ref):
    step = pl.program_id(0)

    @pl.when(step == 0)
    def _():
        out_ref[...] = dot(own_ref[...], cot_ref[...], TN).astype(BF16)

    @pl.when(step == 1)
    def _():
        out_ref[...] = dot(other_ref[...], cot_ref[...], TN).astype(BF16)


def gradient(core, own, other, cot):
    whole = lambda i, _: (0, 0)
    return pl.pallas_call(
        gradient_kernel,
        grid_spec=pltpu.PrefetchScalarGridSpec(
            num_scalar_prefetch=1,
            grid=(NC,),
            in_specs=[
                pl.BlockSpec((NY * CT, HALF), whole),
                pl.BlockSpec((NY * CT, HALF), whole),
                pl.BlockSpec((NY * CT, 2 * COLS), whole),
            ],
            out_specs=pl.BlockSpec(
                (HALF, 2 * COLS), lambda i, c: (jnp.where(i == 0, c[0], 1 - c[0]), 0)
            ),
        ),
        out_shape=jax.ShapeDtypeStruct((CHUNK, 2 * COLS), BF16),
        compiler_params=params(),
        name="gradient",
    )(core, own, other, cot)


def body(
    enc_resid,
    enc_gain,
    text_in_w,
    key_w,
    value_w,
    key_gain,
    img_query,
    img_keys,
    img_values,
    out_grad,
    cap_lengths,
    assignment,
):
    core = lax.axis_index("c").astype(jnp.int32).reshape(1)
    sample = (lax.axis_index("y") * NZL + lax.axis_index("zl")) * NX + lax.axis_index("x")
    length = jnp.sum(jnp.where(assignment == sample, cap_lengths, 0)).reshape(1)
    swap = [(0, 1), (1, 0)]

    both_w = lax.all_gather(
        jnp.concatenate([key_w, value_w], axis=1), ("zl", "x"), axis=0, tiled=True
    )

    send, keep = front(core, assignment, enc_resid, enc_gain.reshape(1, FEAT), text_in_w)
    summed = core_sum(keep, lax.ppermute(send, "c", swap))

    parts = []

    def beside(operand, move, head):
        operand, query = lax.optimization_barrier((operand, img_query))
        moved = move(operand)
        part = image_attention(query, img_keys, img_values, head)
        moved, part = lax.optimization_barrier((moved, tuple(part)))
        parts.extend(part)
        return moved

    got = beside(
        summed.reshape(NZH, CT // NZH, WIDE),
        lambda a: lax.all_to_all(a, "zh", 0, 0, tiled=True),
        0,
    )
    text = finish_text(got).reshape(SAMPLES, TOK, HALF)
    text = lax.all_to_all(text, ("y", "zl", "x"), 0, 0, tiled=True)
    spread = jnp.broadcast_to(text.reshape(1, CT, HALF), (NZH, CT, HALF))
    own = beside(spread, lambda a: lax.all_to_all(a, "zh", 0, 0, tiled=True), 1)
    own = own.reshape(NY * CT, HALF)
    other = lax.ppermute(own, "c", swap)
    kv = project(core, own, other, both_w)
    kv = beside(
        kv.reshape(NY, CT, 2 * COLS), lambda a: lax.all_to_all(a, "y", 0, 0, tiled=True), 2
    )
    attn_out, cot = text_attention(
        length, kv, img_query, out_grad, key_gain.reshape(1, HD), parts
    )
    cot = lax.all_to_all(cot, "y", 0, 0, tiled=True).reshape(NY * CT, 2 * COLS)
    grad = gradient(core, own, other, cot).reshape(GROUP, D // SAMPLES, 2 * COLS)
    grad = lax.all_to_all(grad, ("zl", "x"), 0, 0, tiled=True)
    total = jnp.sum(grad.astype(F32), axis=0)
    return (attn_out, total[:, :COLS], total[:, COLS:])


def solution(mesh):
    fine = Mesh(mesh.devices.reshape(NY, NZL, NX, NZH, NC), ("y", "zl", "x", "zh", "c"))
    dp, mp = ("y", "zl", "x"), ("zh", "c")
    return jax.shard_map(
        body,
        mesh=fine,
        in_specs=(
            P(None, dp, mp),
            P(mp),
            P(mp, None),
            P(dp, mp),
            P(dp, mp),
            P(),
            P(dp, mp),
            P(dp, mp),
            P(dp, mp),
            P(dp, mp),
            P(),
            P(),
        ),
        out_specs=(P(dp, mp), P(dp, mp), P(dp, mp)),
        check_vma=False,
    )
```

time: 641 us -> 209 us (0.33)
  waiting for transfers between devices: 358 us -> 64.9 us
  matrix products: 83.3 us -> 0 us
  blocking collectives: 116 us -> 39.5 us
  Pallas kernels: 0 us -> 56.4 us
  local copies, waits for them, and re-layouts: 37.6 us -> 5.52 us
  other arithmetic: 21.8 us -> 1.47 us
  starting transfers between devices: 8.14 us -> 25 us
    reduce_scatter x1 -> x0, waiting for transfers between devices: 181 us -> none  [body(): lax.psum_scatter(lax.dot_general(columns, both_cots, (((0,), (0,)), ((),...]
    all_gather x2 -> x1, waiting for transfers between devices: 175 us -> 11 us  [body(): lax.all_gather(jnp.concatenate([key_w, value_w], axis=1), ('zl', 'x'), ax...]
    psum x2 -> x0, blocking collectives: 116 us -> none  [the longest x1 87.8 us: text_features(): return lax.psum(partial_sums, 'mp').astype(jnp.bfloat16)]
    dot_general x29 -> x0, matrix products: 83.3 us -> none  [the longest x6 26.5 us: head_attend(): jnp.dot(image_probs, image_values, preferred_element_type=jnp.float32)]
    pallas_call x0 -> x9, Pallas kernels: none -> 56.4 us  [the longest x3 20.2 us: image_attention(): pl.pallas_call(functools.partial(image_kernel, block=512, rows=256), grid...]
    all_to_all x1 -> x4, waiting for transfers between devices: 0.01 us -> 51.4 us  [the longest x1 15.8 us: body(): own = beside(spread, lambda a: lax.all_to_all(a, 'zh', 0, 0, tiled=True), 1)]
    all_to_all x0 -> x2, blocking collectives: none -> 39.5 us  [the longest x1 22.6 us: body(): cot = lax.all_to_all(cot, 'y', 0, 0, tiled=True).reshape(NY * CT, 2 * COLS)]
    all_to_all x1 -> x4, starting transfers between devices: 8.03 us -> 25 us  [the longest x1 8.11 us: body(): lax.all_to_all(a, 'zh', 0, 0, tiled=True)]
  transfers between devices with their start and end apart: 4 -> 7, of which waited for: 3 -> 6; matrix products, arithmetic and copies ran while one was open for 4% -> 1% of each run, Pallas kernels for 0% -> 10%
where the time goes in v1:
time: 209 us; the launch traced here: 207 us
  waiting for transfers between devices  64.9 us (31%)
  Pallas kernels  56.4 us (27%)
  blocking collectives  39.5 us (19%)
  starting transfers between devices  25 us (12%)
  between operations  14.1 us (7%)
  local copies, waits for them, and re-layouts  5.52 us (3%)
    all_to_all x1, blocking collectives, body(): cot = lax.all_to_all(cot, 'y', 0, 0, tiled=True).reshape(NY * CT, 2 * COLS)  22.6 us
    pallas_call x3, Pallas kernels, image_attention(): pl.pallas_call(functools.partial(image_kernel, block=512, rows=256), grid...  20.2 us
    all_to_all x1, blocking collectives, body(): grad = lax.all_to_all(grad, ('zl', 'x'), 0, 0, tiled=True)  16.9 us
    all_to_all x1, waiting for transfers between devices, body(): own = beside(spread, lambda a: lax.all_to_all(a, 'zh', 0, 0, tiled=True), 1)  15.8 us
    all_to_all x1, waiting for transfers between devices, body(): lax.all_to_all(a, 'zh', 0, 0, tiled=True)  15.7 us
    pallas_call x1, Pallas kernels, text_attention(): pl.pallas_call(text_attention_kernel, in_specs=[pl.BlockSpec(memory_space...  13.2 us
    all_to_all x1, waiting for transfers between devices, body(): lax.all_to_all(a, 'y', 0, 0, tiled=True)  11.7 us
    all_gather x1, waiting for transfers between devices, body(): lax.all_gather(jnp.concatenate([key_w, value_w], axis=1), ('zl', 'x'), ax...  11 us
  transfers between devices with their start and end apart: 7, of which 6 were waited for; matrix products, arithmetic and copies ran while one was open for 1% of the time, Pallas kernels for 10%

profile of v1, /device:TPU:64, one launch (start us, length us, event | category | flops | bytes accessed | tf_op | source)
XLA Modules:
  0.0 206.9 jit_solution(4364239872652200732)
XLA Ops:
  7.2 8.5 %text_partial.1 = (bf16[256,1664]{1,0:T(8,128)(2,1)}, f32[256,1664]{1,0:T(8,128)}) custom-call(s32[1]{0:T(128)} %bitcast.1.core_ref, s32[32]{0:T(128)} %assign_ref.1, bf16[32,8,512]{2,1,0:T(8,128)(2,1)} %x_ref.1, f32[1,512]{1,0:T(1,128)} %bitcast.20, bf16[512,3072]{1,0:T(8,128)(2,1)} %w_ref.1), custom_call_target="tpu_custom_call" | custom-call | tf_op jit(solution)/shard_map/text_partial/pallas_call | solution.py:90
  15.6 0.0 collective-permute-start
  15.6 2.6 %collective-permute-done.got_ref = bf16[256,1664]{1,0:T(8,128)(2,1)S(1)} collective-permute-done((bf16[256,1664]{1,0:T(8,128)(2,1)}, bf16[256,1664]{1,0:T(8,128)(2,1)S(1)}, u32[]{:S(2)}, u32[]{:S(2)}) %collective-permute-start) | collective-permute-done | bytes 852000 | tf_op jit(solution)/shard_map/ppermute | solution.py:333
  18.2 0.0 copy-start.4
  18.2 0.9 copy-done.4
  19.1 3.0 %core_sum.1 = bf16[256,1664]{1,0:T(8,128)(2,1)} custom-call(f32[256,1664]{1,0:T(8,128)} %get-tuple-element.34.keep_ref, bf16[256,1664]{1,0:T(8,128)(2,1)} %copy-done.4), custom_call_target="tpu_custom_call" | custom-call | tf_op jit(solution)/shard_map/core_sum/pallas_call | solution.py:124
  22.1 8.1 %all-to-all-start = ((bf16[4,64,1664]{2,1,0:T(8,128)(2,1)}), bf16[4,64,1664]{2,1,0:T(8,128)(2,1)S(1)}, u32[]{:S(2)}, u32[]{:S(2)}) async-start(bf16[4,64,1664]{2,1,0:T(8,128)(2,1)} %bitcast.17), calls=%async_computation | async-start | bytes 1703936 | tf_op jit(solution)/shard_map/all_to_all | solution.py:347
  30.2 0.0 copy-start.5
  30.2 6.7 %image_attention.3 = (f32[768,128]{1,0:T(8,128)}, f32[768,128]{1,0:T(8,128)}, f32[768,128]{1,0:T(8,128)}) custom-call(bf16[768,384]{1,0:T(8,128)(2,1)} %q_ref.4, bf16[4096,384]{1,0:T(8,128)(2,1)} %k_ref.5, bf16[4096,384]{1,0:T(8,128)(2,1)} %v_ref.5), custom_call_target="tpu_custom_call" | custom-call | tf_op jit(solution)/shard_map/image_attention/pallas_call | solution.py:203
  36.9 15.7 %all-to-all-done.got_ref = bf16[4,64,1664]{2,1,0:T(8,128)(2,1)S(1)} async-done(((bf16[4,64,1664]{2,1,0:T(8,128)(2,1)}), bf16[4,64,1664]{2,1,0:T(8,128)(2,1)S(1)}, u32[]{:S(2)}, u32[]{:S(2)}) %all-to-all-start) | async-done | bytes 852000 | tf_op jit(solution)/shard_map/all_to_all | solution.py:347
  52.6 0.0 copy-start.2
  52.6 0.9 copy-done.2
  53.5 2.0 finish_text.1
  55.5 7.3 %all-to-all-start.1 = ((bf16[32,8,384]{2,1,0:T(8,128)(2,1)}), bf16[32,8,384]{2,1,0:T(8,128)(2,1)S(1)}, u32[]{:S(2)}, u32[]{:S(2)}) async-start(bf16[32,8,384]{2,1,0:T(8,128)(2,1)} %bitcast.18), calls=%async_computation.1 | async-start | bytes 393216 | tf_op jit(solution)/shard_map/all_to_all | solution.py:351
  62.9 0.0 all-gather.2.cloned.1.call-start
  62.9 0.0 copy-done.5
  62.9 0.0 copy-done.6
  62.9 0.7 pad_maximum_fusion
  63.6 0.0 all-gather.2.cloned.1.call-update
  63.6 8.2 %all-to-all-done.1 = bf16[32,8,384]{2,1,0:T(8,128)(2,1)S(1)} async-done(((bf16[32,8,384]{2,1,0:T(8,128)(2,1)}), bf16[32,8,384]{2,1,0:T(8,128)(2,1)S(1)}, u32[]{:S(2)}, u32[]{:S(2)}) %all-to-all-start.1) | async-done | bytes 196640 | tf_op jit(solution)/shard_map/all_to_all | solution.py:351
  71.8 0.9 broadcast_in_dim.13
  72.7 5.8 %all-to-all-start.2 = ((bf16[4,256,384]{2,1,0:T(8,128)(2,1)}), bf16[4,256,384]{2,1,0:T(8,128)(2,1)S(1)}, u32[]{:S(2)}, u32[]{:S(2)}) async-start(bf16[4,256,384]{2,1,0:T(8,128)(2,1)} %broadcast_in_dim.13), calls=%async_computation.2 | async-start | bytes 1572864 | tf_op jit(solution)/shard_map/all_to_all | solution.py:353
  78.6 6.7 %image_attention.4 = (f32[768,128]{1,0:T(8,128)}, f32[768,128]{1,0:T(8,128)}, f32[768,128]{1,0:T(8,128)}) custom-call(bf16[768,384]{1,0:T(8,128)(2,1)} %q_ref.4, bf16[4096,384]{1,0:T(8,128)(2,1)} %k_ref.5, bf16[4096,384]{1,0:T(8,128)(2,1)} %v_ref.5), custom_call_target="tpu_custom_call" | custom-call | tf_op jit(solution)/shard_map/image_attention/pallas_call | solution.py:203
  85.2 15.8 %all-to-all-done.2 = bf16[4,256,384]{2,1,0:T(8,128)(2,1)S(1)} async-done(((bf16[4,256,384]{2,1,0:T(8,128)(2,1)}), bf16[4,256,384]{2,1,0:T(8,128)(2,1)S(1)}, u32[]{:S(2)}, u32[]{:S(2)}) %all-to-all-start.2) | async-done | bytes 786464 | tf_op jit(solution)/shard_map/all_to_all | solution.py:353
  101.0 0.0 copy-start
  101.0 0.0 collective-permute-start.1
  101.0 11.0 %all-gather.2.cloned.1.call-done.w_ref = bf16[768,768]{1,0:T(8,128)(2,1)} async-done(((bf16[96,768]{1,0:T(8,128)(2,1)}), bf16[768,768]{1,0:T(8,128)(2,1)}) %all-gather.2.cloned.1.call-update) | async-done | bytes 1179664 | tf_op jit(solution)/shard_map/all_gather | solution.py:328
  112.0 0.0 collective-permute-done.1.other_ref
  112.0 0.0 copy-done
  112.0 0.0 copy-start.3
  112.0 0.9 copy-done.3
  112.9 5.2 %project.1 = bf16[1024,768]{1,0:T(8,128)(2,1)} custom-call(s32[1]{0:T(128)} %bitcast.1.core_ref, bf16[1024,384]{1,0:T(8,128)(2,1)} %bitcast.12, bf16[1024,384]{1,0:T(8,128)(2,1)} %copy-done.3, bf16[768,768]{1,0:T(8,128)(2,1)} %all-gather.2.cloned.1.call-done.w_ref), custom_call_target="tpu_custom_call" | custom-call | tf_op jit(solution)/shard_map/project/pallas_call | solution.py:161
  118.1 0.0 copy-start.7
  118.1 0.0 copy-start.8
  118.1 3.7 %all-to-all-start.3 = ((bf16[4,256,768]{2,1,0:T(8,128)(2,1)}), bf16[4,256,768]{2,1,0:T(8,128)(2,1)S(1)}, u32[]{:S(2)}, u32[]{:S(2)}) async-start(bf16[4,256,768]{2,1,0:T(8,128)(2,1)} %bitcast.14), calls=%async_computation.3 | async-start | bytes 3145728 | tf_op jit(solution)/shard_map/all_to_all | solution.py:358
  121.8 0.0 copy-done.7
  121.8 0.0 copy-done.8
  121.8 0.6 fusion
  122.4 6.8 %image_attention.5 = (f32[768,128]{1,0:T(8,128)}, f32[768,128]{1,0:T(8,128)}, f32[768,128]{1,0:T(8,128)}) custom-call(bf16[768,384]{1,0:T(8,128)(2,1)} %q_ref.4, bf16[4096,384]{1,0:T(8,128)(2,1)} %k_ref.5, bf16[4096,384]{1,0:T(8,128)(2,1)} %v_ref.5), custom_call_target="tpu_custom_call" | custom-call | tf_op jit(solution)/shard_map/image_attention/pallas_call | solution.py:203
  129.2 11.7 %all-to-all-done.3.kv_ref = bf16[4,256,768]{2,1,0:T(8,128)(2,1)S(1)} async-done(((bf16[4,256,768]{2,1,0:T(8,128)(2,1)}), bf16[4,256,768]{2,1,0:T(8,128)(2,1)S(1)}, u32[]{:S(2)}, u32[]{:S(2)}) %all-to-all-start.3) | async-done | bytes 1572896 | tf_op jit(solution)/shard_map/all_to_all | solution.py:358
  140.9 0.0 copy-start.1
  140.9 1.1 copy-done.1
  142.0 13.2 %text_attention.1 = (f32[768,384]{1,0:T(8,128)}, bf16[4,256,768]{2,1,0:T(8,128)(2,1)}) custom-call(s32[1]{0:T(128)} %bitcast.length_ref, bf16[4,256,768]{2,1,0:T(8,128)(2,1)} %copy-done.1, bf16[768,384]{1,0:T(8,128)(2,1)} %q_ref.4, bf16[768,384]{1,0:T(8,128)(2,1)} %g_ref.1, f32[1,128]{1,0:T(1,128)} %bitcast.21, f32[768,128]{1,0:T(8,128)} %get-tuple-element.54.refs_0_, ...), custom_call_target="tpu_custom_call" | custom-call | tf_op jit(solution)/shard_map/text_attention/pallas_call | solution.py:262
  155.3 22.6 %all_to_all.30 = bf16[4,256,768]{2,1,0:T(8,128)(2,1)} all-to-all(bf16[4,256,768]{2,1,0:T(8,128)(2,1)} %get-tuple-element.64), channel_id=1, replica_groups=mesh['y'=4,'zl'=2,'x'=4,'zh'=4,'c'=2] {'y'}, dimensions={0} | all-to-all | bytes 3145728 | tf_op jit(solution)/shard_map/all_to_all | solution.py:363
  177.9 4.4 %gradient.1 = bf16[768,768]{1,0:T(8,128)(2,1)} custom-call(s32[1]{0:T(128)} %bitcast.1.core_ref, bf16[1024,384]{1,0:T(8,128)(2,1)} %bitcast.13, bf16[1024,384]{1,0:T(8,128)(2,1)} %copy-done.3, bf16[1024,768]{1,0:T(8,128)(2,1)} %bitcast.15), custom_call_target="tpu_custom_call" | custom-call | tf_op jit(solution)/shard_map/gradient/pallas_call | solution.py:289
  182.3 16.9 %all_to_all.31 = bf16[8,96,768]{2,1,0:T(8,128)(2,1)S(1)} all-to-all(bf16[8,96,768]{2,1,0:T(8,128)(2,1)} %bitcast.16), channel_id=1, replica_groups=mesh['y'=4,'zl'=2,'x'=4,'zh'=4,'c'=2] {'zl','x'}, dimensions={0} | all-to-all | bytes 2359296 | tf_op jit(solution)/shard_map/all_to_all | solution.py:365
  199.2 0.2 convert_reduce_fusion
  199.3 0.7 fusion.1
  (1 shorter events, 0.0 us)
Async XLA Ops:
  15.6 2.6 %collective-permute-start = (bf16[256,1664]{1,0:T(8,128)(2,1)}, bf16[256,1664]{1,0:T(8,128)(2,1)S(1)}, u32[]{:S(2)}, u32[]{:S(2)}) collective-permute-start(bf16[256,1664]{1,0:T(8,128)(2,1)} %get-tuple-element.35), channel_id=1, source_target_pairs={{0,1},{1,0},{2,3},{3,2},{4,5},{5,4},{6,7},{7,6},{8,9},{9,8},{10,11... | collective-permute-start | bytes 2555912 | tf_op jit(solution)/shard_map/ppermute | solution.py:333
  18.2 0.9 copy-start.4
  22.1 30.6 %all-to-all-start = ((bf16[4,64,1664]{2,1,0:T(8,128)(2,1)}), bf16[4,64,1664]{2,1,0:T(8,128)(2,1)S(1)}, u32[]{:S(2)}, u32[]{:S(2)}) async-start(bf16[4,64,1664]{2,1,0:T(8,128)(2,1)} %bitcast.17), calls=%async_computation | async-start | bytes 1703936 | tf_op jit(solution)/shard_map/all_to_all | solution.py:347
  30.2 32.7 %copy-start.5 = (bf16[96,384]{1,0:T(8,128)(2,1)S(1)}, bf16[96,384]{1,0:T(8,128)(2,1)}, u32[]{:S(2)}) copy-start(bf16[96,384]{1,0:T(8,128)(2,1)} %param.16) | copy-start | bytes 221188
  30.2 32.7 %copy-start.6 = (bf16[96,384]{1,0:T(8,128)(2,1)S(1)}, bf16[96,384]{1,0:T(8,128)(2,1)}, u32[]{:S(2)}) copy-start(bf16[96,384]{1,0:T(8,128)(2,1)} %param.15) | copy-start | bytes 221188
  52.6 0.9 copy-start.2
  55.5 16.2 %all-to-all-start.1 = ((bf16[32,8,384]{2,1,0:T(8,128)(2,1)}), bf16[32,8,384]{2,1,0:T(8,128)(2,1)S(1)}, u32[]{:S(2)}, u32[]{:S(2)}) async-start(bf16[32,8,384]{2,1,0:T(8,128)(2,1)} %bitcast.18), calls=%async_computation.1 | async-start | bytes 393216 | tf_op jit(solution)/shard_map/all_to_all | solution.py:351
  62.9 49.1 %all-gather.2.cloned.1.call-start = ((), (), s32[]{:S(2)}) async-start(), calls=%async_computation.6 | async-start | bytes 1327104 | tf_op jit(solution)/shard_map/all_gather | solution.py:328
  72.7 28.3 %all-to-all-start.2 = ((bf16[4,256,384]{2,1,0:T(8,128)(2,1)}), bf16[4,256,384]{2,1,0:T(8,128)(2,1)S(1)}, u32[]{:S(2)}, u32[]{:S(2)}) async-start(bf16[4,256,384]{2,1,0:T(8,128)(2,1)} %broadcast_in_dim.13), calls=%async_computation.2 | async-start | bytes 1572864 | tf_op jit(solution)/shard_map/all_to_all | solution.py:353
  101.0 11.0 %copy-start = (bf16[4,256,384]{2,1,0:T(8,128)(2,1)}, bf16[4,256,384]{2,1,0:T(8,128)(2,1)S(1)}, u32[]{:S(2)}) copy-start(bf16[4,256,384]{2,1,0:T(8,128)(2,1)S(1)} %all-to-all-done.2) | copy-start | bytes 2359300
  101.0 11.0 %collective-permute-start.1 = (bf16[1024,384]{1,0:T(8,128)(2,1)S(1)}, bf16[1024,384]{1,0:T(8,128)(2,1)S(1)}, u32[]{:S(2)}, u32[]{:S(2)}) collective-permute-start(bf16[1024,384]{1,0:T(8,128)(2,1)S(1)} %bitcast.11), channel_id=1, source_target_pairs={{0,1},{1,0},{2,3},{3,2},{4,5},{5,4},{6,7},{7,6},{8,9},{9,8},{10,11... | collective-permute-start | bytes 2359304 | tf_op jit(solution)/shard_map/ppermute | solution.py:355
  112.0 0.9 copy-start.3
  118.1 3.7 %copy-start.7 = (s32[32]{0:T(128)S(1)}, s32[32]{0:T(128)}, u32[]{:S(2)}) copy-start(s32[32]{0:T(128)} %assign_ref.1) | copy-start | bytes 388
  118.1 3.7 %copy-start.8 = (s32[32]{0:T(128)S(1)}, s32[32]{0:T(128)}, u32[]{:S(2)}) copy-start(s32[32]{0:T(128)} %param.22) | copy-start | bytes 388
  118.1 22.8 %all-to-all-start.3 = ((bf16[4,256,768]{2,1,0:T(8,128)(2,1)}), bf16[4,256,768]{2,1,0:T(8,128)(2,1)S(1)}, u32[]{:S(2)}, u32[]{:S(2)}) async-start(bf16[4,256,768]{2,1,0:T(8,128)(2,1)} %bitcast.14), calls=%async_computation.3 | async-start | bytes 3145728 | tf_op jit(solution)/shard_map/all_to_all | solution.py:358
  140.9 1.1 copy-start.1
Sparse Core Ops, SparseCore 0:
  66.1 45.8 all-gather.1

commit v2 on v0

v2 whole, which is shorter than its diff:
```python
import functools
import math

import jax
import jax.numpy as jnp
from jax import lax
from jax.experimental import pallas as pl
from jax.experimental.pallas import tpu as pltpu
from jax.sharding import Mesh, PartitionSpec as P

BF16 = jnp.bfloat16
F32 = jnp.float32

D_ENC = 4096
D = 3072
HD = 128
CT = 256
IQ = 768
IK = 4096
SAMPLES = 32
NY, NZL, NX, NZH, NC = 4, 2, 4, 4, 2
TOK = CT // SAMPLES
FEAT = D_ENC // (NZH * NC)
COLS = D // (NZH * NC)
HEADS = COLS // HD
CHUNK = D // NY
HALF = CHUNK // NC
GROUP = NZL * NX
IMAGE_MIB = 56
WROWS = D // SAMPLES
EXTRA = 16
ROWS = CT + EXTRA
SCALE = HD ** (-0.5)
LOG2E = math.log2(math.e)
NT = (((1,), (1,)), ((), ()))
TN = (((0,), (0,)), ((), ()))


def params(mib):
    return pltpu.CompilerParams(vmem_limit_bytes=mib * 2**20)


def dot(a, b, dims=(((1,), (0,)), ((), ()))):
    return lax.dot_general(a, b, dims, preferred_element_type=F32)


def square_rows(total):
    hi = total.astype(BF16).astype(F32)
    full = jnp.concatenate([total, jnp.zeros((1, HALF - CT), F32)], axis=1)
    top = jnp.concatenate([hi, jnp.zeros((1, HALF - CT), F32)], axis=1)
    row = lax.broadcasted_iota(jnp.int32, (EXTRA, HALF), 0)
    return jnp.where(row == 0, top, jnp.where(row == 1, full - top, 0.0)).astype(BF16)


def read_squares(block):
    return jnp.sum(block[:, :CT].astype(F32), axis=0, keepdims=True)


def prepare_kernel(assign_ref, x_ref, gain_ref, xg_ref, sq_ref, rows, squares):
    gain = gain_ref[...]
    for c in range(SAMPLES):
        start = pl.multiple_of(assign_ref[c] * TOK, TOK)
        values = x_ref[c].astype(F32)
        rows[pl.ds(start, TOK), :] = values * gain
        squares[pl.ds(start, TOK), :] = jnp.broadcast_to(
            jnp.sum(values * values, axis=1, keepdims=True), (TOK, 128)
        )
    xg_ref[...] = rows[...].astype(BF16)
    sq_ref[...] = squares[...].T[:8, :]


def prepare(assignment, x, gain):
    vmem = pl.BlockSpec(memory_space=pltpu.VMEM)
    return pl.pallas_call(
        prepare_kernel,
        in_specs=[pl.BlockSpec(memory_space=pltpu.SMEM), vmem, vmem],
        out_specs=[vmem, vmem],
        out_shape=[jax.ShapeDtypeStruct((CT, FEAT), BF16), jax.ShapeDtypeStruct((8, CT), F32)],
        scratch_shapes=[pltpu.VMEM((CT, FEAT), F32), pltpu.VMEM((CT, 128), F32)],
        compiler_params=params(8),
        name="prepare",
    )(assignment, x, gain)


def send_kernel(core_ref, xg_ref, sq_ref, w_ref, out_ref):
    out_ref[0, :CT, :] = dot(xg_ref[...], w_ref[...]).astype(BF16)
    out_ref[0, CT:, :] = square_rows(sq_ref[:1, :])


def send_part(core, xg, sq, w):
    return pl.pallas_call(
        send_kernel,
        grid_spec=pltpu.PrefetchScalarGridSpec(
            num_scalar_prefetch=1,
            grid=(NZH,),
            in_specs=[
                pl.BlockSpec((CT, FEAT), lambda i, _: (0, 0)),
                pl.BlockSpec((8, CT), lambda i, _: (0, 0)),
                pl.BlockSpec((FEAT, HALF), lambda i, c: (0, i * NC + 1 - c[0])),
            ],
            out_specs=pl.BlockSpec((1, ROWS, HALF), lambda i, _: (i, 0, 0)),
        ),
        out_shape=jax.ShapeDtypeStruct((NZH, ROWS, HALF), BF16),
        compiler_params=params(16),
        name="text_other_half",
    )(core, xg, sq, w)


def keep_kernel(core_ref, xg_ref, sq_ref, w_ref, got_ref, out_ref):
    total = dot(xg_ref[...], w_ref[...]) + got_ref[0, :CT, :].astype(F32)
    out_ref[0, :CT, :] = total.astype(BF16)
    out_ref[0, CT:, :] = square_rows(sq_ref[:1, :] + read_squares(got_ref[0, CT:, :]))


def keep_part(core, xg, sq, w, got):
    block = pl.BlockSpec((1, ROWS, HALF), lambda i, _: (i, 0, 0))
    return pl.pallas_call(
        keep_kernel,
        grid_spec=pltpu.PrefetchScalarGridSpec(
            num_scalar_prefetch=1,
            grid=(NZH,),
            in_specs=[
                pl.BlockSpec((CT, FEAT), lambda i, _: (0, 0)),
                pl.BlockSpec((8, CT), lambda i, _: (0, 0)),
                pl.BlockSpec((FEAT, HALF), lambda i, c: (0, i * NC + c[0])),
                block,
            ],
            out_specs=block,
        ),
        out_shape=jax.ShapeDtypeStruct((NZH, ROWS, HALF), BF16),
        compiler_params=params(16),
        name="text_own_half",
    )(core, xg, sq, w, got)


def text_kernel(got_ref, out_ref):
    total = got_ref[0].astype(F32)
    for i in range(1, NZH):
        total = total + got_ref[i].astype(F32)
    scale = lax.rsqrt(read_squares(total[CT:, :]) / D_ENC + 1e-06)
    column = jnp.broadcast_to(scale, (128, CT)).T[:, :1]
    out_ref[...] = (total[:CT, :] * column).astype(BF16)


def finish_text(got):
    return pl.pallas_call(
        text_kernel,
        out_shape=jax.ShapeDtypeStruct((CT, HALF), BF16),
        compiler_params=params(16),
        name="finish_text",
    )(got)


def image_kernel(q_ref, k_ref, v_ref, *refs, block, rows):
    o_ref, ml_ref, wide = refs[-3:]
    factor = SCALE * LOG2E
    wide[:, :HD] = v_ref[...]
    wide[:, HD:] = jnp.ones((IK, HD), BF16)
    lane = lax.broadcasted_iota(jnp.int32, (rows, HD), 1)
    for r in range(IQ // rows):
        part = pl.ds(r * rows, rows)
        q = q_ref[part, :]
        top = None
        for j in range(IK // block):
            cols = pl.ds(j * block, block)
            s = dot(q, k_ref[cols, :], NT)
            here = jnp.max(s, axis=1, keepdims=True) * factor
            new = here if top is None else jnp.maximum(top, here)
            p = jnp.exp2(s * factor - new).astype(BF16)
            add = dot(p, wide[cols, :])
            acc = add if top is None else acc * jnp.exp2(top - new) + add
            top = new
        o_ref[part, :] = acc[:, :HD]
        ml_ref[part, :] = jnp.where(lane < HD // 2, top, acc[:, HD:])


def image_attention(q, k, v, heads, before):
    column = lambda i: (0, heads[0] + i)
    return pl.pallas_call(
        functools.partial(image_kernel, block=512, rows=256),
        grid=(len(heads),),
        in_specs=[
            pl.BlockSpec((IQ, HD), column),
            pl.BlockSpec((IK, HD), column),
            pl.BlockSpec((IK, HD), column),
        ]
        + [pl.BlockSpec(memory_space=pl.ANY)] * len(before),
        out_specs=[pl.BlockSpec((IQ, HD), column)] * 2,
        out_shape=[jax.ShapeDtypeStruct((IQ, COLS), F32)] * 2,
        scratch_shapes=[pltpu.VMEM((IK, 2 * HD), BF16)],
        input_output_aliases={3 + i: i for i in range(len(before))},
        cost_estimate=pl.CostEstimate(flops=1, bytes_accessed=1, transcendentals=0),
        compiler_params=params(IMAGE_MIB),
        name="image_attention",
    )(q, k, v, *before)


def head_attention(length, key_pre, value_pre, q, g, gain, image_sum, stats):
    factor = SCALE * LOG2E
    keep = lax.broadcasted_iota(jnp.int32, (CT, 1), 0) < length
    turned = stats.T
    m, l = turned[:1, :], turned[HD // 2 : HD // 2 + 1, :]
    value = value_pre.astype(BF16)
    root = lax.rsqrt(jnp.mean(key_pre * key_pre, axis=1, keepdims=True) + 1e-06)
    key = (key_pre * root * gain).astype(BF16)
    s = jnp.where(keep, dot(key, q, NT) * factor, -1e30)
    top = jnp.maximum(m, jnp.max(s, axis=0, keepdims=True))
    e = jnp.exp2(s - top)
    fade = jnp.exp2(m - top)
    inverse = 1.0 / (l * fade + jnp.sum(e, axis=0, keepdims=True))
    p = e * inverse
    probs = p.astype(BF16)
    image_scale = jnp.broadcast_to(fade * inverse, (HD, IQ)).T
    joint = image_sum * image_scale + dot(probs, value, TN)
    mean = jnp.sum((g.astype(F32) * joint).T, axis=0, keepdims=True)
    ds = (p * (dot(value, g, NT) - mean) * SCALE).astype(BF16)
    d_value = dot(probs, g).astype(BF16)
    d_key = dot(ds, q).astype(BF16).astype(F32) * gain
    along = jnp.mean(d_key * key_pre, axis=1, keepdims=True)
    d_pre = (root * d_key - key_pre * (root * root * root * along)).astype(BF16)
    return joint, d_pre, d_value


def text_side_kernel(length_ref, place_ref, gain_ref, *refs):
    whole, blocks = refs[:6], refs[6 : 6 + NY + NX]
    out_ref, cot_ref = refs[6 + NY + NX : 8 + NY + NX]
    local = refs[8 + NY + NX : 14 + NY + NX]
    w, kv, joined, cots, in_sems, w_sems, out_sems, cot_sems = refs[14 + NY + NX :]
    own, other, q, g, image_sum, stats = local
    y, zl, x, core = (place_ref[i] for i in range(4))

    fetch = [
        pltpu.make_async_copy(source, target, in_sems.at[i])
        for i, (source, target) in enumerate(zip(whole, local))
    ]
    for i in range(2):
        fetch[i].start()
    order = (0, 1, 3, 2)
    moves = {s: [] for s in order}
    for s in order:
        for n in range(2):
            for r in range(NX):
                far, near = (s, r) if n == 0 else (r, s)
                for t in range(NZL):
                    half = zl if t == 0 else 1 - zl
                    target = w.at[s, half, (x + NX - r) % NX, :, n * COLS : (n + 1) * COLS]
                    source = blocks[n * 4 + far].at[near, t]
                    move = pltpu.make_async_copy(source, target, w_sems.at[s, len(moves[s])])
                    move.start()
                    moves[s].append(move)
    for i in range(2, 6):
        fetch[i].start()

    for i in range(2):
        fetch[i].wait()
    for s in order:
        for move in moves[s]:
            move.wait()
        plane = (y + NY - s) % NY
        own_w = w[s, core].reshape(HALF, 2 * COLS)
        other_w = w[s, 1 - core].reshape(HALF, 2 * COLS)
        part = dot(own[plane], own_w) + dot(other[plane], other_w)
        if s == 0:
            kv[...] = part
        else:
            kv[...] += part

    for i in range(2, 6):
        fetch[i].wait()
    leave = []
    for h in range(HEADS):
        cols = slice(h * HD, (h + 1) * HD)
        joint, d_pre, d_value = head_attention(
            length_ref[0],
            kv[:, cols],
            kv[:, COLS + h * HD : COLS + (h + 1) * HD],
            q[:, cols],
            g[:, cols],
            gain_ref[...],
            image_sum[:, cols],
            stats[:, cols],
        )
        for n, value in ((0, d_pre), (1, d_value)):
            span = slice(n * COLS + h * HD, n * COLS + (h + 1) * HD)
            cots[:, span] = value
            for i in range(NY):
                leave.append(
                    pltpu.make_async_copy(
                        cots.at[:, span], cot_ref.at[i, :, span], cot_sems.at[h, n, i]
                    )
                )
                leave[-1].start()
        joined[:, cols] = joint
        leave.append(
            pltpu.make_async_copy(joined.at[:, cols], out_ref.at[:, cols], out_sems.at[h])
        )
        leave[-1].start()
    for move in leave:
        move.wait()


def text_side(length, place, gain, own, other, q, g, image_sum, stats, keys, values):
    smem = pl.BlockSpec(memory_space=pltpu.SMEM)
    anywhere = pl.BlockSpec(memory_space=pl.ANY)
    whole = [own, other, q, g, image_sum, stats]
    return pl.pallas_call(
        text_side_kernel,
        in_specs=[smem, smem, pl.BlockSpec(memory_space=pltpu.VMEM)]
        + [anywhere] * (len(whole) + NY + NX),
        out_specs=[anywhere, anywhere],
        out_shape=[
            jax.ShapeDtypeStruct((IQ, COLS), F32),
            jax.ShapeDtypeStruct((NY, CT, 2 * COLS), BF16),
        ],
        scratch_shapes=[pltpu.VMEM(a.shape, a.dtype) for a in whole]
        + [
            pltpu.VMEM((NY, NZL, NX, WROWS, 2 * COLS), BF16),
            pltpu.VMEM((CT, 2 * COLS), F32),
            pltpu.VMEM((IQ, COLS), F32),
            pltpu.VMEM((CT, 2 * COLS), BF16),
            pltpu.SemaphoreType.DMA((len(whole),)),
            pltpu.SemaphoreType.DMA((NY, 2 * NX * NZL)),
            pltpu.SemaphoreType.DMA((HEADS,)),
            pltpu.SemaphoreType.DMA((HEADS, 2, NY)),
        ],
        compiler_params=params(56),
        name="text_side",
    )(length, place, gain, *whole, *keys, *values)


def turn_kernel(core_ref, own_ref, other_ref, out_ref):
    core = core_ref[0]
    for i, ref in ((0, own_ref), (1, other_ref)):
        half = core if i == 0 else 1 - core
        out_ref[pl.ds(pl.multiple_of(half * HALF, HALF), HALF), :] = ref[...].T


def turn(core, own, other):
    return pl.pallas_call(
        turn_kernel,
        in_specs=[pl.BlockSpec(memory_space=pltpu.SMEM)]
        + [pl.BlockSpec(memory_space=pltpu.VMEM)] * 2,
        out_shape=jax.ShapeDtypeStruct((CHUNK, NY * CT), BF16),
        compiler_params=params(16),
        name="turn_text",
    )(core, own, other)


def gradient_kernel(text_ref, cot_ref, out_ref):
    out_ref[...] = dot(text_ref[...], cot_ref[...]).astype(BF16)


def gradient(text, cot):
    steps = 2
    return pl.pallas_call(
        gradient_kernel,
        grid=(steps,),
        in_specs=[
            pl.BlockSpec((CHUNK // steps, NY * CT), lambda i: (i, 0)),
            pl.BlockSpec((NY * CT, 2 * COLS), lambda i: (0, 0)),
        ],
        out_specs=pl.BlockSpec((CHUNK // steps, 2 * COLS), lambda i: (i, 0)),
        out_shape=jax.ShapeDtypeStruct((CHUNK, 2 * COLS), BF16),
        compiler_params=params(16),
        name="gradient",
    )(text, cot)


def body(
    enc_resid,
    enc_gain,
    text_in_w,
    key_w,
    value_w,
    key_gain,
    img_query,
    img_keys,
    img_values,
    out_grad,
    cap_lengths,
    assignment,
):
    core = lax.axis_index("c").astype(jnp.int32).reshape(1)
    zl = lax.axis_index("zl")
    sample = (lax.axis_index("y") * NZL + zl) * NX + lax.axis_index("x")
    length = jnp.sum(jnp.where(assignment == sample, cap_lengths, 0)).reshape(1)
    swap = [(0, 1), (1, 0)]
    tie = lax.optimization_barrier

    place = jnp.stack([lax.axis_index(n).astype(jnp.int32) for n in ("y", "zl", "x", "c")])

    def ring(step):
        return [(i, (i + step) % 4) for i in range(4)]

    def image(heads, query, before=()):
        return tuple(image_attention(query, img_keys, img_values, heads, before))

    def around(pair, axis):
        block = jnp.stack(pair)
        two, one, three = [lax.ppermute(block, axis, ring(k)) for k in (2, 1, 3)]
        return [block, one, two, three]

    def beside(block, axis):
        return [lax.ppermute(block, axis, ring(k)) for k in (1, 3)]

    key_pair = [key_w, lax.ppermute(key_w, "zl", swap)]
    value_pair = [value_w, lax.ppermute(value_w, "zl", swap)]

    xg, sq = prepare(assignment, enc_resid, enc_gain.reshape(1, FEAT))
    send = send_part(core, xg, sq, text_in_w)
    summed = keep_part(core, xg, sq, text_in_w, lax.ppermute(send, "c", swap))

    summed, key_pair, value_pair, query = tie((summed, key_pair, value_pair, img_query))
    got = lax.all_to_all(summed, "zh", 0, 0, tiled=True)
    key_x = around(key_pair, "x")
    value_y = around(value_pair, "y")
    part = image((0,), query)
    got, key_x, value_y, length, place, part = tie((got, key_x, value_y, length, place, part))

    text = finish_text(got).reshape(SAMPLES, TOK, HALF)
    text, key_x, value_y, part, query = tie(
        (text, jnp.stack(key_x), jnp.stack(value_y), part, img_query)
    )
    text = lax.all_to_all(text, ("y", "zl", "x"), 0, 0, tiled=True)
    key_1, key_3 = beside(key_x, "y")
    value_1, value_3 = beside(value_y, "x")
    text, key_1, key_3, value_1, value_3 = tie((text, key_1, key_3, value_1, value_3))
    spread = jnp.broadcast_to(text.reshape(1, CT, HALF), (NZH, CT, HALF))
    spread, query, part = tie((spread, query, part))
    own = lax.all_to_all(spread, "zh", 0, 0, tiled=True)
    key_2 = lax.ppermute(key_1, "y", ring(1))
    value_2 = lax.ppermute(value_3, "x", ring(3))
    part = image((1, 2), query, part)
    own, (o, ml), key_2, value_2 = tie((own, part, key_2, value_2))
    other = lax.ppermute(own, "c", swap)
    own_group = lax.all_to_all(own, "y", 0, 0, tiled=True).reshape(NY * CT, HALF)
    attn_out, cot = text_side(
        length,
        place,
        key_gain.reshape(1, HD),
        own,
        other,
        img_query,
        out_grad,
        o,
        ml,
        (key_x, key_1, key_2, key_3),
        (value_y, value_1, value_2, value_3),
    )
    cot, own_group = tie((cot, own_group))
    other_group = lax.ppermute(own_group, "c", swap)
    cot = lax.all_to_all(cot, "y", 0, 0, tiled=True)
    turned = turn(core, own_group, other_group)
    cot, turned = tie((cot, turned))
    cot = cot.reshape(NY * CT, 2 * COLS)
    grad = gradient(turned, cot).reshape(GROUP, WROWS, 2 * COLS)
    grad = lax.all_to_all(grad, ("zl", "x"), 0, 0, tiled=True)
    total = jnp.sum(grad.astype(F32), axis=0)
    return (attn_out, total[:, :COLS], total[:, COLS:])


def solution(mesh):
    fine = Mesh(mesh.devices.reshape(NY, NZL, NX, NZH, NC), ("y", "zl", "x", "zh", "c"))
    dp, mp = ("y", "zl", "x"), ("zh", "c")
    return jax.shard_map(
        body,
        mesh=fine,
        in_specs=(
            P(None, dp, mp),
            P(mp),
            P(mp, None),
            P(dp, mp),
            P(dp, mp),
            P(),
            P(dp, mp),
            P(dp, mp),
            P(dp, mp),
            P(dp, mp),
            P(),
            P(),
        ),
        out_specs=(P(dp, mp), P(dp, mp), P(dp, mp)),
        check_vma=False,
    )
```

time: 641 us -> 154 us (0.24)
  waiting for transfers between devices: 358 us -> 26.9 us
  matrix products: 83.3 us -> 0 us
  blocking collectives: 116 us -> 35.5 us
  Pallas kernels: 0 us -> 36.7 us
  starting transfers between devices: 8.14 us -> 43.2 us
  local copies, waits for them, and re-layouts: 37.6 us -> 8.25 us
  other arithmetic: 21.8 us -> 1.63 us
  between operations: 13.8 us -> 0.89 us
    reduce_scatter x1 -> x0, waiting for transfers between devices: 181 us -> none  [body(): lax.psum_scatter(lax.dot_general(columns, both_cots, (((0,), (0,)), ((),...]
    all_gather x2 -> x0, waiting for transfers between devices: 175 us -> none  [the longest x1 154 us: body(): key_piece = lax.all_gather(key_w, 'dp', axis=0, tiled=True)]
    psum x2 -> x0, blocking collectives: 116 us -> none  [the longest x1 87.8 us: text_features(): return lax.psum(partial_sums, 'mp').astype(jnp.bfloat16)]
    dot_general x29 -> x0, matrix products: 83.3 us -> none  [the longest x6 26.5 us: head_attend(): jnp.dot(image_probs, image_values, preferred_element_type=jnp.float32)]
    pallas_call x0 -> x9, Pallas kernels: none -> 36.7 us  [the longest x2 17.9 us: image_attention(): pl.pallas_call(functools.partial(image_kernel, block=512, rows=256), grid...]
    all_to_all x0 -> x2, blocking collectives: none -> 35.5 us  [the longest x1 19.3 us: body(): grad = lax.all_to_all(grad, ('zl', 'x'), 0, 0, tiled=True)]
    all_to_all x1 -> x4, waiting for transfers between devices: 0.01 us -> 22.8 us  [the longest x1 17.2 us: body(): cot = lax.all_to_all(cot, 'y', 0, 0, tiled=True)]
    ppermute x0 -> x17, starting transfers between devices: none -> 21.8 us  [the longest x6 11.6 us: around(): two, one, three = [lax.ppermute(block, axis, ring(k)) for k in (2, 1, 3)]]
  transfers between devices with their start and end apart: 4 -> 21, of which waited for: 3 -> 8; matrix products, arithmetic and copies ran while one was open for 4% -> 1% of each run, Pallas kernels for 0% -> 21%
where the time goes in v2:
time: 154 us; the launch traced here: 153 us
  starting transfers between devices  43.2 us (28%)
  Pallas kernels  36.7 us (24%)
  blocking collectives  35.5 us (23%)
  waiting for transfers between devices  26.9 us (17%)
  local copies, waits for them, and re-layouts  8.25 us (5%)
  other arithmetic  1.63 us (1%)
    all_to_all x1, blocking collectives, body(): grad = lax.all_to_all(grad, ('zl', 'x'), 0, 0, tiled=True)  19.3 us
    pallas_call x2, Pallas kernels, image_attention(): pl.pallas_call(functools.partial(image_kernel, block=512, rows=256), grid...  17.9 us
    all_to_all x1, waiting for transfers between devices, body(): cot = lax.all_to_all(cot, 'y', 0, 0, tiled=True)  17.2 us
    all_to_all x1, blocking collectives, body(): text = lax.all_to_all(text, ('y', 'zl', 'x'), 0, 0, tiled=True)  16.2 us
    pallas_call x1, Pallas kernels, text_side(): pl.pallas_call(text_side_kernel, in_specs=[smem, smem, pl.BlockSpec(memor...  11.9 us
    ppermute x6, starting transfers between devices, around(): two, one, three = [lax.ppermute(block, axis, ring(k)) for k in (2, 1, 3)]  11.6 us
    all_to_all x1, starting transfers between devices, body(): got = lax.all_to_all(summed, 'zh', 0, 0, tiled=True)  7.96 us
    ppermute x4, starting transfers between devices, beside(): return [lax.ppermute(block, axis, ring(k)) for k in (1, 3)]  6.51 us
  transfers between devices with their start and end apart: 21, of which 8 were waited for; matrix products, arithmetic and copies ran while one was open for 1% of the time, Pallas kernels for 21%

profile of v2, /device:TPU:64, one launch (start us, length us, event | category | flops | bytes accessed | tf_op | source)
XLA Modules:
  0.0 153.1 jit_solution(7479815799135783420)
XLA Ops:
  0.6 0.9 copy-done.3
  1.6 0.7 copy-done.4
  2.3 0.7 copy-done.5
  2.9 0.8 prepare.1
  3.7 1.9 %copy-done = bf16[512,3072]{1,0:T(8,128)(2,1)S(1)} copy-done((bf16[512,3072]{1,0:T(8,128)(2,1)S(1)}, bf16[512,3072]{1,0:T(8,128)(2,1)}, u32[]{:S(2)}) %copy-start) | copy-done | bytes 3145752
  5.6 1.4 text_other_half.1
  7.2 2.0 %collective-permute-start.1 = (bf16[96,384]{1,0:T(8,128)(2,1)S(1)}, bf16[96,384]{1,0:T(8,128)(2,1)S(1)}, u32[]{:S(2)}, u32[]{:S(2)}) collective-permute-start(bf16[96,384]{1,0:T(8,128)(2,1)S(1)} %copy-done.17), channel_id=1, source_target_pairs={{0,32},{32,0},{1,33},{33,1},{2,34},{34,2},{3,35},{35,3},{4,36},{36... | collective-permute-start | bytes 221192 | tf_op jit(solution)/shard_map/ppermute | solution.py:406
  9.2 0.1 collective-permute-start.2
  9.3 0.2 collective-permute-done.got_ref
  9.5 2.4 %text_own_half.1 = bf16[4,272,384]{2,1,0:T(8,128)(2,1)} custom-call(s32[1]{0:T(128)} %bitcast.core_ref, bf16[256,512]{1,0:T(8,128)(2,1)S(1)} %get-tuple-element.54.xg_ref, f32[8,256]{1,0:T(8,128)S(1)} %get-tuple-element.55.sq_ref, bf16[512,3072]{1,0:T(8,128)(2,1)S(1)} %copy-done, bf16[4,272,384]{2,1,0:T(8,128)(2,1)S(1)} %collective-permute-done.got_ref), custom_call_target="tpu_custom_call" | custom-call | tf_op jit(solution)/shard_map/text_own_half/pallas_call | solution.py:117
  11.9 0.2 collective-permute-done.1
  12.1 1.5 collective-permute-done.2
  13.6 8.0 %all-to-all-start = ((bf16[4,272,384]{2,1,0:T(8,128)(2,1)}), bf16[4,272,384]{2,1,0:T(8,128)(2,1)S(1)}, u32[]{:S(2)}, u32[]{:S(2)}) async-start(bf16[4,272,384]{2,1,0:T(8,128)(2,1)} %text_own_half.1), calls=%async_computation | async-start | bytes 1671168 | tf_op jit(solution)/shard_map/all_to_all | solution.py:414
  21.6 1.7 %collective-permute-start.6 = (bf16[2,96,384]{2,1,0:T(8,128)(2,1)S(1)}, bf16[2,96,384]{2,1,0:T(8,128)(2,1)S(1)}, u32[]{:S(2)}, u32[]{:S(2)}) collective-permute-start(bf16[2,96,384]{2,1,0:T(8,128)(2,1)S(1)} %pad_maximum_fusion.3), channel_id=1, source_target_pairs={{0,64},{64,128},{128,192},{192,0},{1,65},{65,129},{129,193},{193,1... | collective-permute-start | bytes 442376 | tf_op jit(solution)/shard_map/ppermute | solution.py:400
  23.2 2.9 %collective-permute-start.7 = (bf16[2,96,384]{2,1,0:T(8,128)(2,1)S(1)}, bf16[2,96,384]{2,1,0:T(8,128)(2,1)S(1)}, u32[]{:S(2)}, u32[]{:S(2)}) collective-permute-start(bf16[2,96,384]{2,1,0:T(8,128)(2,1)S(1)} %pad_maximum_fusion.3), channel_id=1, source_target_pairs={{0,128},{64,192},{128,0},{192,64},{1,129},{65,193},{129,1},{193,65... | collective-permute-start | bytes 442376 | tf_op jit(solution)/shard_map/ppermute | solution.py:400
  26.1 1.3 collective-permute-start.8
  27.5 1.6 %collective-permute-start.3 = (bf16[2,96,384]{2,1,0:T(8,128)(2,1)S(1)}, bf16[2,96,384]{2,1,0:T(8,128)(2,1)S(1)}, u32[]{:S(2)}, u32[]{:S(2)}) collective-permute-start(bf16[2,96,384]{2,1,0:T(8,128)(2,1)S(1)} %pad_maximum_fusion.2), channel_id=1, source_target_pairs={{0,8},{8,16},{16,24},{24,0},{1,9},{9,17},{17,25},{25,1},{2,10},{10... | collective-permute-start | bytes 442376 | tf_op jit(solution)/shard_map/ppermute | solution.py:400
  29.1 2.7 %collective-permute-start.4 = (bf16[2,96,384]{2,1,0:T(8,128)(2,1)S(1)}, bf16[2,96,384]{2,1,0:T(8,128)(2,1)S(1)}, u32[]{:S(2)}, u32[]{:S(2)}) collective-permute-start(bf16[2,96,384]{2,1,0:T(8,128)(2,1)S(1)} %pad_maximum_fusion.2), channel_id=1, source_target_pairs={{0,16},{8,24},{16,0},{24,8},{1,17},{9,25},{17,1},{25,9},{2,18},{10... | collective-permute-start | bytes 442376 | tf_op jit(solution)/shard_map/ppermute | solution.py:400
  31.8 1.4 collective-permute-start.5
  33.2 0.6 pad_add_fusion.place_ref
  33.8 0.6 fusion
  34.5 6.8 %image_attention.2 = (f32[768,384]{1,0:T(8,128)}, f32[768,384]{1,0:T(8,128)}) custom-call(bf16[768,384]{1,0:T(8,128)(2,1)} %refs_2_.1, bf16[4096,384]{1,0:T(8,128)(2,1)} %k_ref.3, bf16[4096,384]{1,0:T(8,128)(2,1)} %v_ref.3), custom_call_target="tpu_custom_call" | custom-call | flops 1 | bytes 1 | tf_op jit(solution)/shard_map/image_attention/pallas_call | solution.py:179
  41.3 1.8 %all-to-all-done.got_ref = bf16[4,272,384]{2,1,0:T(8,128)(2,1)S(1)} async-done(((bf16[4,272,384]{2,1,0:T(8,128)(2,1)}), bf16[4,272,384]{2,1,0:T(8,128)(2,1)S(1)}, u32[]{:S(2)}, u32[]{:S(2)}) %all-to-all-start) | async-done | bytes 835616 | tf_op jit(solution)/shard_map/all_to_all | solution.py:414
  43.1 0.2 finish_text.1
  43.3 0.2 pad_maximum_fusion
  43.6 3.3 %collective-permute-start.10 = (bf16[4,2,96,384]{3,2,1,0:T(8,128)(2,1)S(1)}, bf16[4,2,96,384]{3,2,1,0:T(8,128)(2,1)S(1)}, u32[]{:S(2)}, u32[]{:S(2)}) collective-permute-start(bf16[4,2,96,384]{3,2,1,0:T(8,128)(2,1)S(1)} %get-tuple-element.78.refs_6_), channel_id=1, source_target_pairs={{0,192},{64,0},{128,64},{192,128},{1,193},{65,1},{129,65},{193,129... | collective-permute-start | bytes 1769480 | tf_op jit(solution)/shard_map/ppermute | solution.py:404
  46.8 1.5 collective-permute-start.11
  48.3 1.7 %collective-permute-start.12 = (bf16[4,2,96,384]{3,2,1,0:T(8,128)(2,1)S(1)}, bf16[4,2,96,384]{3,2,1,0:T(8,128)(2,1)S(1)}, u32[]{:S(2)}, u32[]{:S(2)}) collective-permute-start(bf16[4,2,96,384]{3,2,1,0:T(8,128)(2,1)S(1)} %get-tuple-element.79.refs_10_), channel_id=1, source_target_pairs={{0,24},{8,0},{16,8},{24,16},{1,25},{9,1},{17,9},{25,17},{2,26},{10... | collective-permute-start | bytes 1769480 | tf_op jit(solution)/shard_map/ppermute | solution.py:404
  50.1 16.2 %all_to_all.30 = bf16[32,8,384]{2,1,0:T(8,128)(2,1)S(1)} all-to-all(bf16[32,8,384]{2,1,0:T(8,128)(2,1)S(1)} %bitcast.28), channel_id=1, replica_groups=mesh['y'=4,'zl'=2,'x'=4,'zh'=4,'c'=2] {'y','zl','x'}, dimensions={0} | all-to-all | bytes 393216 | tf_op jit(solution)/shard_map/all_to_all | solution.py:424
  66.4 1.0 broadcast_in_dim.13
  67.4 0.2 copy-done.11
  67.6 5.2 %all-to-all-start.2 = ((bf16[4,256,384]{2,1,0:T(8,128)(2,1)}), bf16[4,256,384]{2,1,0:T(8,128)(2,1)}, u32[]{:S(2)}, u32[]{:S(2)}) async-start(bf16[4,256,384]{2,1,0:T(8,128)(2,1)} %broadcast_in_dim.13), calls=%async_computation.2 | async-start | bytes 1572864 | tf_op jit(solution)/shard_map/all_to_all | solution.py:430
  72.8 0.6 collective-permute-start.13
  73.4 0.8 collective-permute-start.14
  74.3 11.1 %image_attention.3 = (f32[768,384]{1,0:T(8,128)}, f32[768,384]{1,0:T(8,128)}) custom-call(bf16[768,384]{1,0:T(8,128)(2,1)} %refs_2_.1, bf16[4096,384]{1,0:T(8,128)(2,1)} %k_ref.3, bf16[4096,384]{1,0:T(8,128)(2,1)} %v_ref.3, f32[768,384]{1,0:T(8,128)} %get-tuple-element.86.refs_0_, ...), custom_call_target="tpu_custom_call", output_to_operand_aliasing={{0}: (3, {}), {1}: (4, {})} | custom-call | flops 1 | bytes 1 | tf_op jit(solution)/shard_map/image_attention/pallas_call | solution.py:179
  85.4 3.7 %all-to-all-done.2.refs_0_ = bf16[4,256,384]{2,1,0:T(8,128)(2,1)} async-done(((bf16[4,256,384]{2,1,0:T(8,128)(2,1)}), bf16[4,256,384]{2,1,0:T(8,128)(2,1)}, u32[]{:S(2)}, u32[]{:S(2)}) %all-to-all-start.2) | async-done | bytes 786464 | tf_op jit(solution)/shard_map/all_to_all | solution.py:430
  89.0 3.7 %all-to-all-start.3 = ((bf16[4,256,384]{2,1,0:T(8,128)(2,1)}), bf16[4,256,384]{2,1,0:T(8,128)(2,1)S(1)}, u32[]{:S(2)}, u32[]{:S(2)}) async-start(bf16[4,256,384]{2,1,0:T(8,128)(2,1)} %all-to-all-done.2.refs_0_), calls=%async_computation.3 | async-start | bytes 1572864 | tf_op jit(solution)/shard_map/all_to_all | solution.py:436
  92.8 0.9 copy-done.9
  93.7 11.9 %text_side.1 = (f32[768,384]{1,0:T(8,128)}, bf16[4,256,768]{2,1,0:T(8,128)(2,1)}) custom-call(s32[1]{0:T(128)} %bitcast.6.length_ref, s32[4]{0:T(128)} %pad_add_fusion.place_ref, f32[1,128]{1,0:T(1,128)} %bitcast.43, bf16[4,256,384]{2,1,0:T(8,128)(2,1)} %all-to-all-done.2.refs_0_, bf16[4,256,384]{2,1,0:T(8,128)(2,1)} %copy-done.9, bf16[768,384]{1,0:T(8,128)(2,1)} %refs_2_.1, ...), custom_call_target="tpu_custom_call" | custom-call | tf_op jit(solution)/shard_map/text_side/pallas_call | solution.py:306
  105.7 4.5 %all-to-all-start.4 = ((bf16[4,256,768]{2,1,0:T(8,128)(2,1)}), bf16[4,256,768]{2,1,0:T(8,128)(2,1)S(1)}, u32[]{:S(2)}, u32[]{:S(2)}) async-start(bf16[4,256,768]{2,1,0:T(8,128)(2,1)} %get-tuple-element.101), calls=%async_computation.4 | async-start | bytes 3145728 | tf_op jit(solution)/shard_map/all_to_all | solution.py:452
  110.2 2.3 %collective-permute-done.16.other_ref = bf16[1024,384]{1,0:T(8,128)(2,1)S(1)} collective-permute-done((bf16[1024,384]{1,0:T(8,128)(2,1)S(1)}, bf16[1024,384]{1,0:T(8,128)(2,1)S(1)}, u32[]{:S(2)}, u32[]{:S(2)}) %collective-permute-start.16) | collective-permute-done | bytes 786464 | tf_op jit(solution)/shard_map/ppermute | solution.py:451
  112.5 1.1 copy-done.2
  113.6 0.5 turn_text.1.text_ref
  114.1 17.2 %all-to-all-done.4 = bf16[4,256,768]{2,1,0:T(8,128)(2,1)S(1)} async-done(((bf16[4,256,768]{2,1,0:T(8,128)(2,1)}), bf16[4,256,768]{2,1,0:T(8,128)(2,1)S(1)}, u32[]{:S(2)}, u32[]{:S(2)}) %all-to-all-start.4) | async-done | bytes 1572896 | tf_op jit(solution)/shard_map/all_to_all | solution.py:452
  131.3 1.6 %gradient.1 = bf16[768,768]{1,0:T(8,128)(2,1)S(1)} custom-call(bf16[768,1024]{1,0:T(8,128)(2,1)S(1)} %turn_text.1.text_ref, bf16[1024,768]{1,0:T(8,128)(2,1)S(1)} %bitcast.24), custom_call_target="tpu_custom_call" | custom-call | tf_op jit(solution)/shard_map/gradient/pallas_call | solution.py:355
  132.9 19.3 %all_to_all.31 = bf16[8,96,768]{2,1,0:T(8,128)(2,1)S(1)} all-to-all(bf16[8,96,768]{2,1,0:T(8,128)(2,1)S(1)} %bitcast.25), channel_id=1, replica_groups=mesh['y'=4,'zl'=2,'x'=4,'zh'=4,'c'=2] {'zl','x'}, dimensions={0} | all-to-all | bytes 2359296 | tf_op jit(solution)/shard_map/all_to_all | solution.py:457
  152.2 0.2 convert_reduce_fusion
  152.4 0.7 fusion.1
  (51 shorter events, 0.3 us)
Async XLA Ops:
  0.6 1.0 copy-start.3
  1.6 0.7 copy-start.4
  2.3 0.7 copy-start.5
  3.7 1.9 %copy-start = (bf16[512,3072]{1,0:T(8,128)(2,1)S(1)}, bf16[512,3072]{1,0:T(8,128)(2,1)}, u32[]{:S(2)}) copy-start(bf16[512,3072]{1,0:T(8,128)(2,1)} %w_ref.3) | copy-start | bytes 9437188
  5.6 1.5 %copy-start.17 = (bf16[96,384]{1,0:T(8,128)(2,1)S(1)}, bf16[96,384]{1,0:T(8,128)(2,1)}, u32[]{:S(2)}) copy-start(bf16[96,384]{1,0:T(8,128)(2,1)} %param.15) | copy-start | bytes 221188
  5.6 3.5 %copy-start.16 = (bf16[96,384]{1,0:T(8,128)(2,1)S(1)}, bf16[96,384]{1,0:T(8,128)(2,1)}, u32[]{:S(2)}) copy-start(bf16[96,384]{1,0:T(8,128)(2,1)} %param.16) | copy-start | bytes 221188
  7.0 2.4 %collective-permute-start = (bf16[4,272,384]{2,1,0:T(8,128)(2,1)S(1)}, bf16[4,272,384]{2,1,0:T(8,128)(2,1)S(1)}, u32[]{:S(2)}, u32[]{:S(2)}) collective-permute-start(bf16[4,272,384]{2,1,0:T(8,128)(2,1)S(1)} %text_other_half.1), channel_id=1, source_target_pairs={{0,1},{1,0},{2,3},{3,2},{4,5},{5,4},{6,7},{7,6},{8,9},{9,8},{10,11... | collective-permute-start | bytes 2506760 | tf_op jit(solution)/shard_map/ppermute | solution.py:411
  7.2 4.9 %collective-permute-start.1 = (bf16[96,384]{1,0:T(8,128)(2,1)S(1)}, bf16[96,384]{1,0:T(8,128)(2,1)S(1)}, u32[]{:S(2)}, u32[]{:S(2)}) collective-permute-start(bf16[96,384]{1,0:T(8,128)(2,1)S(1)} %copy-done.17), channel_id=1, source_target_pairs={{0,32},{32,0},{1,33},{33,1},{2,34},{34,2},{3,35},{35,3},{4,36},{36... | collective-permute-start | bytes 221192 | tf_op jit(solution)/shard_map/ppermute | solution.py:406
  9.2 4.4 %collective-permute-start.2 = (bf16[96,384]{1,0:T(8,128)(2,1)S(1)}, bf16[96,384]{1,0:T(8,128)(2,1)S(1)}, u32[]{:S(2)}, u32[]{:S(2)}) collective-permute-start(bf16[96,384]{1,0:T(8,128)(2,1)S(1)} %copy-done.16), channel_id=1, source_target_pairs={{0,32},{32,0},{1,33},{33,1},{2,34},{34,2},{3,35},{35,3},{4,36},{36... | collective-permute-start | bytes 221192 | tf_op jit(solution)/shard_map/ppermute | solution.py:407
  11.9 21.9 %copy-start.6 = (s32[32]{0:T(128)S(1)}, s32[32]{0:T(128)}, u32[]{:S(2)}) copy-start(s32[32]{0:T(128)} %assign_ref.1) | copy-start | bytes 388
  11.9 21.9 %copy-start.18 = (s32[32]{0:T(128)S(1)}, s32[32]{0:T(128)}, u32[]{:S(2)}) copy-start(s32[32]{0:T(128)} %param.22) | copy-start | bytes 388
  13.6 29.6 %all-to-all-start = ((bf16[4,272,384]{2,1,0:T(8,128)(2,1)}), bf16[4,272,384]{2,1,0:T(8,128)(2,1)S(1)}, u32[]{:S(2)}, u32[]{:S(2)}) async-start(bf16[4,272,384]{2,1,0:T(8,128)(2,1)} %text_own_half.1), calls=%async_computation | async-start | bytes 1671168 | tf_op jit(solution)/shard_map/all_to_all | solution.py:414
  21.6 10.2 %collective-permute-start.6 = (bf16[2,96,384]{2,1,0:T(8,128)(2,1)S(1)}, bf16[2,96,384]{2,1,0:T(8,128)(2,1)S(1)}, u32[]{:S(2)}, u32[]{:S(2)}) collective-permute-start(bf16[2,96,384]{2,1,0:T(8,128)(2,1)S(1)} %pad_maximum_fusion.3), channel_id=1, source_target_pairs={{0,64},{64,128},{128,192},{192,0},{1,65},{65,129},{129,193},{193,1... | collective-permute-start | bytes 442376 | tf_op jit(solution)/shard_map/ppermute | solution.py:400
  23.2 18.1 %collective-permute-start.7 = (bf16[2,96,384]{2,1,0:T(8,128)(2,1)S(1)}, bf16[2,96,384]{2,1,0:T(8,128)(2,1)S(1)}, u32[]{:S(2)}, u32[]{:S(2)}) collective-permute-start(bf16[2,96,384]{2,1,0:T(8,128)(2,1)S(1)} %pad_maximum_fusion.3), channel_id=1, source_target_pairs={{0,128},{64,192},{128,0},{192,64},{1,129},{65,193},{129,1},{193,65... | collective-permute-start | bytes 442376 | tf_op jit(solution)/shard_map/ppermute | solution.py:400
  26.1 15.2 %collective-permute-start.8 = (bf16[2,96,384]{2,1,0:T(8,128)(2,1)S(1)}, bf16[2,96,384]{2,1,0:T(8,128)(2,1)S(1)}, u32[]{:S(2)}, u32[]{:S(2)}) collective-permute-start(bf16[2,96,384]{2,1,0:T(8,128)(2,1)S(1)} %pad_maximum_fusion.3), channel_id=1, source_target_pairs={{0,192},{64,0},{128,64},{192,128},{1,193},{65,1},{129,65},{193,129... | collective-permute-start | bytes 442376 | tf_op jit(solution)/shard_map/ppermute | solution.py:400
  27.5 13.8 %collective-permute-start.3 = (bf16[2,96,384]{2,1,0:T(8,128)(2,1)S(1)}, bf16[2,96,384]{2,1,0:T(8,128)(2,1)S(1)}, u32[]{:S(2)}, u32[]{:S(2)}) collective-permute-start(bf16[2,96,384]{2,1,0:T(8,128)(2,1)S(1)} %pad_maximum_fusion.2), channel_id=1, source_target_pairs={{0,8},{8,16},{16,24},{24,0},{1,9},{9,17},{17,25},{25,1},{2,10},{10... | collective-permute-start | bytes 442376 | tf_op jit(solution)/shard_map/ppermute | solution.py:400
  29.1 12.2 %collective-permute-start.4 = (bf16[2,96,384]{2,1,0:T(8,128)(2,1)S(1)}, bf16[2,96,384]{2,1,0:T(8,128)(2,1)S(1)}, u32[]{:S(2)}, u32[]{:S(2)}) collective-permute-start(bf16[2,96,384]{2,1,0:T(8,128)(2,1)S(1)} %pad_maximum_fusion.2), channel_id=1, source_target_pairs={{0,16},{8,24},{16,0},{24,8},{1,17},{9,25},{17,1},{25,9},{2,18},{10... | collective-permute-start | bytes 442376 | tf_op jit(solution)/shard_map/ppermute | solution.py:400
  31.8 9.5 %collective-permute-start.5 = (bf16[2,96,384]{2,1,0:T(8,128)(2,1)S(1)}, bf16[2,96,384]{2,1,0:T(8,128)(2,1)S(1)}, u32[]{:S(2)}, u32[]{:S(2)}) collective-permute-start(bf16[2,96,384]{2,1,0:T(8,128)(2,1)S(1)} %pad_maximum_fusion.2), channel_id=1, source_target_pairs={{0,24},{8,0},{16,8},{24,16},{1,25},{9,1},{17,9},{25,17},{2,26},{10... | collective-permute-start | bytes 442376 | tf_op jit(solution)/shard_map/ppermute | solution.py:400
  43.5 23.9 %copy-start.7 = (bf16[4,2,96,384]{3,2,1,0:T(8,128)(2,1)}, bf16[4,2,96,384]{3,2,1,0:T(8,128)(2,1)S(1)}, u32[]{:S(2)}) copy-start(bf16[4,2,96,384]{3,2,1,0:T(8,128)(2,1)S(1)} %get-tuple-element.78.refs_6_) | copy-start | bytes 1769476
  43.6 23.9 %copy-start.8 = (bf16[4,2,96,384]{3,2,1,0:T(8,128)(2,1)}, bf16[4,2,96,384]{3,2,1,0:T(8,128)(2,1)S(1)}, u32[]{:S(2)}) copy-start(bf16[4,2,96,384]{3,2,1,0:T(8,128)(2,1)S(1)} %get-tuple-element.79.refs_10_) | copy-start | bytes 1769476
  43.6 22.7 %collective-permute-start.10 = (bf16[4,2,96,384]{3,2,1,0:T(8,128)(2,1)S(1)}, bf16[4,2,96,384]{3,2,1,0:T(8,128)(2,1)S(1)}, u32[]{:S(2)}, u32[]{:S(2)}) collective-permute-start(bf16[4,2,96,384]{3,2,1,0:T(8,128)(2,1)S(1)} %get-tuple-element.78.refs_6_), channel_id=1, source_target_pairs={{0,192},{64,0},{128,64},{192,128},{1,193},{65,1},{129,65},{193,129... | collective-permute-start | bytes 1769480 | tf_op jit(solution)/shard_map/ppermute | solution.py:404
  46.8 19.5 %collective-permute-start.11 = (bf16[4,2,96,384]{3,2,1,0:T(8,128)(2,1)S(1)}, bf16[4,2,96,384]{3,2,1,0:T(8,128)(2,1)S(1)}, u32[]{:S(2)}, u32[]{:S(2)}) collective-permute-start(bf16[4,2,96,384]{3,2,1,0:T(8,128)(2,1)S(1)} %get-tuple-element.79.refs_10_), channel_id=1, source_target_pairs={{0,8},{8,16},{16,24},{24,0},{1,9},{9,17},{17,25},{25,1},{2,10},{10... | collective-permute-start | bytes 1769480 | tf_op jit(solution)/shard_map/ppermute | solution.py:404
  48.3 18.0 %collective-permute-start.12 = (bf16[4,2,96,384]{3,2,1,0:T(8,128)(2,1)S(1)}, bf16[4,2,96,384]{3,2,1,0:T(8,128)(2,1)S(1)}, u32[]{:S(2)}, u32[]{:S(2)}) collective-permute-start(bf16[4,2,96,384]{3,2,1,0:T(8,128)(2,1)S(1)} %get-tuple-element.79.refs_10_), channel_id=1, source_target_pairs={{0,24},{8,0},{16,8},{24,16},{1,25},{9,1},{17,9},{25,17},{2,26},{10... | collective-permute-start | bytes 1769480 | tf_op jit(solution)/shard_map/ppermute | solution.py:404
  50.1 16.3 %collective-permute-start.9 = (bf16[4,2,96,384]{3,2,1,0:T(8,128)(2,1)S(1)}, bf16[4,2,96,384]{3,2,1,0:T(8,128)(2,1)S(1)}, u32[]{:S(2)}, u32[]{:S(2)}) collective-permute-start(bf16[4,2,96,384]{3,2,1,0:T(8,128)(2,1)S(1)} %get-tuple-element.78.refs_6_), channel_id=1, source_target_pairs={{0,64},{64,128},{128,192},{192,0},{1,65},{65,129},{129,193},{193,1... | collective-permute-start | bytes 1769480 | tf_op jit(solution)/shard_map/ppermute | solution.py:404
  66.3 1.1 copy-start.10
  66.3 1.3 copy-start.11
  66.3 7.1 %copy-start.12 = (bf16[4,2,96,384]{3,2,1,0:T(8,128)(2,1)}, bf16[4,2,96,384]{3,2,1,0:T(8,128)(2,1)S(1)}, u32[]{:S(2)}) copy-start(bf16[4,2,96,384]{3,2,1,0:T(8,128)(2,1)S(1)} %collective-permute-done.12.refs_13_) | copy-start | bytes 1769476
  66.3 19.0 %copy-start.13 = (bf16[4,2,96,384]{3,2,1,0:T(8,128)(2,1)}, bf16[4,2,96,384]{3,2,1,0:T(8,128)(2,1)S(1)}, u32[]{:S(2)}) copy-start(bf16[4,2,96,384]{3,2,1,0:T(8,128)(2,1)S(1)} %collective-permute-done.9.refs_7_) | copy-start | bytes 1769476
  67.6 21.4 %all-to-all-start.2 = ((bf16[4,256,384]{2,1,0:T(8,128)(2,1)}), bf16[4,256,384]{2,1,0:T(8,128)(2,1)}, u32[]{:S(2)}, u32[]{:S(2)}) async-start(bf16[4,256,384]{2,1,0:T(8,128)(2,1)} %broadcast_in_dim.13), calls=%async_computation.2 | async-start | bytes 1572864 | tf_op jit(solution)/shard_map/all_to_all | solution.py:430
  72.8 12.5 %collective-permute-start.13 = (bf16[4,2,96,384]{3,2,1,0:T(8,128)(2,1)S(1)}, bf16[4,2,96,384]{3,2,1,0:T(8,128)(2,1)S(1)}, u32[]{:S(2)}, u32[]{:S(2)}) collective-permute-start(bf16[4,2,96,384]{3,2,1,0:T(8,128)(2,1)S(1)} %collective-permute-done.9.refs_7_), channel_id=1, source_target_pairs={{0,64},{64,128},{128,192},{192,0},{1,65},{65,129},{129,193},{193,1... | collective-permute-start | bytes 1769480 | tf_op jit(solution)/shard_map/ppermute | solution.py:431
  73.4 11.9 %collective-permute-start.14 = (bf16[4,2,96,384]{3,2,1,0:T(8,128)(2,1)S(1)}, bf16[4,2,96,384]{3,2,1,0:T(8,128)(2,1)S(1)}, u32[]{:S(2)}, u32[]{:S(2)}) collective-permute-start(bf16[4,2,96,384]{3,2,1,0:T(8,128)(2,1)S(1)} %collective-permute-done.12.refs_13_), channel_id=1, source_target_pairs={{0,24},{8,0},{16,8},{24,16},{1,25},{9,1},{17,9},{25,17},{2,26},{10... | collective-permute-start | bytes 1769480 | tf_op jit(solution)/shard_map/ppermute | solution.py:432
  85.3 7.4 %copy-start.14 = (bf16[4,2,96,384]{3,2,1,0:T(8,128)(2,1)}, bf16[4,2,96,384]{3,2,1,0:T(8,128)(2,1)S(1)}, u32[]{:S(2)}) copy-start(bf16[4,2,96,384]{3,2,1,0:T(8,128)(2,1)S(1)} %collective-permute-done.13.refs_8_) | copy-start | bytes 1769476
  85.4 7.4 %copy-start.15 = (bf16[4,2,96,384]{3,2,1,0:T(8,128)(2,1)}, bf16[4,2,96,384]{3,2,1,0:T(8,128)(2,1)S(1)}, u32[]{:S(2)}) copy-start(bf16[4,2,96,384]{3,2,1,0:T(8,128)(2,1)S(1)} %collective-permute-done.14.refs_12_) | copy-start | bytes 1769476
  89.0 3.7 %collective-permute-start.15 = (bf16[4,256,384]{2,1,0:T(8,128)(2,1)}, bf16[4,256,384]{2,1,0:T(8,128)(2,1)S(1)}, u32[]{:S(2)}, u32[]{:S(2)}) collective-permute-start(bf16[4,256,384]{2,1,0:T(8,128)(2,1)} %all-to-all-done.2.refs_0_), channel_id=1, source_target_pairs={{0,1},{1,0},{2,3},{3,2},{4,5},{5,4},{6,7},{7,6},{8,9},{9,8},{10,11... | collective-permute-start | bytes 2359304 | tf_op jit(solution)/shard_map/ppermute | solution.py:435
  89.0 16.7 %all-to-all-start.3 = ((bf16[4,256,384]{2,1,0:T(8,128)(2,1)}), bf16[4,256,384]{2,1,0:T(8,128)(2,1)S(1)}, u32[]{:S(2)}, u32[]{:S(2)}) async-start(bf16[4,256,384]{2,1,0:T(8,128)(2,1)} %all-to-all-done.2.refs_0_), calls=%async_computation.3 | async-start | bytes 1572864 | tf_op jit(solution)/shard_map/all_to_all | solution.py:436
  92.8 0.9 copy-start.9
  105.7 4.5 %copy-start.1 = (bf16[4,256,384]{2,1,0:T(8,128)(2,1)}, bf16[4,256,384]{2,1,0:T(8,128)(2,1)S(1)}, u32[]{:S(2)}) copy-start(bf16[4,256,384]{2,1,0:T(8,128)(2,1)S(1)} %all-to-all-done.3) | copy-start | bytes 2359300
  105.7 25.6 %all-to-all-start.4 = ((bf16[4,256,768]{2,1,0:T(8,128)(2,1)}), bf16[4,256,768]{2,1,0:T(8,128)(2,1)S(1)}, u32[]{:S(2)}, u32[]{:S(2)}) async-start(bf16[4,256,768]{2,1,0:T(8,128)(2,1)} %get-tuple-element.101), calls=%async_computation.4 | async-start | bytes 3145728 | tf_op jit(solution)/shard_map/all_to_all | solution.py:452
  110.2 2.3 %collective-permute-start.16 = (bf16[1024,384]{1,0:T(8,128)(2,1)S(1)}, bf16[1024,384]{1,0:T(8,128)(2,1)S(1)}, u32[]{:S(2)}, u32[]{:S(2)}) collective-permute-start(bf16[1024,384]{1,0:T(8,128)(2,1)S(1)} %bitcast.26), channel_id=1, source_target_pairs={{0,1},{1,0},{2,3},{3,2},{4,5},{5,4},{6,7},{7,6},{8,9},{9,8},{10,11... | collective-permute-start | bytes 2359304 | tf_op jit(solution)/shard_map/ppermute | solution.py:451
  112.5 1.1 copy-start.2

commit v3 on v2

--- a/solution.py
+++ b/solution.py
@@ -27,6 +27,8 @@
 HALF = CHUNK // NC
 GROUP = NZL * NX
 IMAGE_MIB = 56
+SORT_MIB = 56
+FETCH_MIB = 32
 WROWS = D // SAMPLES
 EXTRA = 16
 ROWS = CT + EXTRA
@@ -56,54 +58,85 @@
     return jnp.sum(block[:, :CT].astype(F32), axis=0, keepdims=True)
 
 
-def prepare_kernel(assign_ref, x_ref, gain_ref, xg_ref, sq_ref, rows, squares):
-    gain = gain_ref[...]
+def sort_kernel(assign_ref, x_ref, out_ref):
     for c in range(SAMPLES):
-        start = pl.multiple_of(assign_ref[c] * TOK, TOK)
-        values = x_ref[c].astype(F32)
-        rows[pl.ds(start, TOK), :] = values * gain
-        squares[pl.ds(start, TOK), :] = jnp.broadcast_to(
-            jnp.sum(values * values, axis=1, keepdims=True), (TOK, 128)
-        )
-    xg_ref[...] = rows[...].astype(BF16)
-    sq_ref[...] = squares[...].T[:8, :]
-
-
-def prepare(assignment, x, gain):
+        out_ref[assign_ref[c]] = x_ref[c]
+
+
+def sort_captions(assignment, x):
     vmem = pl.BlockSpec(memory_space=pltpu.VMEM)
     return pl.pallas_call(
-        prepare_kernel,
-        in_specs=[pl.BlockSpec(memory_space=pltpu.SMEM), vmem, vmem],
-        out_specs=[vmem, vmem],
-        out_shape=[jax.ShapeDtypeStruct((CT, FEAT), BF16), jax.ShapeDtypeStruct((8, CT), F32)],
-        scratch_shapes=[pltpu.VMEM((CT, FEAT), F32), pltpu.VMEM((CT, 128), F32)],
-        compiler_params=params(8),
-        name="prepare",
-    )(assignment, x, gain)
-
-
-def send_kernel(core_ref, xg_ref, sq_ref, w_ref, out_ref):
+        sort_kernel,
+        in_specs=[pl.BlockSpec(memory_space=pltpu.SMEM), vmem],
+        out_specs=vmem,
+        out_shape=jax.ShapeDtypeStruct(x.shape, x.dtype),
+        compiler_params=params(SORT_MIB),
+        name="sort_captions",
+    )(assignment, x)
+
+
+def fetch_kernel(*refs):
+    sources, targets, sems = refs[:2], refs[2:4], refs[4]
+    moves = [
+        pltpu.make_async_copy(source, target, sems.at[i])
+        for i, (source, target) in enumerate(zip(sources, targets))
+    ]
+    for move in moves:
+        move.start()
+    for move in moves:
+        move.wait()
+
+
+def fetch(*arrays):
+    return pl.pallas_call(
+        fetch_kernel,
+        in_specs=[pl.BlockSpec(memory_space=pl.ANY)] * 2,
+        out_specs=[pl.BlockSpec(memory_space=pltpu.VMEM)] * 2,
+        out_shape=[jax.ShapeDtypeStruct(a.shape, a.dtype) for a in arrays],
+        scratch_shapes=[pltpu.SemaphoreType.DMA((2,))],
+        compiler_params=params(FETCH_MIB),
+        name="fetch",
+    )(*arrays)
+
+
+def send_kernel(core_ref, x_ref, gain_ref, w_ref, out_ref, xg_ref, sq_ref):
+    @pl.when(pl.program_id(0) == 0)
+    def _():
+        values = x_ref[...].astype(F32)
+        xg_ref[...] = (values * gain_ref[...]).astype(BF16)
+        squares = jnp.sum(values * values, axis=1, keepdims=True)
+        sq_ref[...] = jnp.broadcast_to(squares, (CT, 128)).T[:8, :]
+
     out_ref[0, :CT, :] = dot(xg_ref[...], w_ref[...]).astype(BF16)
     out_ref[0, CT:, :] = square_rows(sq_ref[:1, :])
 
 
-def send_part(core, xg, sq, w):
+def send_part(core, x, gain, w):
+    whole = lambda i, _: (0, 0)
     return pl.pallas_call(
         send_kernel,
         grid_spec=pltpu.PrefetchScalarGridSpec(
             num_scalar_prefetch=1,
             grid=(NZH,),
             in_specs=[
-                pl.BlockSpec((CT, FEAT), lambda i, _: (0, 0)),
-                pl.BlockSpec((8, CT), lambda i, _: (0, 0)),
+                pl.BlockSpec((CT, FEAT), whole),
+                pl.BlockSpec((1, FEAT), whole),
                 pl.BlockSpec((FEAT, HALF), lambda i, c: (0, i * NC + 1 - c[0])),
             ],
-            out_specs=pl.BlockSpec((1, ROWS, HALF), lambda i, _: (i, 0, 0)),
+            out_specs=[
+                pl.BlockSpec((1, ROWS, HALF), lambda i, _: (i, 0, 0)),
+                pl.BlockSpec((CT, FEAT), whole),
+                pl.BlockSpec((8, CT), whole),
+            ],
         ),
-        out_shape=jax.ShapeDtypeStruct((NZH, ROWS, HALF), BF16),
+        out_shape=[
+            jax.ShapeDtypeStruct((NZH, ROWS, HALF), BF16),
+            jax.ShapeDtypeStruct((CT, FEAT), BF16),
+            jax.ShapeDtypeStruct((8, CT), F32),
+        ],
         compiler_params=params(16),
         name="text_other_half",
-    )(core, xg, sq, w)
+    )(core, x, gain, w)
 
 
 def keep_kernel(core_ref, xg_ref, sq_ref, w_ref, got_ref, out_ref):
@@ -406,28 +439,29 @@
     key_pair = [key_w, lax.ppermute(key_w, "zl", swap)]
     value_pair = [value_w, lax.ppermute(value_w, "zl", swap)]
 
-    xg, sq = prepare(assignment, enc_resid, enc_gain.reshape(1, FEAT))
-    send = send_part(core, xg, sq, text_in_w)
-    summed = keep_part(core, xg, sq, text_in_w, lax.ppermute(send, "c", swap))
-
-    summed, key_pair, value_pair, query = tie((summed, key_pair, value_pair, img_query))
+    mine = sort_captions(assignment, enc_resid)
+    mine = lax.all_to_all(mine, ("y", "zl", "x"), 0, 0, tiled=True)
+    text_w, gain = fetch(text_in_w, enc_gain.reshape(1, FEAT))
+    mine, text_w, gain, key_pair, value_pair = tie((mine, text_w, gain, key_pair, value_pair))
+    send, xg, sq = send_part(core, mine.reshape(CT, FEAT), gain, text_w)
+    summed = keep_part(core, xg, sq, text_w, lax.ppermute(send, "c", swap))
+
+    summed, key_pair, value_pair = tie((summed, key_pair, value_pair))
     got = lax.all_to_all(summed, "zh", 0, 0, tiled=True)
-    key_x = around(key_pair, "x")
-    value_y = around(value_pair, "y")
-    part = image((0,), query)
-    got, key_x, value_y, length, place, part = tie((got, key_x, value_y, length, place, part))
-
-    text = finish_text(got).reshape(SAMPLES, TOK, HALF)
-    text, key_x, value_y, part, query = tie(
-        (text, jnp.stack(key_x), jnp.stack(value_y), part, img_query)
-    )
-    text = lax.all_to_all(text, ("y", "zl", "x"), 0, 0, tiled=True)
+    key_x = jnp.stack(around(key_pair, "x"))
+    value_y = jnp.stack(around(value_pair, "y"))
     key_1, key_3 = beside(key_x, "y")
     value_1, value_3 = beside(value_y, "x")
-    text, key_1, key_3, value_1, value_3 = tie((text, key_1, key_3, value_1, value_3))
+    got, length, place = tie((got, length, place))
+
+    text = finish_text(got)
     spread = jnp.broadcast_to(text.reshape(1, CT, HALF), (NZH, CT, HALF))
-    spread, query, part = tie((spread, query, part))
+    spread, query = tie((spread, img_query))
     own = lax.all_to_all(spread, "zh", 0, 0, tiled=True)
+    part = image((0,), query)
+    part, query, key_1, key_3, value_1, value_3 = tie(
+        (part, query, key_1, key_3, value_1, value_3)
+    )
     key_2 = lax.ppermute(key_1, "y", ring(1))
     value_2 = lax.ppermute(value_3, "x", ring(3))
     part = image((1, 2), query, part)

time: 154 us -> 151 us (0.981)
  blocking collectives: 35.5 us -> 19.6 us
  waiting for transfers between devices: 26.9 us -> 34.1 us
  starting transfers between devices: 43.2 us -> 48.7 us
    all_to_all x1 -> x0, blocking collectives: 16.2 us -> none  [body(): text = lax.all_to_all(text, ('y', 'zl', 'x'), 0, 0, tiled=True)]
    all_to_all x0 -> x1, starting transfers between devices: none -> 8.67 us  [body(): mine = lax.all_to_all(mine, ('y', 'zl', 'x'), 0, 0, tiled=True)]
    all_to_all x1, waiting for transfers between devices: 3.66 us -> 0.01 us  [body(): own = lax.all_to_all(spread, 'zh', 0, 0, tiled=True)]
    ppermute x6, waiting for transfers between devices: 0.02 us -> 3.59 us  [around(): two, one, three = [lax.ppermute(block, axis, ring(k)) for k in (2, 1, 3)]]
    ppermute x6, starting transfers between devices: 11.6 us -> 8.25 us  [around(): two, one, three = [lax.ppermute(block, axis, ring(k)) for k in (2, 1, 3)]]
    ppermute x1, waiting for transfers between devices: 0.19 us -> 2.34 us  [body(): summed = keep_part(core, xg, sq, text_w, lax.ppermute(send, 'c', swap))]
    ppermute x1, waiting for transfers between devices: 0.17 us -> 2.26 us  [body(): key_pair = [key_w, lax.ppermute(key_w, 'zl', swap)]]
    ppermute x1, waiting for transfers between devices: 0.01 us -> 2.07 us  [body(): key_2 = lax.ppermute(key_1, 'y', ring(1))]
  transfers between devices with their start and end apart: 21 -> 22, of which waited for: 8 -> 13; matrix products, arithmetic and copies ran while one was open for 1% -> 2% of each run, Pallas kernels for 21% -> 20%
where the time goes in v3:
time: 151 us; the launch traced here: 150 us
  starting transfers between devices  48.7 us (32%)
  Pallas kernels  36.8 us (24%)
  waiting for transfers between devices  34.1 us (23%)
  blocking collectives  19.6 us (13%)
  local copies, waits for them, and re-layouts  7.22 us (5%)
  other arithmetic  2.47 us (2%)
    all_to_all x1, blocking collectives, body(): grad = lax.all_to_all(grad, ('zl', 'x'), 0, 0, tiled=True)  19.6 us
    pallas_call x2, Pallas kernels, image_attention(): pl.pallas_call(functools.partial(image_kernel, block=512, rows=256), grid...  17.8 us
    all_to_all x1, waiting for transfers between devices, body(): cot = lax.all_to_all(cot, 'y', 0, 0, tiled=True)  17.2 us
    pallas_call x1, Pallas kernels, text_side(): pl.pallas_call(text_side_kernel, in_specs=[smem, smem, pl.BlockSpec(memor...  11.8 us
    all_to_all x1, starting transfers between devices, body(): mine = lax.all_to_all(mine, ('y', 'zl', 'x'), 0, 0, tiled=True)  8.67 us
    ppermute x6, starting transfers between devices, around(): two, one, three = [lax.ppermute(block, axis, ring(k)) for k in (2, 1, 3)]  8.25 us
    all_to_all x1, starting transfers between devices, body(): got = lax.all_to_all(summed, 'zh', 0, 0, tiled=True)  7.35 us
    ppermute x4, starting transfers between devices, beside(): return [lax.ppermute(block, axis, ring(k)) for k in (1, 3)]  6.62 us
  transfers between devices with their start and end apart: 22, of which 13 were waited for; matrix products, arithmetic and copies ran while one was open for 2% of the time, Pallas kernels for 20%

profile of v3, /device:TPU:64, one launch (start us, length us, event | category | flops | bytes accessed | tf_op | source)
XLA Modules:
  0.0 149.8 jit_solution(18335846229050953079)
XLA Ops:
  0.6 1.7 %sort_captions.1 = bf16[32,8,512]{2,1,0:T(8,128)(2,1)} custom-call(s32[32]{0:T(128)} %assign_ref.1, bf16[32,8,512]{2,1,0:T(8,128)(2,1)} %x_ref.1), custom_call_target="tpu_custom_call" | custom-call | tf_op jit(solution)/shard_map/sort_captions/pallas_call | solution.py:68
  2.3 8.7 %all-to-all-start = ((bf16[32,8,512]{2,1,0:T(8,128)(2,1)}), bf16[32,8,512]{2,1,0:T(8,128)(2,1)S(1)}, u32[]{:S(2)}, u32[]{:S(2)}) async-start(bf16[32,8,512]{2,1,0:T(8,128)(2,1)} %sort_captions.1), calls=%async_computation | async-start | bytes 524288 | tf_op jit(solution)/shard_map/all_to_all | solution.py:443
  11.0 1.9 %collective-permute-start = (bf16[96,384]{1,0:T(8,128)(2,1)}, bf16[96,384]{1,0:T(8,128)(2,1)S(1)}, u32[]{:S(2)}, u32[]{:S(2)}) collective-permute-start(bf16[96,384]{1,0:T(8,128)(2,1)} %param.15), channel_id=1, source_target_pairs={{0,32},{32,0},{1,33},{33,1},{2,34},{34,2},{3,35},{35,3},{4,36},{36... | collective-permute-start | bytes 221192 | tf_op jit(solution)/shard_map/ppermute | solution.py:439
  12.9 0.2 collective-permute-start.1
  13.1 1.9 %copy-done.1 = bf16[512,3072]{1,0:T(8,128)(2,1)S(1)} copy-done((bf16[512,3072]{1,0:T(8,128)(2,1)S(1)}, bf16[512,3072]{1,0:T(8,128)(2,1)}, u32[]{:S(2)}) %copy-start.1) | copy-done | bytes 3145752
  15.0 0.7 copy-done.4
  15.9 2.3 %collective-permute-done = bf16[96,384]{1,0:T(8,128)(2,1)S(1)} collective-permute-done((bf16[96,384]{1,0:T(8,128)(2,1)}, bf16[96,384]{1,0:T(8,128)(2,1)S(1)}, u32[]{:S(2)}, u32[]{:S(2)}) %collective-permute-start) | collective-permute-done | bytes 73760 | tf_op jit(solution)/shard_map/ppermute | solution.py:439
  18.2 0.9 collective-permute-done.1
  19.1 2.0 %all-to-all-done = bf16[32,8,512]{2,1,0:T(8,128)(2,1)S(1)} async-done(((bf16[32,8,512]{2,1,0:T(8,128)(2,1)}), bf16[32,8,512]{2,1,0:T(8,128)(2,1)S(1)}, u32[]{:S(2)}, u32[]{:S(2)}) %all-to-all-start) | async-done | bytes 262176 | tf_op jit(solution)/shard_map/all_to_all | solution.py:443
  21.1 1.6 %text_other_half.1 = (bf16[4,272,384]{2,1,0:T(8,128)(2,1)S(1)}, bf16[256,512]{1,0:T(8,128)(2,1)S(1)}, f32[8,256]{1,0:T(8,128)S(1)}) custom-call(s32[1]{0:T(128)} %bitcast.core_ref, bf16[256,512]{1,0:T(8,128)(2,1)S(1)} %bitcast.29, f32[1,512]{1,0:T(1,128)S(1)} %get-tuple-element.50.gain_ref, bf16[512,3072]{1,0:T(8,128)(2,1)S(1)} %get-tuple-element.51.w_ref), custom_call_target="tpu_custom_call" | custom-call | tf_op jit(solution)/shard_map/text_other_half/pallas_call | solution.py:116
  22.8 2.3 %collective-permute-done.2.got_ref = bf16[4,272,384]{2,1,0:T(8,128)(2,1)S(1)} collective-permute-done((bf16[4,272,384]{2,1,0:T(8,128)(2,1)S(1)}, bf16[4,272,384]{2,1,0:T(8,128)(2,1)S(1)}, u32[]{:S(2)}, u32[]{:S(2)}) %collective-permute-start.2) | collective-permute-done | bytes 835616 | tf_op jit(solution)/shard_map/ppermute | solution.py:447
  25.1 1.4 text_own_half.1
  26.6 0.9 copy-done
  27.5 7.3 %all-to-all-start.1 = ((bf16[4,272,384]{2,1,0:T(8,128)(2,1)}), bf16[4,272,384]{2,1,0:T(8,128)(2,1)S(1)}, u32[]{:S(2)}, u32[]{:S(2)}) async-start(bf16[4,272,384]{2,1,0:T(8,128)(2,1)} %copy-done), calls=%async_computation.1 | async-start | bytes 1671168 | tf_op jit(solution)/shard_map/all_to_all | solution.py:450
  34.8 0.9 fusion.1
  35.7 0.7 collective-permute-start.8
  36.4 0.6 fusion
  37.1 2.0 %collective-permute-start.9 = (bf16[2,96,384]{2,1,0:T(8,128)(2,1)S(1)}, bf16[2,96,384]{2,1,0:T(8,128)(2,1)S(1)}, u32[]{:S(2)}, u32[]{:S(2)}) collective-permute-start(bf16[2,96,384]{2,1,0:T(8,128)(2,1)S(1)} %get-tuple-element.94), channel_id=1, source_target_pairs={{0,128},{64,192},{128,0},{192,64},{1,129},{65,193},{129,1},{193,65... | collective-permute-start | bytes 442376 | tf_op jit(solution)/shard_map/ppermute | solution.py:433
  39.0 1.6 %collective-permute-start.10 = (bf16[2,96,384]{2,1,0:T(8,128)(2,1)S(1)}, bf16[2,96,384]{2,1,0:T(8,128)(2,1)S(1)}, u32[]{:S(2)}, u32[]{:S(2)}) collective-permute-start(bf16[2,96,384]{2,1,0:T(8,128)(2,1)S(1)} %get-tuple-element.94), channel_id=1, source_target_pairs={{0,192},{64,0},{128,64},{192,128},{1,193},{65,1},{129,65},{193,129... | collective-permute-start | bytes 442376 | tf_op jit(solution)/shard_map/ppermute | solution.py:433
  40.7 1.0 collective-permute-start.3
  41.7 2.7 %collective-permute-start.4 = (bf16[2,96,384]{2,1,0:T(8,128)(2,1)S(1)}, bf16[2,96,384]{2,1,0:T(8,128)(2,1)S(1)}, u32[]{:S(2)}, u32[]{:S(2)}) collective-permute-start(bf16[2,96,384]{2,1,0:T(8,128)(2,1)S(1)} %get-tuple-element.96), channel_id=1, source_target_pairs={{0,16},{8,24},{16,0},{24,8},{1,17},{9,25},{17,1},{25,9},{2,18},{10... | collective-permute-start | bytes 442376 | tf_op jit(solution)/shard_map/ppermute | solution.py:433
  44.3 1.2 collective-permute-done.8
  45.5 0.3 collective-permute-start.5
  45.8 0.6 pad_add_fusion.place_ref
  46.4 0.3 collective-permute-done.10
  46.8 1.5 collective-permute-start.11
  48.3 1.9 %collective-permute-start.12 = (bf16[4,2,96,384]{3,2,1,0:T(8,128)(2,1)S(1)}, bf16[4,2,96,384]{3,2,1,0:T(8,128)(2,1)S(1)}, u32[]{:S(2)}, u32[]{:S(2)}) collective-permute-start(bf16[4,2,96,384]{3,2,1,0:T(8,128)(2,1)S(1)} %pad_maximum_fusion.1.refs_10_), channel_id=1, source_target_pairs={{0,24},{8,0},{16,8},{24,16},{1,25},{9,1},{17,9},{25,17},{2,26},{10... | collective-permute-start | bytes 1769480 | tf_op jit(solution)/shard_map/ppermute | solution.py:437
  50.1 1.3 collective-permute-done.4
  51.5 0.8 collective-permute-done.5
  52.4 3.2 %collective-permute-start.7 = (bf16[4,2,96,384]{3,2,1,0:T(8,128)(2,1)S(1)}, bf16[4,2,96,384]{3,2,1,0:T(8,128)(2,1)}, u32[]{:S(2)}, u32[]{:S(2)}) collective-permute-start(bf16[4,2,96,384]{3,2,1,0:T(8,128)(2,1)S(1)} %pad_maximum_fusion.refs_6_), channel_id=1, source_target_pairs={{0,192},{64,0},{128,64},{192,128},{1,193},{65,1},{129,65},{193,129... | collective-permute-start | bytes 1769480 | tf_op jit(solution)/shard_map/ppermute | solution.py:437
  55.6 1.3 all-to-all-done.1.got_ref
  57.2 0.9 broadcast_in_dim.10
  58.1 5.9 %all-to-all-start.2 = ((bf16[4,256,384]{2,1,0:T(8,128)(2,1)}), bf16[4,256,384]{2,1,0:T(8,128)(2,1)}, u32[]{:S(2)}, u32[]{:S(2)}) async-start(bf16[4,256,384]{2,1,0:T(8,128)(2,1)} %broadcast_in_dim.10), calls=%async_computation.2 | async-start | bytes 1572864 | tf_op jit(solution)/shard_map/all_to_all | solution.py:460
  64.0 6.7 %image_attention.2 = (f32[768,384]{1,0:T(8,128)}, f32[768,384]{1,0:T(8,128)}) custom-call(bf16[768,384]{1,0:T(8,128)(2,1)} %refs_2_.1, bf16[4096,384]{1,0:T(8,128)(2,1)} %k_ref.3, bf16[4096,384]{1,0:T(8,128)(2,1)} %v_ref.3), custom_call_target="tpu_custom_call" | custom-call | flops 1 | bytes 1 | tf_op jit(solution)/shard_map/image_attention/pallas_call | solution.py:212
  70.9 1.4 collective-permute-start.14
  72.3 11.1 %image_attention.3 = (f32[768,384]{1,0:T(8,128)}, f32[768,384]{1,0:T(8,128)}) custom-call(bf16[768,384]{1,0:T(8,128)(2,1)} %refs_2_.1, bf16[4096,384]{1,0:T(8,128)(2,1)} %k_ref.3, bf16[4096,384]{1,0:T(8,128)(2,1)} %v_ref.3, f32[768,384]{1,0:T(8,128)} %get-tuple-element.72.refs_0_, ...), custom_call_target="tpu_custom_call", output_to_operand_aliasing={{0}: (3, {}), {1}: (4, {})} | custom-call | flops 1 | bytes 1 | tf_op jit(solution)/shard_map/image_attention/pallas_call | solution.py:212
  83.4 2.1 %collective-permute-done.13.refs_8_ = bf16[4,2,96,384]{3,2,1,0:T(8,128)(2,1)S(1)} collective-permute-done((bf16[4,2,96,384]{3,2,1,0:T(8,128)(2,1)}, bf16[4,2,96,384]{3,2,1,0:T(8,128)(2,1)S(1)}, u32[]{:S(2)}, u32[]{:S(2)}) %collective-permute-start.13) | collective-permute-done | bytes 589856 | tf_op jit(solution)/shard_map/ppermute | solution.py:465
  85.6 3.7 %all-to-all-start.3 = ((bf16[4,256,384]{2,1,0:T(8,128)(2,1)}), bf16[4,256,384]{2,1,0:T(8,128)(2,1)S(1)}, u32[]{:S(2)}, u32[]{:S(2)}) async-start(bf16[4,256,384]{2,1,0:T(8,128)(2,1)} %all-to-all-done.2.refs_0_), calls=%async_computation.3 | async-start | bytes 1572864 | tf_op jit(solution)/shard_map/all_to_all | solution.py:470
  89.4 0.9 copy-done.7
  90.3 11.8 %text_side.1 = (f32[768,384]{1,0:T(8,128)}, bf16[4,256,768]{2,1,0:T(8,128)(2,1)}) custom-call(s32[1]{0:T(128)} %bitcast.3.length_ref, s32[4]{0:T(128)} %pad_add_fusion.place_ref, f32[1,128]{1,0:T(1,128)} %bitcast.40, bf16[4,256,384]{2,1,0:T(8,128)(2,1)} %all-to-all-done.2.refs_0_, bf16[4,256,384]{2,1,0:T(8,128)(2,1)} %copy-done.7, bf16[768,384]{1,0:T(8,128)(2,1)} %refs_2_.1, ...), custom_call_target="tpu_custom_call" | custom-call | tf_op jit(solution)/shard_map/text_side/pallas_call | solution.py:339
  102.3 4.4 %all-to-all-start.4 = ((bf16[4,256,768]{2,1,0:T(8,128)(2,1)}), bf16[4,256,768]{2,1,0:T(8,128)(2,1)S(1)}, u32[]{:S(2)}, u32[]{:S(2)}) async-start(bf16[4,256,768]{2,1,0:T(8,128)(2,1)} %get-tuple-element.87), calls=%async_computation.4 | async-start | bytes 3145728 | tf_op jit(solution)/shard_map/all_to_all | solution.py:486
  106.7 2.3 %collective-permute-done.16.other_ref = bf16[1024,384]{1,0:T(8,128)(2,1)S(1)} collective-permute-done((bf16[1024,384]{1,0:T(8,128)(2,1)S(1)}, bf16[1024,384]{1,0:T(8,128)(2,1)S(1)}, u32[]{:S(2)}, u32[]{:S(2)}) %collective-permute-start.16) | collective-permute-done | bytes 786464 | tf_op jit(solution)/shard_map/ppermute | solution.py:485
  108.9 1.1 copy-done.3
  110.1 0.5 turn_text.1.text_ref
  110.6 17.2 %all-to-all-done.4 = bf16[4,256,768]{2,1,0:T(8,128)(2,1)S(1)} async-done(((bf16[4,256,768]{2,1,0:T(8,128)(2,1)}), bf16[4,256,768]{2,1,0:T(8,128)(2,1)S(1)}, u32[]{:S(2)}, u32[]{:S(2)}) %all-to-all-start.4) | async-done | bytes 1572896 | tf_op jit(solution)/shard_map/all_to_all | solution.py:486
  127.7 1.6 %gradient.1 = bf16[768,768]{1,0:T(8,128)(2,1)S(1)} custom-call(bf16[768,1024]{1,0:T(8,128)(2,1)S(1)} %turn_text.1.text_ref, bf16[1024,768]{1,0:T(8,128)(2,1)S(1)} %bitcast.25), custom_call_target="tpu_custom_call" | custom-call | tf_op jit(solution)/shard_map/gradient/pallas_call | solution.py:388
  129.3 19.6 %all_to_all.30 = bf16[8,96,768]{2,1,0:T(8,128)(2,1)S(1)} all-to-all(bf16[8,96,768]{2,1,0:T(8,128)(2,1)S(1)} %bitcast.26), channel_id=1, replica_groups=mesh['y'=4,'zl'=2,'x'=4,'zh'=4,'c'=2] {'zl','x'}, dimensions={0} | all-to-all | bytes 2359296 | tf_op jit(solution)/shard_map/all_to_all | solution.py:491
  149.1 0.7 fusion.3
  (48 shorter events, 1.4 us)
Async XLA Ops:
  2.3 18.7 %all-to-all-start = ((bf16[32,8,512]{2,1,0:T(8,128)(2,1)}), bf16[32,8,512]{2,1,0:T(8,128)(2,1)S(1)}, u32[]{:S(2)}, u32[]{:S(2)}) async-start(bf16[32,8,512]{2,1,0:T(8,128)(2,1)} %sort_captions.1), calls=%async_computation | async-start | bytes 524288 | tf_op jit(solution)/shard_map/all_to_all | solution.py:443
  11.0 7.2 %collective-permute-start = (bf16[96,384]{1,0:T(8,128)(2,1)}, bf16[96,384]{1,0:T(8,128)(2,1)S(1)}, u32[]{:S(2)}, u32[]{:S(2)}) collective-permute-start(bf16[96,384]{1,0:T(8,128)(2,1)} %param.15), channel_id=1, source_target_pairs={{0,32},{32,0},{1,33},{33,1},{2,34},{34,2},{3,35},{35,3},{4,36},{36... | collective-permute-start | bytes 221192 | tf_op jit(solution)/shard_map/ppermute | solution.py:439
  12.9 6.2 %collective-permute-start.1 = (bf16[96,384]{1,0:T(8,128)(2,1)}, bf16[96,384]{1,0:T(8,128)(2,1)}, u32[]{:S(2)}, u32[]{:S(2)}) collective-permute-start(bf16[96,384]{1,0:T(8,128)(2,1)} %param.16), channel_id=1, source_target_pairs={{0,32},{32,0},{1,33},{33,1},{2,34},{34,2},{3,35},{35,3},{4,36},{36... | collective-permute-start | bytes 221192 | tf_op jit(solution)/shard_map/ppermute | solution.py:440
  13.1 1.9 %copy-start.1 = (bf16[512,3072]{1,0:T(8,128)(2,1)S(1)}, bf16[512,3072]{1,0:T(8,128)(2,1)}, u32[]{:S(2)}) copy-start(bf16[512,3072]{1,0:T(8,128)(2,1)} %refs_0_.1) | copy-start | bytes 9437188
  15.0 0.7 copy-start.4
  22.7 2.4 %collective-permute-start.2 = (bf16[4,272,384]{2,1,0:T(8,128)(2,1)S(1)}, bf16[4,272,384]{2,1,0:T(8,128)(2,1)S(1)}, u32[]{:S(2)}, u32[]{:S(2)}) collective-permute-start(bf16[4,272,384]{2,1,0:T(8,128)(2,1)S(1)} %get-tuple-element.54), channel_id=1, source_target_pairs={{0,1},{1,0},{2,3},{3,2},{4,5},{5,4},{6,7},{7,6},{8,9},{9,8},{10,11... | collective-permute-start | bytes 2506760 | tf_op jit(solution)/shard_map/ppermute | solution.py:447
  26.5 0.9 copy-start
  27.4 7.4 %copy-start.12 = (bf16[96,384]{1,0:T(8,128)(2,1)S(1)}, bf16[96,384]{1,0:T(8,128)(2,1)}, u32[]{:S(2)}) copy-start(bf16[96,384]{1,0:T(8,128)(2,1)} %param.16) | copy-start | bytes 221188
  27.4 9.0 %copy-start.14 = (s32[32]{0:T(128)S(1)}, s32[32]{0:T(128)}, u32[]{:S(2)}) copy-start(s32[32]{0:T(128)} %assign_ref.1) | copy-start | bytes 388
  27.4 9.0 %copy-start.15 = (s32[32]{0:T(128)S(1)}, s32[32]{0:T(128)}, u32[]{:S(2)}) copy-start(s32[32]{0:T(128)} %param.22) | copy-start | bytes 388
  27.4 13.2 %copy-start.13 = (bf16[96,384]{1,0:T(8,128)(2,1)S(1)}, bf16[96,384]{1,0:T(8,128)(2,1)}, u32[]{:S(2)}) copy-start(bf16[96,384]{1,0:T(8,128)(2,1)} %param.15) | copy-start | bytes 221188
  27.5 29.5 %all-to-all-start.1 = ((bf16[4,272,384]{2,1,0:T(8,128)(2,1)}), bf16[4,272,384]{2,1,0:T(8,128)(2,1)S(1)}, u32[]{:S(2)}, u32[]{:S(2)}) async-start(bf16[4,272,384]{2,1,0:T(8,128)(2,1)} %copy-done), calls=%async_computation.1 | async-start | bytes 1671168 | tf_op jit(solution)/shard_map/all_to_all | solution.py:450
  35.7 9.8 %collective-permute-start.8 = (bf16[2,96,384]{2,1,0:T(8,128)(2,1)S(1)}, bf16[2,96,384]{2,1,0:T(8,128)(2,1)S(1)}, u32[]{:S(2)}, u32[]{:S(2)}) collective-permute-start(bf16[2,96,384]{2,1,0:T(8,128)(2,1)S(1)} %get-tuple-element.94), channel_id=1, source_target_pairs={{0,64},{64,128},{128,192},{192,0},{1,65},{65,129},{129,193},{193,1... | collective-permute-start | bytes 442376 | tf_op jit(solution)/shard_map/ppermute | solution.py:433
  37.1 9.3 %collective-permute-start.9 = (bf16[2,96,384]{2,1,0:T(8,128)(2,1)S(1)}, bf16[2,96,384]{2,1,0:T(8,128)(2,1)S(1)}, u32[]{:S(2)}, u32[]{:S(2)}) collective-permute-start(bf16[2,96,384]{2,1,0:T(8,128)(2,1)S(1)} %get-tuple-element.94), channel_id=1, source_target_pairs={{0,128},{64,192},{128,0},{192,64},{1,129},{65,193},{129,1},{193,65... | collective-permute-start | bytes 442376 | tf_op jit(solution)/shard_map/ppermute | solution.py:433
  39.0 7.7 %collective-permute-start.10 = (bf16[2,96,384]{2,1,0:T(8,128)(2,1)S(1)}, bf16[2,96,384]{2,1,0:T(8,128)(2,1)S(1)}, u32[]{:S(2)}, u32[]{:S(2)}) collective-permute-start(bf16[2,96,384]{2,1,0:T(8,128)(2,1)S(1)} %get-tuple-element.94), channel_id=1, source_target_pairs={{0,192},{64,0},{128,64},{192,128},{1,193},{65,1},{129,65},{193,129... | collective-permute-start | bytes 442376 | tf_op jit(solution)/shard_map/ppermute | solution.py:433
  40.7 9.5 %collective-permute-start.3 = (bf16[2,96,384]{2,1,0:T(8,128)(2,1)S(1)}, bf16[2,96,384]{2,1,0:T(8,128)(2,1)S(1)}, u32[]{:S(2)}, u32[]{:S(2)}) collective-permute-start(bf16[2,96,384]{2,1,0:T(8,128)(2,1)S(1)} %get-tuple-element.96), channel_id=1, source_target_pairs={{0,8},{8,16},{16,24},{24,0},{1,9},{9,17},{17,25},{25,1},{2,10},{10... | collective-permute-start | bytes 442376 | tf_op jit(solution)/shard_map/ppermute | solution.py:433
  41.7 9.8 %collective-permute-start.4 = (bf16[2,96,384]{2,1,0:T(8,128)(2,1)S(1)}, bf16[2,96,384]{2,1,0:T(8,128)(2,1)S(1)}, u32[]{:S(2)}, u32[]{:S(2)}) collective-permute-start(bf16[2,96,384]{2,1,0:T(8,128)(2,1)S(1)} %get-tuple-element.96), channel_id=1, source_target_pairs={{0,16},{8,24},{16,0},{24,8},{1,17},{9,25},{17,1},{25,9},{2,18},{10... | collective-permute-start | bytes 442376 | tf_op jit(solution)/shard_map/ppermute | solution.py:433
  45.5 6.7 %collective-permute-start.5 = (bf16[2,96,384]{2,1,0:T(8,128)(2,1)S(1)}, bf16[2,96,384]{2,1,0:T(8,128)(2,1)S(1)}, u32[]{:S(2)}, u32[]{:S(2)}) collective-permute-start(bf16[2,96,384]{2,1,0:T(8,128)(2,1)S(1)} %get-tuple-element.96), channel_id=1, source_target_pairs={{0,24},{8,0},{16,8},{24,16},{1,25},{9,1},{17,9},{25,17},{2,26},{10... | collective-permute-start | bytes 442376 | tf_op jit(solution)/shard_map/ppermute | solution.py:433
  46.8 11.3 %copy-start.5 = (bf16[4,2,96,384]{3,2,1,0:T(8,128)(2,1)}, bf16[4,2,96,384]{3,2,1,0:T(8,128)(2,1)S(1)}, u32[]{:S(2)}) copy-start(bf16[4,2,96,384]{3,2,1,0:T(8,128)(2,1)S(1)} %pad_maximum_fusion.1.refs_10_) | copy-start | bytes 1769476
  46.8 23.9 %collective-permute-start.11 = (bf16[4,2,96,384]{3,2,1,0:T(8,128)(2,1)S(1)}, bf16[4,2,96,384]{3,2,1,0:T(8,128)(2,1)S(1)}, u32[]{:S(2)}, u32[]{:S(2)}) collective-permute-start(bf16[4,2,96,384]{3,2,1,0:T(8,128)(2,1)S(1)} %pad_maximum_fusion.1.refs_10_), channel_id=1, source_target_pairs={{0,8},{8,16},{16,24},{24,0},{1,9},{9,17},{17,25},{25,1},{2,10},{10... | collective-permute-start | bytes 1769480 | tf_op jit(solution)/shard_map/ppermute | solution.py:437
  48.3 22.5 %collective-permute-start.12 = (bf16[4,2,96,384]{3,2,1,0:T(8,128)(2,1)S(1)}, bf16[4,2,96,384]{3,2,1,0:T(8,128)(2,1)S(1)}, u32[]{:S(2)}, u32[]{:S(2)}) collective-permute-start(bf16[4,2,96,384]{3,2,1,0:T(8,128)(2,1)S(1)} %pad_maximum_fusion.1.refs_10_), channel_id=1, source_target_pairs={{0,24},{8,0},{16,8},{24,16},{1,25},{9,1},{17,9},{25,17},{2,26},{10... | collective-permute-start | bytes 1769480 | tf_op jit(solution)/shard_map/ppermute | solution.py:437
  52.3 5.8 %copy-start.6 = (bf16[4,2,96,384]{3,2,1,0:T(8,128)(2,1)}, bf16[4,2,96,384]{3,2,1,0:T(8,128)(2,1)S(1)}, u32[]{:S(2)}) copy-start(bf16[4,2,96,384]{3,2,1,0:T(8,128)(2,1)S(1)} %pad_maximum_fusion.refs_6_) | copy-start | bytes 1769476
  52.3 18.5 %collective-permute-start.6 = (bf16[4,2,96,384]{3,2,1,0:T(8,128)(2,1)S(1)}, bf16[4,2,96,384]{3,2,1,0:T(8,128)(2,1)}, u32[]{:S(2)}, u32[]{:S(2)}) collective-permute-start(bf16[4,2,96,384]{3,2,1,0:T(8,128)(2,1)S(1)} %pad_maximum_fusion.refs_6_), channel_id=1, source_target_pairs={{0,64},{64,128},{128,192},{192,0},{1,65},{65,129},{129,193},{193,1... | collective-permute-start | bytes 1769480 | tf_op jit(solution)/shard_map/ppermute | solution.py:437
  52.4 18.4 %collective-permute-start.7 = (bf16[4,2,96,384]{3,2,1,0:T(8,128)(2,1)S(1)}, bf16[4,2,96,384]{3,2,1,0:T(8,128)(2,1)}, u32[]{:S(2)}, u32[]{:S(2)}) collective-permute-start(bf16[4,2,96,384]{3,2,1,0:T(8,128)(2,1)S(1)} %pad_maximum_fusion.refs_6_), channel_id=1, source_target_pairs={{0,192},{64,0},{128,64},{192,128},{1,193},{65,1},{129,65},{193,129... | collective-permute-start | bytes 1769480 | tf_op jit(solution)/shard_map/ppermute | solution.py:437
  58.1 27.4 %all-to-all-start.2 = ((bf16[4,256,384]{2,1,0:T(8,128)(2,1)}), bf16[4,256,384]{2,1,0:T(8,128)(2,1)}, u32[]{:S(2)}, u32[]{:S(2)}) async-start(bf16[4,256,384]{2,1,0:T(8,128)(2,1)} %broadcast_in_dim.10), calls=%async_computation.2 | async-start | bytes 1572864 | tf_op jit(solution)/shard_map/all_to_all | solution.py:460
  70.8 12.6 %copy-start.8 = (bf16[4,2,96,384]{3,2,1,0:T(8,128)(2,1)}, bf16[4,2,96,384]{3,2,1,0:T(8,128)(2,1)S(1)}, u32[]{:S(2)}) copy-start(bf16[4,2,96,384]{3,2,1,0:T(8,128)(2,1)S(1)} %collective-permute-done.11.refs_11_) | copy-start | bytes 1769476
  70.8 12.6 %copy-start.9 = (bf16[4,2,96,384]{3,2,1,0:T(8,128)(2,1)}, bf16[4,2,96,384]{3,2,1,0:T(8,128)(2,1)S(1)}, u32[]{:S(2)}) copy-start(bf16[4,2,96,384]{3,2,1,0:T(8,128)(2,1)S(1)} %collective-permute-done.12.refs_13_) | copy-start | bytes 1769476
  70.8 14.7 %collective-permute-start.13 = (bf16[4,2,96,384]{3,2,1,0:T(8,128)(2,1)}, bf16[4,2,96,384]{3,2,1,0:T(8,128)(2,1)S(1)}, u32[]{:S(2)}, u32[]{:S(2)}) collective-permute-start(bf16[4,2,96,384]{3,2,1,0:T(8,128)(2,1)} %collective-permute-done.6.refs_7_), channel_id=1, source_target_pairs={{0,64},{64,128},{128,192},{192,0},{1,65},{65,129},{129,193},{193,1... | collective-permute-start | bytes 1769480 | tf_op jit(solution)/shard_map/ppermute | solution.py:465
  70.9 14.6 %collective-permute-start.14 = (bf16[4,2,96,384]{3,2,1,0:T(8,128)(2,1)S(1)}, bf16[4,2,96,384]{3,2,1,0:T(8,128)(2,1)S(1)}, u32[]{:S(2)}, u32[]{:S(2)}) collective-permute-start(bf16[4,2,96,384]{3,2,1,0:T(8,128)(2,1)S(1)} %collective-permute-done.12.refs_13_), channel_id=1, source_target_pairs={{0,24},{8,0},{16,8},{24,16},{1,25},{9,1},{17,9},{25,17},{2,26},{10... | collective-permute-start | bytes 1769480 | tf_op jit(solution)/shard_map/ppermute | solution.py:466
  85.5 3.9 %copy-start.10 = (bf16[4,2,96,384]{3,2,1,0:T(8,128)(2,1)}, bf16[4,2,96,384]{3,2,1,0:T(8,128)(2,1)S(1)}, u32[]{:S(2)}) copy-start(bf16[4,2,96,384]{3,2,1,0:T(8,128)(2,1)S(1)} %collective-permute-done.13.refs_8_) | copy-start | bytes 1769476
  85.5 3.9 %copy-start.11 = (bf16[4,2,96,384]{3,2,1,0:T(8,128)(2,1)}, bf16[4,2,96,384]{3,2,1,0:T(8,128)(2,1)S(1)}, u32[]{:S(2)}) copy-start(bf16[4,2,96,384]{3,2,1,0:T(8,128)(2,1)S(1)} %collective-permute-done.14.refs_12_) | copy-start | bytes 1769476
  85.5 3.8 %collective-permute-start.15 = (bf16[4,256,384]{2,1,0:T(8,128)(2,1)}, bf16[4,256,384]{2,1,0:T(8,128)(2,1)S(1)}, u32[]{:S(2)}, u32[]{:S(2)}) collective-permute-start(bf16[4,256,384]{2,1,0:T(8,128)(2,1)} %all-to-all-done.2.refs_0_), channel_id=1, source_target_pairs={{0,1},{1,0},{2,3},{3,2},{4,5},{5,4},{6,7},{7,6},{8,9},{9,8},{10,11... | collective-permute-start | bytes 2359304 | tf_op jit(solution)/shard_map/ppermute | solution.py:469
  85.6 16.7 %all-to-all-start.3 = ((bf16[4,256,384]{2,1,0:T(8,128)(2,1)}), bf16[4,256,384]{2,1,0:T(8,128)(2,1)S(1)}, u32[]{:S(2)}, u32[]{:S(2)}) async-start(bf16[4,256,384]{2,1,0:T(8,128)(2,1)} %all-to-all-done.2.refs_0_), calls=%async_computation.3 | async-start | bytes 1572864 | tf_op jit(solution)/shard_map/all_to_all | solution.py:470
  89.3 0.9 copy-start.7
  102.3 4.4 %copy-start.2 = (bf16[4,256,384]{2,1,0:T(8,128)(2,1)}, bf16[4,256,384]{2,1,0:T(8,128)(2,1)S(1)}, u32[]{:S(2)}) copy-start(bf16[4,256,384]{2,1,0:T(8,128)(2,1)S(1)} %all-to-all-done.3) | copy-start | bytes 2359300
  102.3 25.5 %all-to-all-start.4 = ((bf16[4,256,768]{2,1,0:T(8,128)(2,1)}), bf16[4,256,768]{2,1,0:T(8,128)(2,1)S(1)}, u32[]{:S(2)}, u32[]{:S(2)}) async-start(bf16[4,256,768]{2,1,0:T(8,128)(2,1)} %get-tuple-element.87), calls=%async_computation.4 | async-start | bytes 3145728 | tf_op jit(solution)/shard_map/all_to_all | solution.py:486
  106.7 2.3 %collective-permute-start.16 = (bf16[1024,384]{1,0:T(8,128)(2,1)S(1)}, bf16[1024,384]{1,0:T(8,128)(2,1)S(1)}, u32[]{:S(2)}, u32[]{:S(2)}) collective-permute-start(bf16[1024,384]{1,0:T(8,128)(2,1)S(1)} %bitcast.27), channel_id=1, source_target_pairs={{0,1},{1,0},{2,3},{3,2},{4,5},{5,4},{6,7},{7,6},{8,9},{9,8},{10,11... | collective-permute-start | bytes 2359304 | tf_op jit(solution)/shard_map/ppermute | solution.py:485
  108.9 1.1 copy-start.3

commit v4 on v3

--- a/solution.py
+++ b/solution.py
@@ -228,30 +228,48 @@
     )(q, k, v, *before)
 
 
-def head_attention(length, key_pre, value_pre, q, g, gain, image_sum, stats):
+def heads_attention(length, key_pres, values, qs, gs, gain, image_sums, stats):
     factor = SCALE * LOG2E
+    every = range(HEADS)
     keep = lax.broadcasted_iota(jnp.int32, (CT, 1), 0) < length
-    turned = stats.T
-    m, l = turned[:1, :], turned[HD // 2 : HD // 2 + 1, :]
-    value = value_pre.astype(BF16)
-    root = lax.rsqrt(jnp.mean(key_pre * key_pre, axis=1, keepdims=True) + 1e-06)
-    key = (key_pre * root * gain).astype(BF16)
-    s = jnp.where(keep, dot(key, q, NT) * factor, -1e30)
-    top = jnp.maximum(m, jnp.max(s, axis=0, keepdims=True))
-    e = jnp.exp2(s - top)
-    fade = jnp.exp2(m - top)
-    inverse = 1.0 / (l * fade + jnp.sum(e, axis=0, keepdims=True))
-    p = e * inverse
-    probs = p.astype(BF16)
-    image_scale = jnp.broadcast_to(fade * inverse, (HD, IQ)).T
-    joint = image_sum * image_scale + dot(probs, value, TN)
-    mean = jnp.sum((g.astype(F32) * joint).T, axis=0, keepdims=True)
-    ds = (p * (dot(value, g, NT) - mean) * SCALE).astype(BF16)
-    d_value = dot(probs, g).astype(BF16)
-    d_key = dot(ds, q).astype(BF16).astype(F32) * gain
-    along = jnp.mean(d_key * key_pre, axis=1, keepdims=True)
-    d_pre = (root * d_key - key_pre * (root * root * root * along)).astype(BF16)
-    return joint, d_pre, d_value
+    roots = [
+        lax.rsqrt(jnp.mean(k * k, axis=1, keepdims=True) + 1e-06) for k in key_pres
+    ]
+    keys = [(key_pres[h] * roots[h] * gain).astype(BF16) for h in every]
+    scores = [jnp.where(keep, dot(keys[h], qs[h], NT) * factor, -1e30) for h in every]
+    turned = [a.T for a in stats]
+    tops = [
+        jnp.maximum(turned[h][:1, :], jnp.max(scores[h], axis=0, keepdims=True)) for h in every
+    ]
+    exps = [jnp.exp2(scores[h] - tops[h]) for h in every]
+    fades = [jnp.exp2(turned[h][:1, :] - tops[h]) for h in every]
+    inverses = [
+        1.0
+        / (
+            turned[h][HD // 2 : HD // 2 + 1, :] * fades[h]
+            + jnp.sum(exps[h], axis=0, keepdims=True)
+        )
+        for h in every
+    ]
+    ps = [exps[h] * inverses[h] for h in every]
+    probs = [p.astype(BF16) for p in ps]
+    scales = [jnp.broadcast_to(fades[h] * inverses[h], (HD, IQ)).T for h in every]
+    joints = [image_sums[h] * scales[h] + dot(probs[h], values[h], TN) for h in every]
+    means = [
+        jnp.sum((gs[h].astype(F32) * joints[h]).T, axis=0, keepdims=True) for h in every
+    ]
+    d_probs = [dot(values[h], gs[h], NT) for h in every]
+    ds = [(ps[h] * (d_probs[h] - means[h]) * SCALE).astype(BF16) for h in every]
+    d_values = [dot(probs[h], gs[h]).astype(BF16) for h in every]
+    d_keys = [dot(ds[h], qs[h]).astype(BF16).astype(F32) * gain for h in every]
+    d_pres = []
+    for h in every:
+        root, key_pre, d_key = roots[h], key_pres[h], d_keys[h]
+        along = jnp.mean(d_key * key_pre, axis=1, keepdims=True)
+        d_pres.append(
+            (root * d_key - key_pre * (root * root * root * along)).astype(BF16)
+        )
+    return joints, d_pres, d_values
 
 
 def text_side_kernel(length_ref, place_ref, gain_ref, *refs):
@@ -300,19 +318,20 @@
 
     for i in range(2, 6):
         fetch[i].wait()
+    columns = [slice(h * HD, (h + 1) * HD) for h in range(HEADS)]
+    joints, d_pres, d_values = heads_attention(
+        length_ref[0],
+        [kv[:, cols] for cols in columns],
+        [kv[:, COLS + h * HD : COLS + (h + 1) * HD].astype(BF16) for h in range(HEADS)],
+        [q[:, cols] for cols in columns],
+        [g[:, cols] for cols in columns],
+        gain_ref[...],
+        [image_sum[:, cols] for cols in columns],
+        [stats[:, cols] for cols in columns],
+    )
     leave = []
-    for h in range(HEADS):
-        cols = slice(h * HD, (h + 1) * HD)
-        joint, d_pre, d_value = head_attention(
-            length_ref[0],
-            kv[:, cols],
-            kv[:, COLS + h * HD : COLS + (h + 1) * HD],
-            q[:, cols],
-            g[:, cols],
-            gain_ref[...],
-            image_sum[:, cols],
-            stats[:, cols],
-        )
+    for h, cols in enumerate(columns):
+        joint, d_pre, d_value = joints[h], d_pres[h], d_values[h]
         for n, value in ((0, d_pre), (1, d_value)):
             span = slice(n * COLS + h * HD, n * COLS + (h + 1) * HD)
             cots[:, span] = value

time: 151 us -> 150 us (level)
  no operation moved by 1% of the time
where the time goes in v4:
time: 150 us; the launch traced here: 149 us
  starting transfers between devices  48.1 us (32%)
  Pallas kernels  36.3 us (24%)
  waiting for transfers between devices  34.7 us (23%)
  blocking collectives  19.6 us (13%)
  local copies, waits for them, and re-layouts  7.22 us (5%)
  other arithmetic  2.47 us (2%)
    all_to_all x1, blocking collectives, body(): grad = lax.all_to_all(grad, ('zl', 'x'), 0, 0, tiled=True)  19.6 us
    pallas_call x2, Pallas kernels, image_attention(): pl.pallas_call(functools.partial(image_kernel, block=512, rows=256), grid...  17.8 us
    all_to_all x1, waiting for transfers between devices, body(): cot = lax.all_to_all(cot, 'y', 0, 0, tiled=True)  17.2 us
    pallas_call x1, Pallas kernels, text_side(): pl.pallas_call(text_side_kernel, in_specs=[smem, smem, pl.BlockSpec(memor...  11.3 us
    all_to_all x1, starting transfers between devices, body(): mine = lax.all_to_all(mine, ('y', 'zl', 'x'), 0, 0, tiled=True)  8.67 us
    ppermute x6, starting transfers between devices, around(): two, one, three = [lax.ppermute(block, axis, ring(k)) for k in (2, 1, 3)]  8.25 us
    all_to_all x1, starting transfers between devices, body(): got = lax.all_to_all(summed, 'zh', 0, 0, tiled=True)  7.35 us
    ppermute x4, starting transfers between devices, beside(): return [lax.ppermute(block, axis, ring(k)) for k in (1, 3)]  6.62 us
  transfers between devices with their start and end apart: 22, of which 13 were waited for; matrix products, arithmetic and copies ran while one was open for 2% of the time, Pallas kernels for 20%

profile of v4, /device:TPU:64, one launch (start us, length us, event | category | flops | bytes accessed | tf_op | source)
XLA Modules:
  0.0 149.3 jit_solution(11904697638834726277)
XLA Ops:
  0.6 1.7 %sort_captions.1 = bf16[32,8,512]{2,1,0:T(8,128)(2,1)} custom-call(s32[32]{0:T(128)} %assign_ref.1, bf16[32,8,512]{2,1,0:T(8,128)(2,1)} %x_ref.1), custom_call_target="tpu_custom_call" | custom-call | tf_op jit(solution)/shard_map/sort_captions/pallas_call | solution.py:68
  2.3 8.7 %all-to-all-start = ((bf16[32,8,512]{2,1,0:T(8,128)(2,1)}), bf16[32,8,512]{2,1,0:T(8,128)(2,1)S(1)}, u32[]{:S(2)}, u32[]{:S(2)}) async-start(bf16[32,8,512]{2,1,0:T(8,128)(2,1)} %sort_captions.1), calls=%async_computation | async-start | bytes 524288 | tf_op jit(solution)/shard_map/all_to_all | solution.py:462
  11.0 1.9 %collective-permute-start = (bf16[96,384]{1,0:T(8,128)(2,1)}, bf16[96,384]{1,0:T(8,128)(2,1)S(1)}, u32[]{:S(2)}, u32[]{:S(2)}) collective-permute-start(bf16[96,384]{1,0:T(8,128)(2,1)} %param.15), channel_id=1, source_target_pairs={{0,32},{32,0},{1,33},{33,1},{2,34},{34,2},{3,35},{35,3},{4,36},{36... | collective-permute-start | bytes 221192 | tf_op jit(solution)/shard_map/ppermute | solution.py:458
  13.1 1.9 %copy-done.1 = bf16[512,3072]{1,0:T(8,128)(2,1)S(1)} copy-done((bf16[512,3072]{1,0:T(8,128)(2,1)S(1)}, bf16[512,3072]{1,0:T(8,128)(2,1)}, u32[]{:S(2)}) %copy-start.1) | copy-done | bytes 3145752
  15.0 0.7 copy-done.4
  15.9 2.3 %collective-permute-done = bf16[96,384]{1,0:T(8,128)(2,1)S(1)} collective-permute-done((bf16[96,384]{1,0:T(8,128)(2,1)}, bf16[96,384]{1,0:T(8,128)(2,1)S(1)}, u32[]{:S(2)}, u32[]{:S(2)}) %collective-permute-start) | collective-permute-done | bytes 73760 | tf_op jit(solution)/shard_map/ppermute | solution.py:458
  18.2 0.9 collective-permute-done.1
  19.1 2.0 %all-to-all-done = bf16[32,8,512]{2,1,0:T(8,128)(2,1)S(1)} async-done(((bf16[32,8,512]{2,1,0:T(8,128)(2,1)}), bf16[32,8,512]{2,1,0:T(8,128)(2,1)S(1)}, u32[]{:S(2)}, u32[]{:S(2)}) %all-to-all-start) | async-done | bytes 262176 | tf_op jit(solution)/shard_map/all_to_all | solution.py:462
  21.1 1.6 %text_other_half.1 = (bf16[4,272,384]{2,1,0:T(8,128)(2,1)S(1)}, bf16[256,512]{1,0:T(8,128)(2,1)S(1)}, f32[8,256]{1,0:T(8,128)S(1)}) custom-call(s32[1]{0:T(128)} %bitcast.core_ref, bf16[256,512]{1,0:T(8,128)(2,1)S(1)} %bitcast.29, f32[1,512]{1,0:T(1,128)S(1)} %get-tuple-element.50.gain_ref, bf16[512,3072]{1,0:T(8,128)(2,1)S(1)} %get-tuple-element.51.w_ref), custom_call_target="tpu_custom_call" | custom-call | tf_op jit(solution)/shard_map/text_other_half/pallas_call | solution.py:116
  22.8 2.3 %collective-permute-done.2.got_ref = bf16[4,272,384]{2,1,0:T(8,128)(2,1)S(1)} collective-permute-done((bf16[4,272,384]{2,1,0:T(8,128)(2,1)S(1)}, bf16[4,272,384]{2,1,0:T(8,128)(2,1)S(1)}, u32[]{:S(2)}, u32[]{:S(2)}) %collective-permute-start.2) | collective-permute-done | bytes 835616 | tf_op jit(solution)/shard_map/ppermute | solution.py:466
  25.1 1.4 text_own_half.1
  26.6 0.9 copy-done
  27.5 7.3 %all-to-all-start.1 = ((bf16[4,272,384]{2,1,0:T(8,128)(2,1)}), bf16[4,272,384]{2,1,0:T(8,128)(2,1)S(1)}, u32[]{:S(2)}, u32[]{:S(2)}) async-start(bf16[4,272,384]{2,1,0:T(8,128)(2,1)} %copy-done), calls=%async_computation.1 | async-start | bytes 1671168 | tf_op jit(solution)/shard_map/all_to_all | solution.py:469
  34.8 0.9 fusion.1
  35.7 0.7 collective-permute-start.8
  36.4 0.6 fusion
  37.1 2.0 %collective-permute-start.9 = (bf16[2,96,384]{2,1,0:T(8,128)(2,1)S(1)}, bf16[2,96,384]{2,1,0:T(8,128)(2,1)S(1)}, u32[]{:S(2)}, u32[]{:S(2)}) collective-permute-start(bf16[2,96,384]{2,1,0:T(8,128)(2,1)S(1)} %get-tuple-element.94), channel_id=1, source_target_pairs={{0,128},{64,192},{128,0},{192,64},{1,129},{65,193},{129,1},{193,65... | collective-permute-start | bytes 442376 | tf_op jit(solution)/shard_map/ppermute | solution.py:452
  39.0 1.6 %collective-permute-start.10 = (bf16[2,96,384]{2,1,0:T(8,128)(2,1)S(1)}, bf16[2,96,384]{2,1,0:T(8,128)(2,1)S(1)}, u32[]{:S(2)}, u32[]{:S(2)}) collective-permute-start(bf16[2,96,384]{2,1,0:T(8,128)(2,1)S(1)} %get-tuple-element.94), channel_id=1, source_target_pairs={{0,192},{64,0},{128,64},{192,128},{1,193},{65,1},{129,65},{193,129... | collective-permute-start | bytes 442376 | tf_op jit(solution)/shard_map/ppermute | solution.py:452
  40.7 1.0 collective-permute-start.3
  41.7 2.7 %collective-permute-start.4 = (bf16[2,96,384]{2,1,0:T(8,128)(2,1)S(1)}, bf16[2,96,384]{2,1,0:T(8,128)(2,1)S(1)}, u32[]{:S(2)}, u32[]{:S(2)}) collective-permute-start(bf16[2,96,384]{2,1,0:T(8,128)(2,1)S(1)} %get-tuple-element.96), channel_id=1, source_target_pairs={{0,16},{8,24},{16,0},{24,8},{1,17},{9,25},{17,1},{25,9},{2,18},{10... | collective-permute-start | bytes 442376 | tf_op jit(solution)/shard_map/ppermute | solution.py:452
  44.3 1.2 collective-permute-done.8
  45.5 0.3 collective-permute-start.5
  45.8 0.6 pad_add_fusion.place_ref
  46.4 0.3 collective-permute-done.10
  46.8 1.5 collective-permute-start.11
  48.3 1.9 %collective-permute-start.12 = (bf16[4,2,96,384]{3,2,1,0:T(8,128)(2,1)S(1)}, bf16[4,2,96,384]{3,2,1,0:T(8,128)(2,1)S(1)}, u32[]{:S(2)}, u32[]{:S(2)}) collective-permute-start(bf16[4,2,96,384]{3,2,1,0:T(8,128)(2,1)S(1)} %pad_maximum_fusion.1.refs_10_), channel_id=1, source_target_pairs={{0,24},{8,0},{16,8},{24,16},{1,25},{9,1},{17,9},{25,17},{2,26},{10... | collective-permute-start | bytes 1769480 | tf_op jit(solution)/shard_map/ppermute | solution.py:456
  50.1 1.3 collective-permute-done.4
  51.5 0.8 collective-permute-done.5
  52.4 3.2 %collective-permute-start.7 = (bf16[4,2,96,384]{3,2,1,0:T(8,128)(2,1)S(1)}, bf16[4,2,96,384]{3,2,1,0:T(8,128)(2,1)}, u32[]{:S(2)}, u32[]{:S(2)}) collective-permute-start(bf16[4,2,96,384]{3,2,1,0:T(8,128)(2,1)S(1)} %pad_maximum_fusion.refs_6_), channel_id=1, source_target_pairs={{0,192},{64,0},{128,64},{192,128},{1,193},{65,1},{129,65},{193,129... | collective-permute-start | bytes 1769480 | tf_op jit(solution)/shard_map/ppermute | solution.py:456
  55.6 1.3 all-to-all-done.1.got_ref
  57.2 0.9 broadcast_in_dim.10
  58.1 5.9 %all-to-all-start.2 = ((bf16[4,256,384]{2,1,0:T(8,128)(2,1)}), bf16[4,256,384]{2,1,0:T(8,128)(2,1)}, u32[]{:S(2)}, u32[]{:S(2)}) async-start(bf16[4,256,384]{2,1,0:T(8,128)(2,1)} %broadcast_in_dim.10), calls=%async_computation.2 | async-start | bytes 1572864 | tf_op jit(solution)/shard_map/all_to_all | solution.py:479
  64.0 6.7 %image_attention.2 = (f32[768,384]{1,0:T(8,128)}, f32[768,384]{1,0:T(8,128)}) custom-call(bf16[768,384]{1,0:T(8,128)(2,1)} %refs_2_.1, bf16[4096,384]{1,0:T(8,128)(2,1)} %k_ref.3, bf16[4096,384]{1,0:T(8,128)(2,1)} %v_ref.3), custom_call_target="tpu_custom_call" | custom-call | flops 1 | bytes 1 | tf_op jit(solution)/shard_map/image_attention/pallas_call | solution.py:212
  70.9 1.4 collective-permute-start.14
  72.3 11.1 %image_attention.3 = (f32[768,384]{1,0:T(8,128)}, f32[768,384]{1,0:T(8,128)}) custom-call(bf16[768,384]{1,0:T(8,128)(2,1)} %refs_2_.1, bf16[4096,384]{1,0:T(8,128)(2,1)} %k_ref.3, bf16[4096,384]{1,0:T(8,128)(2,1)} %v_ref.3, f32[768,384]{1,0:T(8,128)} %get-tuple-element.72.refs_0_, ...), custom_call_target="tpu_custom_call", output_to_operand_aliasing={{0}: (3, {}), {1}: (4, {})} | custom-call | flops 1 | bytes 1 | tf_op jit(solution)/shard_map/image_attention/pallas_call | solution.py:212
  83.4 2.1 %collective-permute-done.13.refs_8_ = bf16[4,2,96,384]{3,2,1,0:T(8,128)(2,1)S(1)} collective-permute-done((bf16[4,2,96,384]{3,2,1,0:T(8,128)(2,1)}, bf16[4,2,96,384]{3,2,1,0:T(8,128)(2,1)S(1)}, u32[]{:S(2)}, u32[]{:S(2)}) %collective-permute-start.13) | collective-permute-done | bytes 589856 | tf_op jit(solution)/shard_map/ppermute | solution.py:484
  85.6 3.7 %all-to-all-start.3 = ((bf16[4,256,384]{2,1,0:T(8,128)(2,1)}), bf16[4,256,384]{2,1,0:T(8,128)(2,1)S(1)}, u32[]{:S(2)}, u32[]{:S(2)}) async-start(bf16[4,256,384]{2,1,0:T(8,128)(2,1)} %all-to-all-done.2.refs_0_), calls=%async_computation.3 | async-start | bytes 1572864 | tf_op jit(solution)/shard_map/all_to_all | solution.py:489
  89.4 0.9 copy-done.7
  90.3 11.3 %text_side.1 = (f32[768,384]{1,0:T(8,128)}, bf16[4,256,768]{2,1,0:T(8,128)(2,1)}) custom-call(s32[1]{0:T(128)} %bitcast.3.length_ref, s32[4]{0:T(128)} %pad_add_fusion.place_ref, f32[1,128]{1,0:T(1,128)} %bitcast.40, bf16[4,256,384]{2,1,0:T(8,128)(2,1)} %all-to-all-done.2.refs_0_, bf16[4,256,384]{2,1,0:T(8,128)(2,1)} %copy-done.7, bf16[768,384]{1,0:T(8,128)(2,1)} %refs_2_.1, ...), custom_call_target="tpu_custom_call" | custom-call | tf_op jit(solution)/shard_map/text_side/pallas_call | solution.py:358
  101.5 0.7 all-to-all-done.3
  102.3 3.8 %all-to-all-start.4 = ((bf16[4,256,768]{2,1,0:T(8,128)(2,1)}), bf16[4,256,768]{2,1,0:T(8,128)(2,1)S(1)}, u32[]{:S(2)}, u32[]{:S(2)}) async-start(bf16[4,256,768]{2,1,0:T(8,128)(2,1)} %get-tuple-element.87), calls=%async_computation.4 | async-start | bytes 3145728 | tf_op jit(solution)/shard_map/all_to_all | solution.py:505
  106.1 2.3 %collective-permute-done.16.other_ref = bf16[1024,384]{1,0:T(8,128)(2,1)S(1)} collective-permute-done((bf16[1024,384]{1,0:T(8,128)(2,1)S(1)}, bf16[1024,384]{1,0:T(8,128)(2,1)S(1)}, u32[]{:S(2)}, u32[]{:S(2)}) %collective-permute-start.16) | collective-permute-done | bytes 786464 | tf_op jit(solution)/shard_map/ppermute | solution.py:504
  108.4 1.1 copy-done.3
  109.5 0.5 turn_text.1.text_ref
  110.0 17.2 %all-to-all-done.4 = bf16[4,256,768]{2,1,0:T(8,128)(2,1)S(1)} async-done(((bf16[4,256,768]{2,1,0:T(8,128)(2,1)}), bf16[4,256,768]{2,1,0:T(8,128)(2,1)S(1)}, u32[]{:S(2)}, u32[]{:S(2)}) %all-to-all-start.4) | async-done | bytes 1572896 | tf_op jit(solution)/shard_map/all_to_all | solution.py:505
  127.2 1.6 %gradient.1 = bf16[768,768]{1,0:T(8,128)(2,1)S(1)} custom-call(bf16[768,1024]{1,0:T(8,128)(2,1)S(1)} %turn_text.1.text_ref, bf16[1024,768]{1,0:T(8,128)(2,1)S(1)} %bitcast.25), custom_call_target="tpu_custom_call" | custom-call | tf_op jit(solution)/shard_map/gradient/pallas_call | solution.py:407
  128.8 19.6 %all_to_all.30 = bf16[8,96,768]{2,1,0:T(8,128)(2,1)S(1)} all-to-all(bf16[8,96,768]{2,1,0:T(8,128)(2,1)S(1)} %bitcast.26), channel_id=1, replica_groups=mesh['y'=4,'zl'=2,'x'=4,'zh'=4,'c'=2] {'zl','x'}, dimensions={0} | all-to-all | bytes 2359296 | tf_op jit(solution)/shard_map/all_to_all | solution.py:510
  148.5 0.7 fusion.3
  (48 shorter events, 1.5 us)
Async XLA Ops:
  2.3 18.7 %all-to-all-start = ((bf16[32,8,512]{2,1,0:T(8,128)(2,1)}), bf16[32,8,512]{2,1,0:T(8,128)(2,1)S(1)}, u32[]{:S(2)}, u32[]{:S(2)}) async-start(bf16[32,8,512]{2,1,0:T(8,128)(2,1)} %sort_captions.1), calls=%async_computation | async-start | bytes 524288 | tf_op jit(solution)/shard_map/all_to_all | solution.py:462
  11.0 7.2 %collective-permute-start = (bf16[96,384]{1,0:T(8,128)(2,1)}, bf16[96,384]{1,0:T(8,128)(2,1)S(1)}, u32[]{:S(2)}, u32[]{:S(2)}) collective-permute-start(bf16[96,384]{1,0:T(8,128)(2,1)} %param.15), channel_id=1, source_target_pairs={{0,32},{32,0},{1,33},{33,1},{2,34},{34,2},{3,35},{35,3},{4,36},{36... | collective-permute-start | bytes 221192 | tf_op jit(solution)/shard_map/ppermute | solution.py:458
  12.9 6.2 %collective-permute-start.1 = (bf16[96,384]{1,0:T(8,128)(2,1)}, bf16[96,384]{1,0:T(8,128)(2,1)}, u32[]{:S(2)}, u32[]{:S(2)}) collective-permute-start(bf16[96,384]{1,0:T(8,128)(2,1)} %param.16), channel_id=1, source_target_pairs={{0,32},{32,0},{1,33},{33,1},{2,34},{34,2},{3,35},{35,3},{4,36},{36... | collective-permute-start | bytes 221192 | tf_op jit(solution)/shard_map/ppermute | solution.py:459
  13.1 1.9 %copy-start.1 = (bf16[512,3072]{1,0:T(8,128)(2,1)S(1)}, bf16[512,3072]{1,0:T(8,128)(2,1)}, u32[]{:S(2)}) copy-start(bf16[512,3072]{1,0:T(8,128)(2,1)} %refs_0_.1) | copy-start | bytes 9437188
  15.0 0.7 copy-start.4
  22.7 2.4 %collective-permute-start.2 = (bf16[4,272,384]{2,1,0:T(8,128)(2,1)S(1)}, bf16[4,272,384]{2,1,0:T(8,128)(2,1)S(1)}, u32[]{:S(2)}, u32[]{:S(2)}) collective-permute-start(bf16[4,272,384]{2,1,0:T(8,128)(2,1)S(1)} %get-tuple-element.54), channel_id=1, source_target_pairs={{0,1},{1,0},{2,3},{3,2},{4,5},{5,4},{6,7},{7,6},{8,9},{9,8},{10,11... | collective-permute-start | bytes 2506760 | tf_op jit(solution)/shard_map/ppermute | solution.py:466
  26.5 0.9 copy-start
  27.4 7.4 %copy-start.12 = (bf16[96,384]{1,0:T(8,128)(2,1)S(1)}, bf16[96,384]{1,0:T(8,128)(2,1)}, u32[]{:S(2)}) copy-start(bf16[96,384]{1,0:T(8,128)(2,1)} %param.16) | copy-start | bytes 221188
  27.4 9.0 %copy-start.14 = (s32[32]{0:T(128)S(1)}, s32[32]{0:T(128)}, u32[]{:S(2)}) copy-start(s32[32]{0:T(128)} %assign_ref.1) | copy-start | bytes 388
  27.4 9.0 %copy-start.15 = (s32[32]{0:T(128)S(1)}, s32[32]{0:T(128)}, u32[]{:S(2)}) copy-start(s32[32]{0:T(128)} %param.22) | copy-start | bytes 388
  27.4 13.2 %copy-start.13 = (bf16[96,384]{1,0:T(8,128)(2,1)S(1)}, bf16[96,384]{1,0:T(8,128)(2,1)}, u32[]{:S(2)}) copy-start(bf16[96,384]{1,0:T(8,128)(2,1)} %param.15) | copy-start | bytes 221188
  27.5 29.5 %all-to-all-start.1 = ((bf16[4,272,384]{2,1,0:T(8,128)(2,1)}), bf16[4,272,384]{2,1,0:T(8,128)(2,1)S(1)}, u32[]{:S(2)}, u32[]{:S(2)}) async-start(bf16[4,272,384]{2,1,0:T(8,128)(2,1)} %copy-done), calls=%async_computation.1 | async-start | bytes 1671168 | tf_op jit(solution)/shard_map/all_to_all | solution.py:469
  35.7 9.8 %collective-permute-start.8 = (bf16[2,96,384]{2,1,0:T(8,128)(2,1)S(1)}, bf16[2,96,384]{2,1,0:T(8,128)(2,1)S(1)}, u32[]{:S(2)}, u32[]{:S(2)}) collective-permute-start(bf16[2,96,384]{2,1,0:T(8,128)(2,1)S(1)} %get-tuple-element.94), channel_id=1, source_target_pairs={{0,64},{64,128},{128,192},{192,0},{1,65},{65,129},{129,193},{193,1... | collective-permute-start | bytes 442376 | tf_op jit(solution)/shard_map/ppermute | solution.py:452
  37.1 9.3 %collective-permute-start.9 = (bf16[2,96,384]{2,1,0:T(8,128)(2,1)S(1)}, bf16[2,96,384]{2,1,0:T(8,128)(2,1)S(1)}, u32[]{:S(2)}, u32[]{:S(2)}) collective-permute-start(bf16[2,96,384]{2,1,0:T(8,128)(2,1)S(1)} %get-tuple-element.94), channel_id=1, source_target_pairs={{0,128},{64,192},{128,0},{192,64},{1,129},{65,193},{129,1},{193,65... | collective-permute-start | bytes 442376 | tf_op jit(solution)/shard_map/ppermute | solution.py:452
  39.0 7.7 %collective-permute-start.10 = (bf16[2,96,384]{2,1,0:T(8,128)(2,1)S(1)}, bf16[2,96,384]{2,1,0:T(8,128)(2,1)S(1)}, u32[]{:S(2)}, u32[]{:S(2)}) collective-permute-start(bf16[2,96,384]{2,1,0:T(8,128)(2,1)S(1)} %get-tuple-element.94), channel_id=1, source_target_pairs={{0,192},{64,0},{128,64},{192,128},{1,193},{65,1},{129,65},{193,129... | collective-permute-start | bytes 442376 | tf_op jit(solution)/shard_map/ppermute | solution.py:452
  40.7 9.5 %collective-permute-start.3 = (bf16[2,96,384]{2,1,0:T(8,128)(2,1)S(1)}, bf16[2,96,384]{2,1,0:T(8,128)(2,1)S(1)}, u32[]{:S(2)}, u32[]{:S(2)}) collective-permute-start(bf16[2,96,384]{2,1,0:T(8,128)(2,1)S(1)} %get-tuple-element.96), channel_id=1, source_target_pairs={{0,8},{8,16},{16,24},{24,0},{1,9},{9,17},{17,25},{25,1},{2,10},{10... | collective-permute-start | bytes 442376 | tf_op jit(solution)/shard_map/ppermute | solution.py:452
  41.7 9.8 %collective-permute-start.4 = (bf16[2,96,384]{2,1,0:T(8,128)(2,1)S(1)}, bf16[2,96,384]{2,1,0:T(8,128)(2,1)S(1)}, u32[]{:S(2)}, u32[]{:S(2)}) collective-permute-start(bf16[2,96,384]{2,1,0:T(8,128)(2,1)S(1)} %get-tuple-element.96), channel_id=1, source_target_pairs={{0,16},{8,24},{16,0},{24,8},{1,17},{9,25},{17,1},{25,9},{2,18},{10... | collective-permute-start | bytes 442376 | tf_op jit(solution)/shard_map/ppermute | solution.py:452
  45.5 6.7 %collective-permute-start.5 = (bf16[2,96,384]{2,1,0:T(8,128)(2,1)S(1)}, bf16[2,96,384]{2,1,0:T(8,128)(2,1)S(1)}, u32[]{:S(2)}, u32[]{:S(2)}) collective-permute-start(bf16[2,96,384]{2,1,0:T(8,128)(2,1)S(1)} %get-tuple-element.96), channel_id=1, source_target_pairs={{0,24},{8,0},{16,8},{24,16},{1,25},{9,1},{17,9},{25,17},{2,26},{10... | collective-permute-start | bytes 442376 | tf_op jit(solution)/shard_map/ppermute | solution.py:452
  46.8 11.3 %copy-start.5 = (bf16[4,2,96,384]{3,2,1,0:T(8,128)(2,1)}, bf16[4,2,96,384]{3,2,1,0:T(8,128)(2,1)S(1)}, u32[]{:S(2)}) copy-start(bf16[4,2,96,384]{3,2,1,0:T(8,128)(2,1)S(1)} %pad_maximum_fusion.1.refs_10_) | copy-start | bytes 1769476
  46.8 23.9 %collective-permute-start.11 = (bf16[4,2,96,384]{3,2,1,0:T(8,128)(2,1)S(1)}, bf16[4,2,96,384]{3,2,1,0:T(8,128)(2,1)S(1)}, u32[]{:S(2)}, u32[]{:S(2)}) collective-permute-start(bf16[4,2,96,384]{3,2,1,0:T(8,128)(2,1)S(1)} %pad_maximum_fusion.1.refs_10_), channel_id=1, source_target_pairs={{0,8},{8,16},{16,24},{24,0},{1,9},{9,17},{17,25},{25,1},{2,10},{10... | collective-permute-start | bytes 1769480 | tf_op jit(solution)/shard_map/ppermute | solution.py:456
  48.3 22.5 %collective-permute-start.12 = (bf16[4,2,96,384]{3,2,1,0:T(8,128)(2,1)S(1)}, bf16[4,2,96,384]{3,2,1,0:T(8,128)(2,1)S(1)}, u32[]{:S(2)}, u32[]{:S(2)}) collective-permute-start(bf16[4,2,96,384]{3,2,1,0:T(8,128)(2,1)S(1)} %pad_maximum_fusion.1.refs_10_), channel_id=1, source_target_pairs={{0,24},{8,0},{16,8},{24,16},{1,25},{9,1},{17,9},{25,17},{2,26},{10... | collective-permute-start | bytes 1769480 | tf_op jit(solution)/shard_map/ppermute | solution.py:456
  52.3 5.8 %copy-start.6 = (bf16[4,2,96,384]{3,2,1,0:T(8,128)(2,1)}, bf16[4,2,96,384]{3,2,1,0:T(8,128)(2,1)S(1)}, u32[]{:S(2)}) copy-start(bf16[4,2,96,384]{3,2,1,0:T(8,128)(2,1)S(1)} %pad_maximum_fusion.refs_6_) | copy-start | bytes 1769476
  52.3 18.5 %collective-permute-start.6 = (bf16[4,2,96,384]{3,2,1,0:T(8,128)(2,1)S(1)}, bf16[4,2,96,384]{3,2,1,0:T(8,128)(2,1)}, u32[]{:S(2)}, u32[]{:S(2)}) collective-permute-start(bf16[4,2,96,384]{3,2,1,0:T(8,128)(2,1)S(1)} %pad_maximum_fusion.refs_6_), channel_id=1, source_target_pairs={{0,64},{64,128},{128,192},{192,0},{1,65},{65,129},{129,193},{193,1... | collective-permute-start | bytes 1769480 | tf_op jit(solution)/shard_map/ppermute | solution.py:456
  52.4 18.4 %collective-permute-start.7 = (bf16[4,2,96,384]{3,2,1,0:T(8,128)(2,1)S(1)}, bf16[4,2,96,384]{3,2,1,0:T(8,128)(2,1)}, u32[]{:S(2)}, u32[]{:S(2)}) collective-permute-start(bf16[4,2,96,384]{3,2,1,0:T(8,128)(2,1)S(1)} %pad_maximum_fusion.refs_6_), channel_id=1, source_target_pairs={{0,192},{64,0},{128,64},{192,128},{1,193},{65,1},{129,65},{193,129... | collective-permute-start | bytes 1769480 | tf_op jit(solution)/shard_map/ppermute | solution.py:456
  58.1 27.4 %all-to-all-start.2 = ((bf16[4,256,384]{2,1,0:T(8,128)(2,1)}), bf16[4,256,384]{2,1,0:T(8,128)(2,1)}, u32[]{:S(2)}, u32[]{:S(2)}) async-start(bf16[4,256,384]{2,1,0:T(8,128)(2,1)} %broadcast_in_dim.10), calls=%async_computation.2 | async-start | bytes 1572864 | tf_op jit(solution)/shard_map/all_to_all | solution.py:479
  70.8 12.6 %copy-start.8 = (bf16[4,2,96,384]{3,2,1,0:T(8,128)(2,1)}, bf16[4,2,96,384]{3,2,1,0:T(8,128)(2,1)S(1)}, u32[]{:S(2)}) copy-start(bf16[4,2,96,384]{3,2,1,0:T(8,128)(2,1)S(1)} %collective-permute-done.11.refs_11_) | copy-start | bytes 1769476
  70.8 12.6 %copy-start.9 = (bf16[4,2,96,384]{3,2,1,0:T(8,128)(2,1)}, bf16[4,2,96,384]{3,2,1,0:T(8,128)(2,1)S(1)}, u32[]{:S(2)}) copy-start(bf16[4,2,96,384]{3,2,1,0:T(8,128)(2,1)S(1)} %collective-permute-done.12.refs_13_) | copy-start | bytes 1769476
  70.8 14.7 %collective-permute-start.13 = (bf16[4,2,96,384]{3,2,1,0:T(8,128)(2,1)}, bf16[4,2,96,384]{3,2,1,0:T(8,128)(2,1)S(1)}, u32[]{:S(2)}, u32[]{:S(2)}) collective-permute-start(bf16[4,2,96,384]{3,2,1,0:T(8,128)(2,1)} %collective-permute-done.6.refs_7_), channel_id=1, source_target_pairs={{0,64},{64,128},{128,192},{192,0},{1,65},{65,129},{129,193},{193,1... | collective-permute-start | bytes 1769480 | tf_op jit(solution)/shard_map/ppermute | solution.py:484
  70.9 14.6 %collective-permute-start.14 = (bf16[4,2,96,384]{3,2,1,0:T(8,128)(2,1)S(1)}, bf16[4,2,96,384]{3,2,1,0:T(8,128)(2,1)S(1)}, u32[]{:S(2)}, u32[]{:S(2)}) collective-permute-start(bf16[4,2,96,384]{3,2,1,0:T(8,128)(2,1)S(1)} %collective-permute-done.12.refs_13_), channel_id=1, source_target_pairs={{0,24},{8,0},{16,8},{24,16},{1,25},{9,1},{17,9},{25,17},{2,26},{10... | collective-permute-start | bytes 1769480 | tf_op jit(solution)/shard_map/ppermute | solution.py:485
  85.5 3.9 %copy-start.10 = (bf16[4,2,96,384]{3,2,1,0:T(8,128)(2,1)}, bf16[4,2,96,384]{3,2,1,0:T(8,128)(2,1)S(1)}, u32[]{:S(2)}) copy-start(bf16[4,2,96,384]{3,2,1,0:T(8,128)(2,1)S(1)} %collective-permute-done.13.refs_8_) | copy-start | bytes 1769476
  85.5 3.9 %copy-start.11 = (bf16[4,2,96,384]{3,2,1,0:T(8,128)(2,1)}, bf16[4,2,96,384]{3,2,1,0:T(8,128)(2,1)S(1)}, u32[]{:S(2)}) copy-start(bf16[4,2,96,384]{3,2,1,0:T(8,128)(2,1)S(1)} %collective-permute-done.14.refs_12_) | copy-start | bytes 1769476
  85.5 3.8 %collective-permute-start.15 = (bf16[4,256,384]{2,1,0:T(8,128)(2,1)}, bf16[4,256,384]{2,1,0:T(8,128)(2,1)S(1)}, u32[]{:S(2)}, u32[]{:S(2)}) collective-permute-start(bf16[4,256,384]{2,1,0:T(8,128)(2,1)} %all-to-all-done.2.refs_0_), channel_id=1, source_target_pairs={{0,1},{1,0},{2,3},{3,2},{4,5},{5,4},{6,7},{7,6},{8,9},{9,8},{10,11... | collective-permute-start | bytes 2359304 | tf_op jit(solution)/shard_map/ppermute | solution.py:488
  85.6 16.7 %all-to-all-start.3 = ((bf16[4,256,384]{2,1,0:T(8,128)(2,1)}), bf16[4,256,384]{2,1,0:T(8,128)(2,1)S(1)}, u32[]{:S(2)}, u32[]{:S(2)}) async-start(bf16[4,256,384]{2,1,0:T(8,128)(2,1)} %all-to-all-done.2.refs_0_), calls=%async_computation.3 | async-start | bytes 1572864 | tf_op jit(solution)/shard_map/all_to_all | solution.py:489
  89.3 0.9 copy-start.7
  102.3 3.8 %copy-start.2 = (bf16[4,256,384]{2,1,0:T(8,128)(2,1)}, bf16[4,256,384]{2,1,0:T(8,128)(2,1)S(1)}, u32[]{:S(2)}) copy-start(bf16[4,256,384]{2,1,0:T(8,128)(2,1)S(1)} %all-to-all-done.3) | copy-start | bytes 2359300
  102.3 24.9 %all-to-all-start.4 = ((bf16[4,256,768]{2,1,0:T(8,128)(2,1)}), bf16[4,256,768]{2,1,0:T(8,128)(2,1)S(1)}, u32[]{:S(2)}, u32[]{:S(2)}) async-start(bf16[4,256,768]{2,1,0:T(8,128)(2,1)} %get-tuple-element.87), calls=%async_computation.4 | async-start | bytes 3145728 | tf_op jit(solution)/shard_map/all_to_all | solution.py:505
  106.1 2.3 %collective-permute-start.16 = (bf16[1024,384]{1,0:T(8,128)(2,1)S(1)}, bf16[1024,384]{1,0:T(8,128)(2,1)S(1)}, u32[]{:S(2)}, u32[]{:S(2)}) collective-permute-start(bf16[1024,384]{1,0:T(8,128)(2,1)S(1)} %bitcast.27), channel_id=1, source_target_pairs={{0,1},{1,0},{2,3},{3,2},{4,5},{5,4},{6,7},{7,6},{8,9},{9,8},{10,11... | collective-permute-start | bytes 2359304 | tf_op jit(solution)/shard_map/ppermute | solution.py:504
  108.4 1.1 copy-start.3

commit v5 on v4

--- a/solution.py
+++ b/solution.py
@@ -210,7 +210,7 @@
 def image_attention(q, k, v, heads, before):
     column = lambda i: (0, heads[0] + i)
     return pl.pallas_call(
-        functools.partial(image_kernel, block=512, rows=256),
+        functools.partial(image_kernel, block=256, rows=384),
         grid=(len(heads),),
         in_specs=[
             pl.BlockSpec((IQ, HD), column),
@@ -228,7 +228,9 @@
     )(q, k, v, *before)
 
 
-def heads_attention(length, key_pres, values, qs, gs, gain, image_sums, stats):
+def heads_attention(
+    length, key_pres, values, qs, gs, gain, image_sums, stats, leave_joint, leave_cot
+):
     factor = SCALE * LOG2E
     every = range(HEADS)
     keep = lax.broadcasted_iota(jnp.int32, (CT, 1), 0) < length
@@ -255,21 +257,22 @@
     probs = [p.astype(BF16) for p in ps]
     scales = [jnp.broadcast_to(fades[h] * inverses[h], (HD, IQ)).T for h in every]
     joints = [image_sums[h] * scales[h] + dot(probs[h], values[h], TN) for h in every]
+    for h in every:
+        leave_joint(h, joints[h])
+    d_values = [dot(probs[h], gs[h]).astype(BF16) for h in every]
+    for h in every:
+        leave_cot(h, 1, d_values[h])
     means = [
         jnp.sum((gs[h].astype(F32) * joints[h]).T, axis=0, keepdims=True) for h in every
     ]
     d_probs = [dot(values[h], gs[h], NT) for h in every]
     ds = [(ps[h] * (d_probs[h] - means[h]) * SCALE).astype(BF16) for h in every]
-    d_values = [dot(probs[h], gs[h]).astype(BF16) for h in every]
     d_keys = [dot(ds[h], qs[h]).astype(BF16).astype(F32) * gain for h in every]
-    d_pres = []
     for h in every:
         root, key_pre, d_key = roots[h], key_pres[h], d_keys[h]
         along = jnp.mean(d_key * key_pre, axis=1, keepdims=True)
-        d_pres.append(
-            (root * d_key - key_pre * (root * root * root * along)).astype(BF16)
-        )
-    return joints, d_pres, d_values
+        d_pre = root * d_key - key_pre * (root * root * root * along)
+        leave_cot(h, 0, d_pre.astype(BF16))
 
 
 def text_side_kernel(length_ref, place_ref, gain_ref, *refs):
@@ -319,7 +322,29 @@
     for i in range(2, 6):
         fetch[i].wait()
     columns = [slice(h * HD, (h + 1) * HD) for h in range(HEADS)]
-    joints, d_pres, d_values = heads_attention(
+    leave = []
+
+    def leave_joint(h, joint):
+        joined[:, columns[h]] = joint
+        leave.append(
+            pltpu.make_async_copy(
+                joined.at[:, columns[h]], out_ref.at[:, columns[h]], out_sems.at[h]
+            )
+        )
+        leave[-1].start()
+
+    def leave_cot(h, n, value):
+        span = slice(n * COLS + h * HD, n * COLS + (h + 1) * HD)
+        cots[:, span] = value
+        for i in range(NY):
+            leave.append(
+                pltpu.make_async_copy(
+                    cots.at[:, span], cot_ref.at[i, :, span], cot_sems.at[h, n, i]
+                )
+            )
+            leave[-1].start()
+
+    heads_attention(
         length_ref[0],
         [kv[:, cols] for cols in columns],
         [kv[:, COLS + h * HD : COLS + (h + 1) * HD].astype(BF16) for h in range(HEADS)],
@@ -328,25 +353,9 @@
         gain_ref[...],
         [image_sum[:, cols] for cols in columns],
         [stats[:, cols] for cols in columns],
+        leave_joint,
+        leave_cot,
     )
-    leave = []
-    for h, cols in enumerate(columns):
-        joint, d_pre, d_value = joints[h], d_pres[h], d_values[h]
-        for n, value in ((0, d_pre), (1, d_value)):
-            span = slice(n * COLS + h * HD, n * COLS + (h + 1) * HD)
-            cots[:, span] = value
-            for i in range(NY):
-                leave.append(
-                    pltpu.make_async_copy(
-                        cots.at[:, span], cot_ref.at[i, :, span], cot_sems.at[h, n, i]
-                    )
-                )
-                leave[-1].start()
-        joined[:, cols] = joint
-        leave.append(
-            pltpu.make_async_copy(joined.at[:, cols], out_ref.at[:, cols], out_sems.at[h])
-        )
-        leave[-1].start()
     for move in leave:
         move.wait()
 

time: 150 us -> 149 us (level)
  transfers between devices with their start and end apart: 22 -> 22, of which waited for: 13 -> 13; matrix products, arithmetic and copies ran while one was open for 2% -> 2% of each run, Pallas kernels for 20% -> 19%
where the time goes in v5:
time: 149 us; the launch traced here: 148 us
  starting transfers between devices  48 us (32%)
  waiting for transfers between devices  35.3 us (24%)
  Pallas kernels  35 us (23%)
  blocking collectives  19.4 us (13%)
  local copies, waits for them, and re-layouts  7.22 us (5%)
  other arithmetic  2.47 us (2%)
    all_to_all x1, blocking collectives, body(): grad = lax.all_to_all(grad, ('zl', 'x'), 0, 0, tiled=True)  19.4 us
    pallas_call x2, Pallas kernels, image_attention(): pl.pallas_call(functools.partial(image_kernel, block=256, rows=384), grid...  17.1 us
    all_to_all x1, waiting for transfers between devices, body(): cot = lax.all_to_all(cot, 'y', 0, 0, tiled=True)  16.8 us
    pallas_call x1, Pallas kernels, text_side(): pl.pallas_call(text_side_kernel, in_specs=[smem, smem, pl.BlockSpec(memor...  10.8 us
    all_to_all x1, starting transfers between devices, body(): mine = lax.all_to_all(mine, ('y', 'zl', 'x'), 0, 0, tiled=True)  8.67 us
    ppermute x6, starting transfers between devices, around(): two, one, three = [lax.ppermute(block, axis, ring(k)) for k in (2, 1, 3)]  8.25 us
    all_to_all x1, starting transfers between devices, body(): got = lax.all_to_all(summed, 'zh', 0, 0, tiled=True)  7.35 us
    ppermute x4, starting transfers between devices, beside(): return [lax.ppermute(block, axis, ring(k)) for k in (1, 3)]  6.62 us
  transfers between devices with their start and end apart: 22, of which 13 were waited for; matrix products, arithmetic and copies ran while one was open for 2% of the time, Pallas kernels for 19%

profile of v5, /device:TPU:64, one launch (start us, length us, event | category | flops | bytes accessed | tf_op | source)
XLA Modules:
  0.0 148.3 jit_solution(15943850291254447716)
XLA Ops:
  0.6 1.7 %sort_captions.1 = bf16[32,8,512]{2,1,0:T(8,128)(2,1)} custom-call(s32[32]{0:T(128)} %assign_ref.1, bf16[32,8,512]{2,1,0:T(8,128)(2,1)} %x_ref.1), custom_call_target="tpu_custom_call" | custom-call | tf_op jit(solution)/shard_map/sort_captions/pallas_call | solution.py:68
  2.3 8.7 %all-to-all-start = ((bf16[32,8,512]{2,1,0:T(8,128)(2,1)}), bf16[32,8,512]{2,1,0:T(8,128)(2,1)S(1)}, u32[]{:S(2)}, u32[]{:S(2)}) async-start(bf16[32,8,512]{2,1,0:T(8,128)(2,1)} %sort_captions.1), calls=%async_computation | async-start | bytes 524288 | tf_op jit(solution)/shard_map/all_to_all | solution.py:471
  11.0 1.9 %collective-permute-start = (bf16[96,384]{1,0:T(8,128)(2,1)}, bf16[96,384]{1,0:T(8,128)(2,1)S(1)}, u32[]{:S(2)}, u32[]{:S(2)}) collective-permute-start(bf16[96,384]{1,0:T(8,128)(2,1)} %param.15), channel_id=1, source_target_pairs={{0,32},{32,0},{1,33},{33,1},{2,34},{34,2},{3,35},{35,3},{4,36},{36... | collective-permute-start | bytes 221192 | tf_op jit(solution)/shard_map/ppermute | solution.py:467
  13.1 1.9 %copy-done.1 = bf16[512,3072]{1,0:T(8,128)(2,1)S(1)} copy-done((bf16[512,3072]{1,0:T(8,128)(2,1)S(1)}, bf16[512,3072]{1,0:T(8,128)(2,1)}, u32[]{:S(2)}) %copy-start.1) | copy-done | bytes 3145752
  15.0 0.7 copy-done.4
  15.9 2.3 %collective-permute-done = bf16[96,384]{1,0:T(8,128)(2,1)S(1)} collective-permute-done((bf16[96,384]{1,0:T(8,128)(2,1)}, bf16[96,384]{1,0:T(8,128)(2,1)S(1)}, u32[]{:S(2)}, u32[]{:S(2)}) %collective-permute-start) | collective-permute-done | bytes 73760 | tf_op jit(solution)/shard_map/ppermute | solution.py:467
  18.2 0.9 collective-permute-done.1
  19.1 2.0 %all-to-all-done = bf16[32,8,512]{2,1,0:T(8,128)(2,1)S(1)} async-done(((bf16[32,8,512]{2,1,0:T(8,128)(2,1)}), bf16[32,8,512]{2,1,0:T(8,128)(2,1)S(1)}, u32[]{:S(2)}, u32[]{:S(2)}) %all-to-all-start) | async-done | bytes 262176 | tf_op jit(solution)/shard_map/all_to_all | solution.py:471
  21.1 1.6 %text_other_half.1 = (bf16[4,272,384]{2,1,0:T(8,128)(2,1)S(1)}, bf16[256,512]{1,0:T(8,128)(2,1)S(1)}, f32[8,256]{1,0:T(8,128)S(1)}) custom-call(s32[1]{0:T(128)} %bitcast.core_ref, bf16[256,512]{1,0:T(8,128)(2,1)S(1)} %bitcast.29, f32[1,512]{1,0:T(1,128)S(1)} %get-tuple-element.50.gain_ref, bf16[512,3072]{1,0:T(8,128)(2,1)S(1)} %get-tuple-element.51.w_ref), custom_call_target="tpu_custom_call" | custom-call | tf_op jit(solution)/shard_map/text_other_half/pallas_call | solution.py:116
  22.8 2.3 %collective-permute-done.2.got_ref = bf16[4,272,384]{2,1,0:T(8,128)(2,1)S(1)} collective-permute-done((bf16[4,272,384]{2,1,0:T(8,128)(2,1)S(1)}, bf16[4,272,384]{2,1,0:T(8,128)(2,1)S(1)}, u32[]{:S(2)}, u32[]{:S(2)}) %collective-permute-start.2) | collective-permute-done | bytes 835616 | tf_op jit(solution)/shard_map/ppermute | solution.py:475
  25.1 1.4 text_own_half.1
  26.6 0.9 copy-done
  27.5 7.3 %all-to-all-start.1 = ((bf16[4,272,384]{2,1,0:T(8,128)(2,1)}), bf16[4,272,384]{2,1,0:T(8,128)(2,1)S(1)}, u32[]{:S(2)}, u32[]{:S(2)}) async-start(bf16[4,272,384]{2,1,0:T(8,128)(2,1)} %copy-done), calls=%async_computation.1 | async-start | bytes 1671168 | tf_op jit(solution)/shard_map/all_to_all | solution.py:478
  34.8 0.9 fusion.1
  35.7 0.7 collective-permute-start.8
  36.4 0.6 fusion
  37.1 2.0 %collective-permute-start.9 = (bf16[2,96,384]{2,1,0:T(8,128)(2,1)S(1)}, bf16[2,96,384]{2,1,0:T(8,128)(2,1)S(1)}, u32[]{:S(2)}, u32[]{:S(2)}) collective-permute-start(bf16[2,96,384]{2,1,0:T(8,128)(2,1)S(1)} %get-tuple-element.94), channel_id=1, source_target_pairs={{0,128},{64,192},{128,0},{192,64},{1,129},{65,193},{129,1},{193,65... | collective-permute-start | bytes 442376 | tf_op jit(solution)/shard_map/ppermute | solution.py:461
  39.0 1.6 %collective-permute-start.10 = (bf16[2,96,384]{2,1,0:T(8,128)(2,1)S(1)}, bf16[2,96,384]{2,1,0:T(8,128)(2,1)S(1)}, u32[]{:S(2)}, u32[]{:S(2)}) collective-permute-start(bf16[2,96,384]{2,1,0:T(8,128)(2,1)S(1)} %get-tuple-element.94), channel_id=1, source_target_pairs={{0,192},{64,0},{128,64},{192,128},{1,193},{65,1},{129,65},{193,129... | collective-permute-start | bytes 442376 | tf_op jit(solution)/shard_map/ppermute | solution.py:461
  40.7 1.0 collective-permute-start.3
  41.7 2.7 %collective-permute-start.4 = (bf16[2,96,384]{2,1,0:T(8,128)(2,1)S(1)}, bf16[2,96,384]{2,1,0:T(8,128)(2,1)S(1)}, u32[]{:S(2)}, u32[]{:S(2)}) collective-permute-start(bf16[2,96,384]{2,1,0:T(8,128)(2,1)S(1)} %get-tuple-element.96), channel_id=1, source_target_pairs={{0,16},{8,24},{16,0},{24,8},{1,17},{9,25},{17,1},{25,9},{2,18},{10... | collective-permute-start | bytes 442376 | tf_op jit(solution)/shard_map/ppermute | solution.py:461
  44.3 1.2 collective-permute-done.8
  45.5 0.3 collective-permute-start.5
  45.8 0.6 pad_add_fusion.place_ref
  46.4 0.3 collective-permute-done.10
  46.8 1.5 collective-permute-start.11
  48.3 1.9 %collective-permute-start.12 = (bf16[4,2,96,384]{3,2,1,0:T(8,128)(2,1)S(1)}, bf16[4,2,96,384]{3,2,1,0:T(8,128)(2,1)S(1)}, u32[]{:S(2)}, u32[]{:S(2)}) collective-permute-start(bf16[4,2,96,384]{3,2,1,0:T(8,128)(2,1)S(1)} %pad_maximum_fusion.1.refs_10_), channel_id=1, source_target_pairs={{0,24},{8,0},{16,8},{24,16},{1,25},{9,1},{17,9},{25,17},{2,26},{10... | collective-permute-start | bytes 1769480 | tf_op jit(solution)/shard_map/ppermute | solution.py:465
  50.1 1.3 collective-permute-done.4
  51.5 0.8 collective-permute-done.5
  52.4 3.2 %collective-permute-start.7 = (bf16[4,2,96,384]{3,2,1,0:T(8,128)(2,1)S(1)}, bf16[4,2,96,384]{3,2,1,0:T(8,128)(2,1)}, u32[]{:S(2)}, u32[]{:S(2)}) collective-permute-start(bf16[4,2,96,384]{3,2,1,0:T(8,128)(2,1)S(1)} %pad_maximum_fusion.refs_6_), channel_id=1, source_target_pairs={{0,192},{64,0},{128,64},{192,128},{1,193},{65,1},{129,65},{193,129... | collective-permute-start | bytes 1769480 | tf_op jit(solution)/shard_map/ppermute | solution.py:465
  55.6 1.3 all-to-all-done.1.got_ref
  57.2 0.9 broadcast_in_dim.10
  58.1 5.9 %all-to-all-start.2 = ((bf16[4,256,384]{2,1,0:T(8,128)(2,1)}), bf16[4,256,384]{2,1,0:T(8,128)(2,1)}, u32[]{:S(2)}, u32[]{:S(2)}) async-start(bf16[4,256,384]{2,1,0:T(8,128)(2,1)} %broadcast_in_dim.10), calls=%async_computation.2 | async-start | bytes 1572864 | tf_op jit(solution)/shard_map/all_to_all | solution.py:488
  64.0 6.5 %image_attention.2 = (f32[768,384]{1,0:T(8,128)}, f32[768,384]{1,0:T(8,128)}) custom-call(bf16[768,384]{1,0:T(8,128)(2,1)} %refs_2_.1, bf16[4096,384]{1,0:T(8,128)(2,1)} %k_ref.3, bf16[4096,384]{1,0:T(8,128)(2,1)} %v_ref.3), custom_call_target="tpu_custom_call" | custom-call | flops 1 | bytes 1 | tf_op jit(solution)/shard_map/image_attention/pallas_call | solution.py:212
  70.6 1.4 collective-permute-start.14
  72.1 10.6 %image_attention.3 = (f32[768,384]{1,0:T(8,128)}, f32[768,384]{1,0:T(8,128)}) custom-call(bf16[768,384]{1,0:T(8,128)(2,1)} %refs_2_.1, bf16[4096,384]{1,0:T(8,128)(2,1)} %k_ref.3, bf16[4096,384]{1,0:T(8,128)(2,1)} %v_ref.3, f32[768,384]{1,0:T(8,128)} %get-tuple-element.72.refs_0_, ...), custom_call_target="tpu_custom_call", output_to_operand_aliasing={{0}: (3, {}), {1}: (4, {})} | custom-call | flops 1 | bytes 1 | tf_op jit(solution)/shard_map/image_attention/pallas_call | solution.py:212
  82.7 2.6 %collective-permute-done.13.refs_8_ = bf16[4,2,96,384]{3,2,1,0:T(8,128)(2,1)S(1)} collective-permute-done((bf16[4,2,96,384]{3,2,1,0:T(8,128)(2,1)}, bf16[4,2,96,384]{3,2,1,0:T(8,128)(2,1)S(1)}, u32[]{:S(2)}, u32[]{:S(2)}) %collective-permute-start.13) | collective-permute-done | bytes 589856 | tf_op jit(solution)/shard_map/ppermute | solution.py:493
  85.3 3.7 %all-to-all-start.3 = ((bf16[4,256,384]{2,1,0:T(8,128)(2,1)}), bf16[4,256,384]{2,1,0:T(8,128)(2,1)S(1)}, u32[]{:S(2)}, u32[]{:S(2)}) async-start(bf16[4,256,384]{2,1,0:T(8,128)(2,1)} %all-to-all-done.2.refs_0_), calls=%async_computation.3 | async-start | bytes 1572864 | tf_op jit(solution)/shard_map/all_to_all | solution.py:498
  89.1 0.9 copy-done.7
  90.0 10.8 %text_side.1 = (f32[768,384]{1,0:T(8,128)}, bf16[4,256,768]{2,1,0:T(8,128)(2,1)}) custom-call(s32[1]{0:T(128)} %bitcast.3.length_ref, s32[4]{0:T(128)} %pad_add_fusion.place_ref, f32[1,128]{1,0:T(1,128)} %bitcast.40, bf16[4,256,384]{2,1,0:T(8,128)(2,1)} %all-to-all-done.2.refs_0_, bf16[4,256,384]{2,1,0:T(8,128)(2,1)} %copy-done.7, bf16[768,384]{1,0:T(8,128)(2,1)} %refs_2_.1, ...), custom_call_target="tpu_custom_call" | custom-call | tf_op jit(solution)/shard_map/text_side/pallas_call | solution.py:367
  100.8 1.2 all-to-all-done.3
  102.0 3.6 %all-to-all-start.4 = ((bf16[4,256,768]{2,1,0:T(8,128)(2,1)}), bf16[4,256,768]{2,1,0:T(8,128)(2,1)S(1)}, u32[]{:S(2)}, u32[]{:S(2)}) async-start(bf16[4,256,768]{2,1,0:T(8,128)(2,1)} %get-tuple-element.87), calls=%async_computation.4 | async-start | bytes 3145728 | tf_op jit(solution)/shard_map/all_to_all | solution.py:514
  105.7 2.3 %collective-permute-done.16.other_ref = bf16[1024,384]{1,0:T(8,128)(2,1)S(1)} collective-permute-done((bf16[1024,384]{1,0:T(8,128)(2,1)S(1)}, bf16[1024,384]{1,0:T(8,128)(2,1)S(1)}, u32[]{:S(2)}, u32[]{:S(2)}) %collective-permute-start.16) | collective-permute-done | bytes 786464 | tf_op jit(solution)/shard_map/ppermute | solution.py:513
  108.0 1.1 copy-done.3
  109.1 0.5 turn_text.1.text_ref
  109.6 16.8 %all-to-all-done.4 = bf16[4,256,768]{2,1,0:T(8,128)(2,1)S(1)} async-done(((bf16[4,256,768]{2,1,0:T(8,128)(2,1)}), bf16[4,256,768]{2,1,0:T(8,128)(2,1)S(1)}, u32[]{:S(2)}, u32[]{:S(2)}) %all-to-all-start.4) | async-done | bytes 1572896 | tf_op jit(solution)/shard_map/all_to_all | solution.py:514
  126.4 1.6 %gradient.1 = bf16[768,768]{1,0:T(8,128)(2,1)S(1)} custom-call(bf16[768,1024]{1,0:T(8,128)(2,1)S(1)} %turn_text.1.text_ref, bf16[1024,768]{1,0:T(8,128)(2,1)S(1)} %bitcast.25), custom_call_target="tpu_custom_call" | custom-call | tf_op jit(solution)/shard_map/gradient/pallas_call | solution.py:416
  128.0 19.4 %all_to_all.30 = bf16[8,96,768]{2,1,0:T(8,128)(2,1)S(1)} all-to-all(bf16[8,96,768]{2,1,0:T(8,128)(2,1)S(1)} %bitcast.26), channel_id=1, replica_groups=mesh['y'=4,'zl'=2,'x'=4,'zh'=4,'c'=2] {'zl','x'}, dimensions={0} | all-to-all | bytes 2359296 | tf_op jit(solution)/shard_map/all_to_all | solution.py:519
  147.6 0.7 fusion.3
  (48 shorter events, 1.6 us)
Async XLA Ops:
  2.3 18.7 %all-to-all-start = ((bf16[32,8,512]{2,1,0:T(8,128)(2,1)}), bf16[32,8,512]{2,1,0:T(8,128)(2,1)S(1)}, u32[]{:S(2)}, u32[]{:S(2)}) async-start(bf16[32,8,512]{2,1,0:T(8,128)(2,1)} %sort_captions.1), calls=%async_computation | async-start | bytes 524288 | tf_op jit(solution)/shard_map/all_to_all | solution.py:471
  11.0 7.2 %collective-permute-start = (bf16[96,384]{1,0:T(8,128)(2,1)}, bf16[96,384]{1,0:T(8,128)(2,1)S(1)}, u32[]{:S(2)}, u32[]{:S(2)}) collective-permute-start(bf16[96,384]{1,0:T(8,128)(2,1)} %param.15), channel_id=1, source_target_pairs={{0,32},{32,0},{1,33},{33,1},{2,34},{34,2},{3,35},{35,3},{4,36},{36... | collective-permute-start | bytes 221192 | tf_op jit(solution)/shard_map/ppermute | solution.py:467
  12.9 6.2 %collective-permute-start.1 = (bf16[96,384]{1,0:T(8,128)(2,1)}, bf16[96,384]{1,0:T(8,128)(2,1)}, u32[]{:S(2)}, u32[]{:S(2)}) collective-permute-start(bf16[96,384]{1,0:T(8,128)(2,1)} %param.16), channel_id=1, source_target_pairs={{0,32},{32,0},{1,33},{33,1},{2,34},{34,2},{3,35},{35,3},{4,36},{36... | collective-permute-start | bytes 221192 | tf_op jit(solution)/shard_map/ppermute | solution.py:468
  13.1 1.9 %copy-start.1 = (bf16[512,3072]{1,0:T(8,128)(2,1)S(1)}, bf16[512,3072]{1,0:T(8,128)(2,1)}, u32[]{:S(2)}) copy-start(bf16[512,3072]{1,0:T(8,128)(2,1)} %refs_0_.1) | copy-start | bytes 9437188
  15.0 0.7 copy-start.4
  22.7 2.4 %collective-permute-start.2 = (bf16[4,272,384]{2,1,0:T(8,128)(2,1)S(1)}, bf16[4,272,384]{2,1,0:T(8,128)(2,1)S(1)}, u32[]{:S(2)}, u32[]{:S(2)}) collective-permute-start(bf16[4,272,384]{2,1,0:T(8,128)(2,1)S(1)} %get-tuple-element.54), channel_id=1, source_target_pairs={{0,1},{1,0},{2,3},{3,2},{4,5},{5,4},{6,7},{7,6},{8,9},{9,8},{10,11... | collective-permute-start | bytes 2506760 | tf_op jit(solution)/shard_map/ppermute | solution.py:475
  26.5 0.9 copy-start
  27.4 7.4 %copy-start.12 = (bf16[96,384]{1,0:T(8,128)(2,1)S(1)}, bf16[96,384]{1,0:T(8,128)(2,1)}, u32[]{:S(2)}) copy-start(bf16[96,384]{1,0:T(8,128)(2,1)} %param.16) | copy-start | bytes 221188
  27.4 9.0 %copy-start.14 = (s32[32]{0:T(128)S(1)}, s32[32]{0:T(128)}, u32[]{:S(2)}) copy-start(s32[32]{0:T(128)} %assign_ref.1) | copy-start | bytes 388
  27.4 9.0 %copy-start.15 = (s32[32]{0:T(128)S(1)}, s32[32]{0:T(128)}, u32[]{:S(2)}) copy-start(s32[32]{0:T(128)} %param.22) | copy-start | bytes 388
  27.4 13.2 %copy-start.13 = (bf16[96,384]{1,0:T(8,128)(2,1)S(1)}, bf16[96,384]{1,0:T(8,128)(2,1)}, u32[]{:S(2)}) copy-start(bf16[96,384]{1,0:T(8,128)(2,1)} %param.15) | copy-start | bytes 221188
  27.5 29.5 %all-to-all-start.1 = ((bf16[4,272,384]{2,1,0:T(8,128)(2,1)}), bf16[4,272,384]{2,1,0:T(8,128)(2,1)S(1)}, u32[]{:S(2)}, u32[]{:S(2)}) async-start(bf16[4,272,384]{2,1,0:T(8,128)(2,1)} %copy-done), calls=%async_computation.1 | async-start | bytes 1671168 | tf_op jit(solution)/shard_map/all_to_all | solution.py:478
  35.7 9.8 %collective-permute-start.8 = (bf16[2,96,384]{2,1,0:T(8,128)(2,1)S(1)}, bf16[2,96,384]{2,1,0:T(8,128)(2,1)S(1)}, u32[]{:S(2)}, u32[]{:S(2)}) collective-permute-start(bf16[2,96,384]{2,1,0:T(8,128)(2,1)S(1)} %get-tuple-element.94), channel_id=1, source_target_pairs={{0,64},{64,128},{128,192},{192,0},{1,65},{65,129},{129,193},{193,1... | collective-permute-start | bytes 442376 | tf_op jit(solution)/shard_map/ppermute | solution.py:461
  37.1 9.3 %collective-permute-start.9 = (bf16[2,96,384]{2,1,0:T(8,128)(2,1)S(1)}, bf16[2,96,384]{2,1,0:T(8,128)(2,1)S(1)}, u32[]{:S(2)}, u32[]{:S(2)}) collective-permute-start(bf16[2,96,384]{2,1,0:T(8,128)(2,1)S(1)} %get-tuple-element.94), channel_id=1, source_target_pairs={{0,128},{64,192},{128,0},{192,64},{1,129},{65,193},{129,1},{193,65... | collective-permute-start | bytes 442376 | tf_op jit(solution)/shard_map/ppermute | solution.py:461
  39.0 7.7 %collective-permute-start.10 = (bf16[2,96,384]{2,1,0:T(8,128)(2,1)S(1)}, bf16[2,96,384]{2,1,0:T(8,128)(2,1)S(1)}, u32[]{:S(2)}, u32[]{:S(2)}) collective-permute-start(bf16[2,96,384]{2,1,0:T(8,128)(2,1)S(1)} %get-tuple-element.94), channel_id=1, source_target_pairs={{0,192},{64,0},{128,64},{192,128},{1,193},{65,1},{129,65},{193,129... | collective-permute-start | bytes 442376 | tf_op jit(solution)/shard_map/ppermute | solution.py:461
  40.7 9.5 %collective-permute-start.3 = (bf16[2,96,384]{2,1,0:T(8,128)(2,1)S(1)}, bf16[2,96,384]{2,1,0:T(8,128)(2,1)S(1)}, u32[]{:S(2)}, u32[]{:S(2)}) collective-permute-start(bf16[2,96,384]{2,1,0:T(8,128)(2,1)S(1)} %get-tuple-element.96), channel_id=1, source_target_pairs={{0,8},{8,16},{16,24},{24,0},{1,9},{9,17},{17,25},{25,1},{2,10},{10... | collective-permute-start | bytes 442376 | tf_op jit(solution)/shard_map/ppermute | solution.py:461
  41.7 9.8 %collective-permute-start.4 = (bf16[2,96,384]{2,1,0:T(8,128)(2,1)S(1)}, bf16[2,96,384]{2,1,0:T(8,128)(2,1)S(1)}, u32[]{:S(2)}, u32[]{:S(2)}) collective-permute-start(bf16[2,96,384]{2,1,0:T(8,128)(2,1)S(1)} %get-tuple-element.96), channel_id=1, source_target_pairs={{0,16},{8,24},{16,0},{24,8},{1,17},{9,25},{17,1},{25,9},{2,18},{10... | collective-permute-start | bytes 442376 | tf_op jit(solution)/shard_map/ppermute | solution.py:461
  45.5 6.7 %collective-permute-start.5 = (bf16[2,96,384]{2,1,0:T(8,128)(2,1)S(1)}, bf16[2,96,384]{2,1,0:T(8,128)(2,1)S(1)}, u32[]{:S(2)}, u32[]{:S(2)}) collective-permute-start(bf16[2,96,384]{2,1,0:T(8,128)(2,1)S(1)} %get-tuple-element.96), channel_id=1, source_target_pairs={{0,24},{8,0},{16,8},{24,16},{1,25},{9,1},{17,9},{25,17},{2,26},{10... | collective-permute-start | bytes 442376 | tf_op jit(solution)/shard_map/ppermute | solution.py:461
  46.8 11.3 %copy-start.5 = (bf16[4,2,96,384]{3,2,1,0:T(8,128)(2,1)}, bf16[4,2,96,384]{3,2,1,0:T(8,128)(2,1)S(1)}, u32[]{:S(2)}) copy-start(bf16[4,2,96,384]{3,2,1,0:T(8,128)(2,1)S(1)} %pad_maximum_fusion.1.refs_10_) | copy-start | bytes 1769476
  46.8 23.7 %collective-permute-start.11 = (bf16[4,2,96,384]{3,2,1,0:T(8,128)(2,1)S(1)}, bf16[4,2,96,384]{3,2,1,0:T(8,128)(2,1)S(1)}, u32[]{:S(2)}, u32[]{:S(2)}) collective-permute-start(bf16[4,2,96,384]{3,2,1,0:T(8,128)(2,1)S(1)} %pad_maximum_fusion.1.refs_10_), channel_id=1, source_target_pairs={{0,8},{8,16},{16,24},{24,0},{1,9},{9,17},{17,25},{25,1},{2,10},{10... | collective-permute-start | bytes 1769480 | tf_op jit(solution)/shard_map/ppermute | solution.py:465
  48.3 22.3 %collective-permute-start.12 = (bf16[4,2,96,384]{3,2,1,0:T(8,128)(2,1)S(1)}, bf16[4,2,96,384]{3,2,1,0:T(8,128)(2,1)S(1)}, u32[]{:S(2)}, u32[]{:S(2)}) collective-permute-start(bf16[4,2,96,384]{3,2,1,0:T(8,128)(2,1)S(1)} %pad_maximum_fusion.1.refs_10_), channel_id=1, source_target_pairs={{0,24},{8,0},{16,8},{24,16},{1,25},{9,1},{17,9},{25,17},{2,26},{10... | collective-permute-start | bytes 1769480 | tf_op jit(solution)/shard_map/ppermute | solution.py:465
  52.3 5.8 %copy-start.6 = (bf16[4,2,96,384]{3,2,1,0:T(8,128)(2,1)}, bf16[4,2,96,384]{3,2,1,0:T(8,128)(2,1)S(1)}, u32[]{:S(2)}) copy-start(bf16[4,2,96,384]{3,2,1,0:T(8,128)(2,1)S(1)} %pad_maximum_fusion.refs_6_) | copy-start | bytes 1769476
  52.3 18.2 %collective-permute-start.6 = (bf16[4,2,96,384]{3,2,1,0:T(8,128)(2,1)S(1)}, bf16[4,2,96,384]{3,2,1,0:T(8,128)(2,1)}, u32[]{:S(2)}, u32[]{:S(2)}) collective-permute-start(bf16[4,2,96,384]{3,2,1,0:T(8,128)(2,1)S(1)} %pad_maximum_fusion.refs_6_), channel_id=1, source_target_pairs={{0,64},{64,128},{128,192},{192,0},{1,65},{65,129},{129,193},{193,1... | collective-permute-start | bytes 1769480 | tf_op jit(solution)/shard_map/ppermute | solution.py:465
  52.4 18.1 %collective-permute-start.7 = (bf16[4,2,96,384]{3,2,1,0:T(8,128)(2,1)S(1)}, bf16[4,2,96,384]{3,2,1,0:T(8,128)(2,1)}, u32[]{:S(2)}, u32[]{:S(2)}) collective-permute-start(bf16[4,2,96,384]{3,2,1,0:T(8,128)(2,1)S(1)} %pad_maximum_fusion.refs_6_), channel_id=1, source_target_pairs={{0,192},{64,0},{128,64},{192,128},{1,193},{65,1},{129,65},{193,129... | collective-permute-start | bytes 1769480 | tf_op jit(solution)/shard_map/ppermute | solution.py:465
  58.1 27.1 %all-to-all-start.2 = ((bf16[4,256,384]{2,1,0:T(8,128)(2,1)}), bf16[4,256,384]{2,1,0:T(8,128)(2,1)}, u32[]{:S(2)}, u32[]{:S(2)}) async-start(bf16[4,256,384]{2,1,0:T(8,128)(2,1)} %broadcast_in_dim.10), calls=%async_computation.2 | async-start | bytes 1572864 | tf_op jit(solution)/shard_map/all_to_all | solution.py:488
  70.5 12.1 %copy-start.8 = (bf16[4,2,96,384]{3,2,1,0:T(8,128)(2,1)}, bf16[4,2,96,384]{3,2,1,0:T(8,128)(2,1)S(1)}, u32[]{:S(2)}) copy-start(bf16[4,2,96,384]{3,2,1,0:T(8,128)(2,1)S(1)} %collective-permute-done.11.refs_11_) | copy-start | bytes 1769476
  70.5 12.1 %copy-start.9 = (bf16[4,2,96,384]{3,2,1,0:T(8,128)(2,1)}, bf16[4,2,96,384]{3,2,1,0:T(8,128)(2,1)S(1)}, u32[]{:S(2)}) copy-start(bf16[4,2,96,384]{3,2,1,0:T(8,128)(2,1)S(1)} %collective-permute-done.12.refs_13_) | copy-start | bytes 1769476
  70.6 14.7 %collective-permute-start.13 = (bf16[4,2,96,384]{3,2,1,0:T(8,128)(2,1)}, bf16[4,2,96,384]{3,2,1,0:T(8,128)(2,1)S(1)}, u32[]{:S(2)}, u32[]{:S(2)}) collective-permute-start(bf16[4,2,96,384]{3,2,1,0:T(8,128)(2,1)} %collective-permute-done.6.refs_7_), channel_id=1, source_target_pairs={{0,64},{64,128},{128,192},{192,0},{1,65},{65,129},{129,193},{193,1... | collective-permute-start | bytes 1769480 | tf_op jit(solution)/shard_map/ppermute | solution.py:493
  70.6 14.6 %collective-permute-start.14 = (bf16[4,2,96,384]{3,2,1,0:T(8,128)(2,1)S(1)}, bf16[4,2,96,384]{3,2,1,0:T(8,128)(2,1)S(1)}, u32[]{:S(2)}, u32[]{:S(2)}) collective-permute-start(bf16[4,2,96,384]{3,2,1,0:T(8,128)(2,1)S(1)} %collective-permute-done.12.refs_13_), channel_id=1, source_target_pairs={{0,24},{8,0},{16,8},{24,16},{1,25},{9,1},{17,9},{25,17},{2,26},{10... | collective-permute-start | bytes 1769480 | tf_op jit(solution)/shard_map/ppermute | solution.py:494
  85.2 3.9 %copy-start.10 = (bf16[4,2,96,384]{3,2,1,0:T(8,128)(2,1)}, bf16[4,2,96,384]{3,2,1,0:T(8,128)(2,1)S(1)}, u32[]{:S(2)}) copy-start(bf16[4,2,96,384]{3,2,1,0:T(8,128)(2,1)S(1)} %collective-permute-done.13.refs_8_) | copy-start | bytes 1769476
  85.2 3.9 %copy-start.11 = (bf16[4,2,96,384]{3,2,1,0:T(8,128)(2,1)}, bf16[4,2,96,384]{3,2,1,0:T(8,128)(2,1)S(1)}, u32[]{:S(2)}) copy-start(bf16[4,2,96,384]{3,2,1,0:T(8,128)(2,1)S(1)} %collective-permute-done.14.refs_12_) | copy-start | bytes 1769476
  85.2 3.8 %collective-permute-start.15 = (bf16[4,256,384]{2,1,0:T(8,128)(2,1)}, bf16[4,256,384]{2,1,0:T(8,128)(2,1)S(1)}, u32[]{:S(2)}, u32[]{:S(2)}) collective-permute-start(bf16[4,256,384]{2,1,0:T(8,128)(2,1)} %all-to-all-done.2.refs_0_), channel_id=1, source_target_pairs={{0,1},{1,0},{2,3},{3,2},{4,5},{5,4},{6,7},{7,6},{8,9},{9,8},{10,11... | collective-permute-start | bytes 2359304 | tf_op jit(solution)/shard_map/ppermute | solution.py:497
  85.3 16.7 %all-to-all-start.3 = ((bf16[4,256,384]{2,1,0:T(8,128)(2,1)}), bf16[4,256,384]{2,1,0:T(8,128)(2,1)S(1)}, u32[]{:S(2)}, u32[]{:S(2)}) async-start(bf16[4,256,384]{2,1,0:T(8,128)(2,1)} %all-to-all-done.2.refs_0_), calls=%async_computation.3 | async-start | bytes 1572864 | tf_op jit(solution)/shard_map/all_to_all | solution.py:498
  89.1 0.9 copy-start.7
  102.0 3.6 %copy-start.2 = (bf16[4,256,384]{2,1,0:T(8,128)(2,1)}, bf16[4,256,384]{2,1,0:T(8,128)(2,1)S(1)}, u32[]{:S(2)}) copy-start(bf16[4,256,384]{2,1,0:T(8,128)(2,1)S(1)} %all-to-all-done.3) | copy-start | bytes 2359300
  102.0 24.4 %all-to-all-start.4 = ((bf16[4,256,768]{2,1,0:T(8,128)(2,1)}), bf16[4,256,768]{2,1,0:T(8,128)(2,1)S(1)}, u32[]{:S(2)}, u32[]{:S(2)}) async-start(bf16[4,256,768]{2,1,0:T(8,128)(2,1)} %get-tuple-element.87), calls=%async_computation.4 | async-start | bytes 3145728 | tf_op jit(solution)/shard_map/all_to_all | solution.py:514
  105.6 2.4 %collective-permute-start.16 = (bf16[1024,384]{1,0:T(8,128)(2,1)S(1)}, bf16[1024,384]{1,0:T(8,128)(2,1)S(1)}, u32[]{:S(2)}, u32[]{:S(2)}) collective-permute-start(bf16[1024,384]{1,0:T(8,128)(2,1)S(1)} %bitcast.27), channel_id=1, source_target_pairs={{0,1},{1,0},{2,3},{3,2},{4,5},{5,4},{6,7},{7,6},{8,9},{9,8},{10,11... | collective-permute-start | bytes 2359304 | tf_op jit(solution)/shard_map/ppermute | solution.py:513
  108.0 1.1 copy-start.3

commit v6 on v5

--- a/solution.py
+++ b/solution.py
@@ -470,7 +470,7 @@
     mine = sort_captions(assignment, enc_resid)
     mine = lax.all_to_all(mine, ("y", "zl", "x"), 0, 0, tiled=True)
     text_w, gain = fetch(text_in_w, enc_gain.reshape(1, FEAT))
-    mine, text_w, gain, key_pair, value_pair = tie((mine, text_w, gain, key_pair, value_pair))
+    mine, text_w, gain, key_pair = tie((mine, text_w, gain, key_pair))
     send, xg, sq = send_part(core, mine.reshape(CT, FEAT), gain, text_w)
     summed = keep_part(core, xg, sq, text_w, lax.ppermute(send, "c", swap))
 

time: 149 us -> 149 us (level)
  waiting for transfers between devices: 35.3 us -> 38.2 us
  starting transfers between devices: 48 us -> 46.1 us
    all_to_all x1, waiting for transfers between devices: 1.98 us -> 3.52 us  [body(): mine = lax.all_to_all(mine, ('y', 'zl', 'x'), 0, 0, tiled=True)]
    ppermute x1, waiting for transfers between devices: 2.57 us -> 4.09 us  [body(): key_2 = lax.ppermute(key_1, 'y', ring(1))]
    unnamed x32 -> x36, local copies, waits for them, and re-layouts: 5.54 us -> 5.55 us
  transfers between devices with their start and end apart: 22 -> 22, of which waited for: 13 -> 11; matrix products, arithmetic and copies ran while one was open for 2% -> 2% of each run, Pallas kernels for 19% -> 20%
where the time goes in v6:
time: 149 us; the launch traced here: 148 us
  starting transfers between devices  46.1 us (31%)
  waiting for transfers between devices  38.2 us (26%)
  Pallas kernels  35.1 us (24%)
  blocking collectives  18.9 us (13%)
  local copies, waits for them, and re-layouts  7.23 us (5%)
  other arithmetic  1.63 us (1%)
    all_to_all x1, blocking collectives, body(): grad = lax.all_to_all(grad, ('zl', 'x'), 0, 0, tiled=True)  18.9 us
    pallas_call x2, Pallas kernels, image_attention(): pl.pallas_call(functools.partial(image_kernel, block=256, rows=384), grid...  17.1 us
    all_to_all x1, waiting for transfers between devices, body(): cot = lax.all_to_all(cot, 'y', 0, 0, tiled=True)  16.9 us
    pallas_call x1, Pallas kernels, text_side(): pl.pallas_call(text_side_kernel, in_specs=[smem, smem, pl.BlockSpec(memor...  10.8 us
    all_to_all x1, starting transfers between devices, body(): mine = lax.all_to_all(mine, ('y', 'zl', 'x'), 0, 0, tiled=True)  8.67 us
    all_to_all x1, starting transfers between devices, body(): got = lax.all_to_all(summed, 'zh', 0, 0, tiled=True)  7.34 us
    ppermute x6, starting transfers between devices, around(): two, one, three = [lax.ppermute(block, axis, ring(k)) for k in (2, 1, 3)]  7.03 us
    ppermute x4, starting transfers between devices, beside(): return [lax.ppermute(block, axis, ring(k)) for k in (1, 3)]  6.62 us
  transfers between devices with their start and end apart: 22, of which 11 were waited for; matrix products, arithmetic and copies ran while one was open for 2% of the time, Pallas kernels for 20%

profile of v6, /device:TPU:64, one launch (start us, length us, event | category | flops | bytes accessed | tf_op | source)
XLA Modules:
  0.0 148.0 jit_solution(10423027206430941955)
XLA Ops:
  0.6 1.7 %sort_captions.1 = bf16[32,8,512]{2,1,0:T(8,128)(2,1)} custom-call(s32[32]{0:T(128)} %assign_ref.1, bf16[32,8,512]{2,1,0:T(8,128)(2,1)} %x_ref.1), custom_call_target="tpu_custom_call" | custom-call | tf_op jit(solution)/shard_map/sort_captions/pallas_call | solution.py:68
  2.3 8.7 %all-to-all-start = ((bf16[32,8,512]{2,1,0:T(8,128)(2,1)}), bf16[32,8,512]{2,1,0:T(8,128)(2,1)S(1)}, u32[]{:S(2)}, u32[]{:S(2)}) async-start(bf16[32,8,512]{2,1,0:T(8,128)(2,1)} %sort_captions.1), calls=%async_computation | async-start | bytes 524288 | tf_op jit(solution)/shard_map/all_to_all | solution.py:471
  11.0 1.9 %collective-permute-start = (bf16[96,384]{1,0:T(8,128)(2,1)}, bf16[96,384]{1,0:T(8,128)(2,1)S(1)}, u32[]{:S(2)}, u32[]{:S(2)}) collective-permute-start(bf16[96,384]{1,0:T(8,128)(2,1)} %param.15), channel_id=1, source_target_pairs={{0,32},{32,0},{1,33},{33,1},{2,34},{34,2},{3,35},{35,3},{4,36},{36... | collective-permute-start | bytes 221192 | tf_op jit(solution)/shard_map/ppermute | solution.py:467
  12.9 1.9 %copy-done.1 = bf16[512,3072]{1,0:T(8,128)(2,1)S(1)} copy-done((bf16[512,3072]{1,0:T(8,128)(2,1)S(1)}, bf16[512,3072]{1,0:T(8,128)(2,1)}, u32[]{:S(2)}) %copy-start.1) | copy-done | bytes 3145752
  14.8 0.7 copy-done.4
  15.4 0.2 fetch.1
  15.7 1.7 %collective-permute-done = bf16[96,384]{1,0:T(8,128)(2,1)S(1)} collective-permute-done((bf16[96,384]{1,0:T(8,128)(2,1)}, bf16[96,384]{1,0:T(8,128)(2,1)S(1)}, u32[]{:S(2)}, u32[]{:S(2)}) %collective-permute-start) | collective-permute-done | bytes 73760 | tf_op jit(solution)/shard_map/ppermute | solution.py:467
  17.4 3.5 %all-to-all-done = bf16[32,8,512]{2,1,0:T(8,128)(2,1)S(1)} async-done(((bf16[32,8,512]{2,1,0:T(8,128)(2,1)}), bf16[32,8,512]{2,1,0:T(8,128)(2,1)S(1)}, u32[]{:S(2)}, u32[]{:S(2)}) %all-to-all-start) | async-done | bytes 262176 | tf_op jit(solution)/shard_map/all_to_all | solution.py:471
  20.9 1.6 %text_other_half.1 = (bf16[4,272,384]{2,1,0:T(8,128)(2,1)S(1)}, bf16[256,512]{1,0:T(8,128)(2,1)S(1)}, f32[8,256]{1,0:T(8,128)S(1)}) custom-call(s32[1]{0:T(128)} %bitcast.core_ref, bf16[256,512]{1,0:T(8,128)(2,1)S(1)} %bitcast.29, f32[1,512]{1,0:T(1,128)S(1)} %get-tuple-element.48.gain_ref, bf16[512,3072]{1,0:T(8,128)(2,1)S(1)} %get-tuple-element.49.w_ref), custom_call_target="tpu_custom_call" | custom-call | tf_op jit(solution)/shard_map/text_other_half/pallas_call | solution.py:116
  22.6 0.8 collective-permute-start.2
  23.5 1.5 %collective-permute-done.1.got_ref = bf16[4,272,384]{2,1,0:T(8,128)(2,1)S(1)} collective-permute-done((bf16[4,272,384]{2,1,0:T(8,128)(2,1)S(1)}, bf16[4,272,384]{2,1,0:T(8,128)(2,1)S(1)}, u32[]{:S(2)}, u32[]{:S(2)}) %collective-permute-start.1) | collective-permute-done | bytes 835616 | tf_op jit(solution)/shard_map/ppermute | solution.py:475
  25.0 1.4 text_own_half.1
  26.4 0.9 copy-done
  27.3 7.3 %all-to-all-start.1 = ((bf16[4,272,384]{2,1,0:T(8,128)(2,1)}), bf16[4,272,384]{2,1,0:T(8,128)(2,1)S(1)}, u32[]{:S(2)}, u32[]{:S(2)}) async-start(bf16[4,272,384]{2,1,0:T(8,128)(2,1)} %copy-done), calls=%async_computation.1 | async-start | bytes 1671168 | tf_op jit(solution)/shard_map/all_to_all | solution.py:478
  34.7 0.7 collective-permute-start.8
  35.4 0.6 fusion
  36.1 2.0 %collective-permute-start.9 = (bf16[2,96,384]{2,1,0:T(8,128)(2,1)S(1)}, bf16[2,96,384]{2,1,0:T(8,128)(2,1)S(1)}, u32[]{:S(2)}, u32[]{:S(2)}) collective-permute-start(bf16[2,96,384]{2,1,0:T(8,128)(2,1)S(1)} %get-tuple-element.90), channel_id=1, source_target_pairs={{0,128},{64,192},{128,0},{192,64},{1,129},{65,193},{129,1},{193,65... | collective-permute-start | bytes 442376 | tf_op jit(solution)/shard_map/ppermute | solution.py:461
  38.0 1.4 collective-permute-start.10
  39.5 0.8 collective-permute-start.3
  40.3 2.1 %collective-permute-start.4 = (bf16[2,96,384]{2,1,0:T(8,128)(2,1)S(1)}, bf16[2,96,384]{2,1,0:T(8,128)(2,1)S(1)}, u32[]{:S(2)}, u32[]{:S(2)}) collective-permute-start(bf16[2,96,384]{2,1,0:T(8,128)(2,1)S(1)} %get-tuple-element.92), channel_id=1, source_target_pairs={{0,16},{8,24},{16,0},{24,8},{1,17},{9,25},{17,1},{25,9},{2,18},{10... | collective-permute-start | bytes 442376 | tf_op jit(solution)/shard_map/ppermute | solution.py:461
  42.4 2.0 %collective-permute-done.8 = bf16[2,96,384]{2,1,0:T(8,128)(2,1)S(1)} collective-permute-done((bf16[2,96,384]{2,1,0:T(8,128)(2,1)S(1)}, bf16[2,96,384]{2,1,0:T(8,128)(2,1)S(1)}, u32[]{:S(2)}, u32[]{:S(2)}) %collective-permute-start.8) | collective-permute-done | bytes 147488 | tf_op jit(solution)/shard_map/ppermute | solution.py:461
  44.5 0.6 pad_add_fusion.place_ref
  45.1 0.6 collective-permute-done.10
  45.8 1.5 collective-permute-start.11
  47.3 1.8 %collective-permute-start.12 = (bf16[4,2,96,384]{3,2,1,0:T(8,128)(2,1)S(1)}, bf16[4,2,96,384]{3,2,1,0:T(8,128)(2,1)S(1)}, u32[]{:S(2)}, u32[]{:S(2)}) collective-permute-start(bf16[4,2,96,384]{3,2,1,0:T(8,128)(2,1)S(1)} %pad_maximum_fusion.1.refs_10_), channel_id=1, source_target_pairs={{0,24},{8,0},{16,8},{24,16},{1,25},{9,1},{17,9},{25,17},{2,26},{10... | collective-permute-start | bytes 1769480 | tf_op jit(solution)/shard_map/ppermute | solution.py:465
  49.1 2.0 %collective-permute-done.5 = bf16[2,96,384]{2,1,0:T(8,128)(2,1)S(1)} collective-permute-done((bf16[2,96,384]{2,1,0:T(8,128)(2,1)S(1)}, bf16[2,96,384]{2,1,0:T(8,128)(2,1)S(1)}, u32[]{:S(2)}, u32[]{:S(2)}) %collective-permute-start.5) | collective-permute-done | bytes 147488 | tf_op jit(solution)/shard_map/ppermute | solution.py:461
  51.3 3.2 %collective-permute-start.7 = (bf16[4,2,96,384]{3,2,1,0:T(8,128)(2,1)S(1)}, bf16[4,2,96,384]{3,2,1,0:T(8,128)(2,1)}, u32[]{:S(2)}, u32[]{:S(2)}) collective-permute-start(bf16[4,2,96,384]{3,2,1,0:T(8,128)(2,1)S(1)} %pad_maximum_fusion.refs_6_), channel_id=1, source_target_pairs={{0,192},{64,0},{128,64},{192,128},{1,193},{65,1},{129,65},{193,129... | collective-permute-start | bytes 1769480 | tf_op jit(solution)/shard_map/ppermute | solution.py:465
  54.5 2.2 %all-to-all-done.1.got_ref = bf16[4,272,384]{2,1,0:T(8,128)(2,1)S(1)} async-done(((bf16[4,272,384]{2,1,0:T(8,128)(2,1)}), bf16[4,272,384]{2,1,0:T(8,128)(2,1)S(1)}, u32[]{:S(2)}, u32[]{:S(2)}) %all-to-all-start.1) | async-done | bytes 835616 | tf_op jit(solution)/shard_map/all_to_all | solution.py:478
  56.8 0.2 finish_text.1
  57.0 0.9 broadcast_in_dim.10
  57.9 5.0 %all-to-all-start.2 = ((bf16[4,256,384]{2,1,0:T(8,128)(2,1)}), bf16[4,256,384]{2,1,0:T(8,128)(2,1)}, u32[]{:S(2)}, u32[]{:S(2)}) async-start(bf16[4,256,384]{2,1,0:T(8,128)(2,1)} %broadcast_in_dim.10), calls=%async_computation.2 | async-start | bytes 1572864 | tf_op jit(solution)/shard_map/all_to_all | solution.py:488
  62.9 6.6 %image_attention.2 = (f32[768,384]{1,0:T(8,128)}, f32[768,384]{1,0:T(8,128)}) custom-call(bf16[768,384]{1,0:T(8,128)(2,1)} %refs_2_.1, bf16[4096,384]{1,0:T(8,128)(2,1)} %k_ref.3, bf16[4096,384]{1,0:T(8,128)(2,1)} %v_ref.3), custom_call_target="tpu_custom_call" | custom-call | flops 1 | bytes 1 | tf_op jit(solution)/shard_map/image_attention/pallas_call | solution.py:212
  69.6 1.1 collective-permute-start.14
  70.7 10.6 %image_attention.3 = (f32[768,384]{1,0:T(8,128)}, f32[768,384]{1,0:T(8,128)}) custom-call(bf16[768,384]{1,0:T(8,128)(2,1)} %refs_2_.1, bf16[4096,384]{1,0:T(8,128)(2,1)} %k_ref.3, bf16[4096,384]{1,0:T(8,128)(2,1)} %v_ref.3, f32[768,384]{1,0:T(8,128)} %get-tuple-element.68.refs_0_, ...), custom_call_target="tpu_custom_call", output_to_operand_aliasing={{0}: (3, {}), {1}: (4, {})} | custom-call | flops 1 | bytes 1 | tf_op jit(solution)/shard_map/image_attention/pallas_call | solution.py:212
  81.3 4.1 %collective-permute-done.13.refs_8_ = bf16[4,2,96,384]{3,2,1,0:T(8,128)(2,1)S(1)} collective-permute-done((bf16[4,2,96,384]{3,2,1,0:T(8,128)(2,1)}, bf16[4,2,96,384]{3,2,1,0:T(8,128)(2,1)S(1)}, u32[]{:S(2)}, u32[]{:S(2)}) %collective-permute-start.13) | collective-permute-done | bytes 589856 | tf_op jit(solution)/shard_map/ppermute | solution.py:493
  85.5 3.7 %all-to-all-start.3 = ((bf16[4,256,384]{2,1,0:T(8,128)(2,1)}), bf16[4,256,384]{2,1,0:T(8,128)(2,1)S(1)}, u32[]{:S(2)}, u32[]{:S(2)}) async-start(bf16[4,256,384]{2,1,0:T(8,128)(2,1)} %all-to-all-done.2.refs_0_), calls=%async_computation.3 | async-start | bytes 1572864 | tf_op jit(solution)/shard_map/all_to_all | solution.py:498
  89.3 0.9 copy-done.7
  90.2 10.8 %text_side.1 = (f32[768,384]{1,0:T(8,128)}, bf16[4,256,768]{2,1,0:T(8,128)(2,1)}) custom-call(s32[1]{0:T(128)} %bitcast.3.length_ref, s32[4]{0:T(128)} %pad_add_fusion.place_ref, f32[1,128]{1,0:T(1,128)} %bitcast.41, bf16[4,256,384]{2,1,0:T(8,128)(2,1)} %all-to-all-done.2.refs_0_, bf16[4,256,384]{2,1,0:T(8,128)(2,1)} %copy-done.7, bf16[768,384]{1,0:T(8,128)(2,1)} %refs_2_.1, ...), custom_call_target="tpu_custom_call" | custom-call | tf_op jit(solution)/shard_map/text_side/pallas_call | solution.py:367
  101.0 1.2 all-to-all-done.3
  102.2 3.6 %all-to-all-start.4 = ((bf16[4,256,768]{2,1,0:T(8,128)(2,1)}), bf16[4,256,768]{2,1,0:T(8,128)(2,1)S(1)}, u32[]{:S(2)}, u32[]{:S(2)}) async-start(bf16[4,256,768]{2,1,0:T(8,128)(2,1)} %get-tuple-element.83), calls=%async_computation.4 | async-start | bytes 3145728 | tf_op jit(solution)/shard_map/all_to_all | solution.py:514
  105.9 2.3 %collective-permute-done.16.other_ref = bf16[1024,384]{1,0:T(8,128)(2,1)S(1)} collective-permute-done((bf16[1024,384]{1,0:T(8,128)(2,1)S(1)}, bf16[1024,384]{1,0:T(8,128)(2,1)S(1)}, u32[]{:S(2)}, u32[]{:S(2)}) %collective-permute-start.16) | collective-permute-done | bytes 786464 | tf_op jit(solution)/shard_map/ppermute | solution.py:513
  108.1 1.1 copy-done.3
  109.3 0.5 turn_text.1.text_ref
  109.8 16.9 %all-to-all-done.4 = bf16[4,256,768]{2,1,0:T(8,128)(2,1)S(1)} async-done(((bf16[4,256,768]{2,1,0:T(8,128)(2,1)}), bf16[4,256,768]{2,1,0:T(8,128)(2,1)S(1)}, u32[]{:S(2)}, u32[]{:S(2)}) %all-to-all-start.4) | async-done | bytes 1572896 | tf_op jit(solution)/shard_map/all_to_all | solution.py:514
  126.7 1.6 %gradient.1 = bf16[768,768]{1,0:T(8,128)(2,1)S(1)} custom-call(bf16[768,1024]{1,0:T(8,128)(2,1)S(1)} %turn_text.1.text_ref, bf16[1024,768]{1,0:T(8,128)(2,1)S(1)} %bitcast.25), custom_call_target="tpu_custom_call" | custom-call | tf_op jit(solution)/shard_map/gradient/pallas_call | solution.py:416
  128.2 18.9 %all_to_all.30 = bf16[8,96,768]{2,1,0:T(8,128)(2,1)S(1)} all-to-all(bf16[8,96,768]{2,1,0:T(8,128)(2,1)S(1)} %bitcast.26), channel_id=1, replica_groups=mesh['y'=4,'zl'=2,'x'=4,'zh'=4,'c'=2] {'zl','x'}, dimensions={0} | all-to-all | bytes 2359296 | tf_op jit(solution)/shard_map/all_to_all | solution.py:519
  147.1 0.2 convert_reduce_fusion
  147.3 0.7 fusion.3
  (52 shorter events, 0.8 us)
Async XLA Ops:
  2.3 18.6 %all-to-all-start = ((bf16[32,8,512]{2,1,0:T(8,128)(2,1)}), bf16[32,8,512]{2,1,0:T(8,128)(2,1)S(1)}, u32[]{:S(2)}, u32[]{:S(2)}) async-start(bf16[32,8,512]{2,1,0:T(8,128)(2,1)} %sort_captions.1), calls=%async_computation | async-start | bytes 524288 | tf_op jit(solution)/shard_map/all_to_all | solution.py:471
  11.0 6.4 %collective-permute-start = (bf16[96,384]{1,0:T(8,128)(2,1)}, bf16[96,384]{1,0:T(8,128)(2,1)S(1)}, u32[]{:S(2)}, u32[]{:S(2)}) collective-permute-start(bf16[96,384]{1,0:T(8,128)(2,1)} %param.15), channel_id=1, source_target_pairs={{0,32},{32,0},{1,33},{33,1},{2,34},{34,2},{3,35},{35,3},{4,36},{36... | collective-permute-start | bytes 221192 | tf_op jit(solution)/shard_map/ppermute | solution.py:467
  12.9 1.9 %copy-start.1 = (bf16[512,3072]{1,0:T(8,128)(2,1)S(1)}, bf16[512,3072]{1,0:T(8,128)(2,1)}, u32[]{:S(2)}) copy-start(bf16[512,3072]{1,0:T(8,128)(2,1)} %refs_0_.1) | copy-start | bytes 9437188
  14.8 0.7 copy-start.4
  17.4 3.5 %copy-start.14 = (bf16[96,384]{1,0:T(8,128)(2,1)}, bf16[96,384]{1,0:T(8,128)(2,1)S(1)}, u32[]{:S(2)}) copy-start(bf16[96,384]{1,0:T(8,128)(2,1)S(1)} %collective-permute-done) | copy-start | bytes 221188
  20.9 1.7 %copy-start.12 = (bf16[96,384]{1,0:T(8,128)(2,1)S(1)}, bf16[96,384]{1,0:T(8,128)(2,1)}, u32[]{:S(2)}) copy-start(bf16[96,384]{1,0:T(8,128)(2,1)} %param.16) | copy-start | bytes 221188
  22.5 2.4 %collective-permute-start.1 = (bf16[4,272,384]{2,1,0:T(8,128)(2,1)S(1)}, bf16[4,272,384]{2,1,0:T(8,128)(2,1)S(1)}, u32[]{:S(2)}, u32[]{:S(2)}) collective-permute-start(bf16[4,272,384]{2,1,0:T(8,128)(2,1)S(1)} %get-tuple-element.52), channel_id=1, source_target_pairs={{0,1},{1,0},{2,3},{3,2},{4,5},{5,4},{6,7},{7,6},{8,9},{9,8},{10,11... | collective-permute-start | bytes 2506760 | tf_op jit(solution)/shard_map/ppermute | solution.py:475
  22.6 4.7 %collective-permute-start.2 = (bf16[96,384]{1,0:T(8,128)(2,1)S(1)}, bf16[96,384]{1,0:T(8,128)(2,1)S(1)}, u32[]{:S(2)}, u32[]{:S(2)}) collective-permute-start(bf16[96,384]{1,0:T(8,128)(2,1)S(1)} %copy-done.12), channel_id=1, source_target_pairs={{0,32},{32,0},{1,33},{33,1},{2,34},{34,2},{3,35},{35,3},{4,36},{36... | collective-permute-start | bytes 221192 | tf_op jit(solution)/shard_map/ppermute | solution.py:468
  26.4 0.9 copy-start
  27.3 8.1 %copy-start.16 = (s32[32]{0:T(128)S(1)}, s32[32]{0:T(128)}, u32[]{:S(2)}) copy-start(s32[32]{0:T(128)} %assign_ref.1) | copy-start | bytes 388
  27.3 8.1 %copy-start.17 = (s32[32]{0:T(128)S(1)}, s32[32]{0:T(128)}, u32[]{:S(2)}) copy-start(s32[32]{0:T(128)} %param.22) | copy-start | bytes 388
  27.3 12.2 %copy-start.13 = (bf16[96,384]{1,0:T(8,128)(2,1)S(1)}, bf16[96,384]{1,0:T(8,128)(2,1)}, u32[]{:S(2)}) copy-start(bf16[96,384]{1,0:T(8,128)(2,1)} %param.15) | copy-start | bytes 221188
  27.3 12.2 %copy-start.15 = (bf16[96,384]{1,0:T(8,128)(2,1)S(1)}, bf16[96,384]{1,0:T(8,128)(2,1)}, u32[]{:S(2)}) copy-start(bf16[96,384]{1,0:T(8,128)(2,1)} %copy-done.14) | copy-start | bytes 221188
  27.3 29.4 %all-to-all-start.1 = ((bf16[4,272,384]{2,1,0:T(8,128)(2,1)}), bf16[4,272,384]{2,1,0:T(8,128)(2,1)S(1)}, u32[]{:S(2)}, u32[]{:S(2)}) async-start(bf16[4,272,384]{2,1,0:T(8,128)(2,1)} %copy-done), calls=%async_computation.1 | async-start | bytes 1671168 | tf_op jit(solution)/shard_map/all_to_all | solution.py:478
  34.7 9.8 %collective-permute-start.8 = (bf16[2,96,384]{2,1,0:T(8,128)(2,1)S(1)}, bf16[2,96,384]{2,1,0:T(8,128)(2,1)S(1)}, u32[]{:S(2)}, u32[]{:S(2)}) collective-permute-start(bf16[2,96,384]{2,1,0:T(8,128)(2,1)S(1)} %get-tuple-element.90), channel_id=1, source_target_pairs={{0,64},{64,128},{128,192},{192,0},{1,65},{65,129},{129,193},{193,1... | collective-permute-start | bytes 442376 | tf_op jit(solution)/shard_map/ppermute | solution.py:461
  36.1 9.0 %collective-permute-start.9 = (bf16[2,96,384]{2,1,0:T(8,128)(2,1)S(1)}, bf16[2,96,384]{2,1,0:T(8,128)(2,1)S(1)}, u32[]{:S(2)}, u32[]{:S(2)}) collective-permute-start(bf16[2,96,384]{2,1,0:T(8,128)(2,1)S(1)} %get-tuple-element.90), channel_id=1, source_target_pairs={{0,128},{64,192},{128,0},{192,64},{1,129},{65,193},{129,1},{193,65... | collective-permute-start | bytes 442376 | tf_op jit(solution)/shard_map/ppermute | solution.py:461
  38.0 7.7 %collective-permute-start.10 = (bf16[2,96,384]{2,1,0:T(8,128)(2,1)S(1)}, bf16[2,96,384]{2,1,0:T(8,128)(2,1)S(1)}, u32[]{:S(2)}, u32[]{:S(2)}) collective-permute-start(bf16[2,96,384]{2,1,0:T(8,128)(2,1)S(1)} %get-tuple-element.90), channel_id=1, source_target_pairs={{0,192},{64,0},{128,64},{192,128},{1,193},{65,1},{129,65},{193,129... | collective-permute-start | bytes 442376 | tf_op jit(solution)/shard_map/ppermute | solution.py:461
  39.5 9.6 %collective-permute-start.3 = (bf16[2,96,384]{2,1,0:T(8,128)(2,1)S(1)}, bf16[2,96,384]{2,1,0:T(8,128)(2,1)S(1)}, u32[]{:S(2)}, u32[]{:S(2)}) collective-permute-start(bf16[2,96,384]{2,1,0:T(8,128)(2,1)S(1)} %get-tuple-element.92), channel_id=1, source_target_pairs={{0,8},{8,16},{16,24},{24,0},{1,9},{9,17},{17,25},{25,1},{2,10},{10... | collective-permute-start | bytes 442376 | tf_op jit(solution)/shard_map/ppermute | solution.py:461
  40.3 8.8 %collective-permute-start.4 = (bf16[2,96,384]{2,1,0:T(8,128)(2,1)S(1)}, bf16[2,96,384]{2,1,0:T(8,128)(2,1)S(1)}, u32[]{:S(2)}, u32[]{:S(2)}) collective-permute-start(bf16[2,96,384]{2,1,0:T(8,128)(2,1)S(1)} %get-tuple-element.92), channel_id=1, source_target_pairs={{0,16},{8,24},{16,0},{24,8},{1,17},{9,25},{17,1},{25,9},{2,18},{10... | collective-permute-start | bytes 442376 | tf_op jit(solution)/shard_map/ppermute | solution.py:461
  44.5 6.6 %collective-permute-start.5 = (bf16[2,96,384]{2,1,0:T(8,128)(2,1)S(1)}, bf16[2,96,384]{2,1,0:T(8,128)(2,1)S(1)}, u32[]{:S(2)}, u32[]{:S(2)}) collective-permute-start(bf16[2,96,384]{2,1,0:T(8,128)(2,1)S(1)} %get-tuple-element.92), channel_id=1, source_target_pairs={{0,24},{8,0},{16,8},{24,16},{1,25},{9,1},{17,9},{25,17},{2,26},{10... | collective-permute-start | bytes 442376 | tf_op jit(solution)/shard_map/ppermute | solution.py:461
  45.8 12.1 %copy-start.5 = (bf16[4,2,96,384]{3,2,1,0:T(8,128)(2,1)}, bf16[4,2,96,384]{3,2,1,0:T(8,128)(2,1)S(1)}, u32[]{:S(2)}) copy-start(bf16[4,2,96,384]{3,2,1,0:T(8,128)(2,1)S(1)} %pad_maximum_fusion.1.refs_10_) | copy-start | bytes 1769476
  45.8 23.7 %collective-permute-start.11 = (bf16[4,2,96,384]{3,2,1,0:T(8,128)(2,1)S(1)}, bf16[4,2,96,384]{3,2,1,0:T(8,128)(2,1)S(1)}, u32[]{:S(2)}, u32[]{:S(2)}) collective-permute-start(bf16[4,2,96,384]{3,2,1,0:T(8,128)(2,1)S(1)} %pad_maximum_fusion.1.refs_10_), channel_id=1, source_target_pairs={{0,8},{8,16},{16,24},{24,0},{1,9},{9,17},{17,25},{25,1},{2,10},{10... | collective-permute-start | bytes 1769480 | tf_op jit(solution)/shard_map/ppermute | solution.py:465
  47.3 22.2 %collective-permute-start.12 = (bf16[4,2,96,384]{3,2,1,0:T(8,128)(2,1)S(1)}, bf16[4,2,96,384]{3,2,1,0:T(8,128)(2,1)S(1)}, u32[]{:S(2)}, u32[]{:S(2)}) collective-permute-start(bf16[4,2,96,384]{3,2,1,0:T(8,128)(2,1)S(1)} %pad_maximum_fusion.1.refs_10_), channel_id=1, source_target_pairs={{0,24},{8,0},{16,8},{24,16},{1,25},{9,1},{17,9},{25,17},{2,26},{10... | collective-permute-start | bytes 1769480 | tf_op jit(solution)/shard_map/ppermute | solution.py:465
  51.2 6.7 %copy-start.6 = (bf16[4,2,96,384]{3,2,1,0:T(8,128)(2,1)}, bf16[4,2,96,384]{3,2,1,0:T(8,128)(2,1)S(1)}, u32[]{:S(2)}) copy-start(bf16[4,2,96,384]{3,2,1,0:T(8,128)(2,1)S(1)} %pad_maximum_fusion.refs_6_) | copy-start | bytes 1769476
  51.2 18.3 %collective-permute-start.6 = (bf16[4,2,96,384]{3,2,1,0:T(8,128)(2,1)S(1)}, bf16[4,2,96,384]{3,2,1,0:T(8,128)(2,1)}, u32[]{:S(2)}, u32[]{:S(2)}) collective-permute-start(bf16[4,2,96,384]{3,2,1,0:T(8,128)(2,1)S(1)} %pad_maximum_fusion.refs_6_), channel_id=1, source_target_pairs={{0,64},{64,128},{128,192},{192,0},{1,65},{65,129},{129,193},{193,1... | collective-permute-start | bytes 1769480 | tf_op jit(solution)/shard_map/ppermute | solution.py:465
  51.3 18.2 %collective-permute-start.7 = (bf16[4,2,96,384]{3,2,1,0:T(8,128)(2,1)S(1)}, bf16[4,2,96,384]{3,2,1,0:T(8,128)(2,1)}, u32[]{:S(2)}, u32[]{:S(2)}) collective-permute-start(bf16[4,2,96,384]{3,2,1,0:T(8,128)(2,1)S(1)} %pad_maximum_fusion.refs_6_), channel_id=1, source_target_pairs={{0,192},{64,0},{128,64},{192,128},{1,193},{65,1},{129,65},{193,129... | collective-permute-start | bytes 1769480 | tf_op jit(solution)/shard_map/ppermute | solution.py:465
  57.9 27.5 %all-to-all-start.2 = ((bf16[4,256,384]{2,1,0:T(8,128)(2,1)}), bf16[4,256,384]{2,1,0:T(8,128)(2,1)}, u32[]{:S(2)}, u32[]{:S(2)}) async-start(bf16[4,256,384]{2,1,0:T(8,128)(2,1)} %broadcast_in_dim.10), calls=%async_computation.2 | async-start | bytes 1572864 | tf_op jit(solution)/shard_map/all_to_all | solution.py:488
  69.5 11.8 %copy-start.8 = (bf16[4,2,96,384]{3,2,1,0:T(8,128)(2,1)}, bf16[4,2,96,384]{3,2,1,0:T(8,128)(2,1)S(1)}, u32[]{:S(2)}) copy-start(bf16[4,2,96,384]{3,2,1,0:T(8,128)(2,1)S(1)} %collective-permute-done.11.refs_11_) | copy-start | bytes 1769476
  69.5 11.8 %copy-start.9 = (bf16[4,2,96,384]{3,2,1,0:T(8,128)(2,1)}, bf16[4,2,96,384]{3,2,1,0:T(8,128)(2,1)S(1)}, u32[]{:S(2)}) copy-start(bf16[4,2,96,384]{3,2,1,0:T(8,128)(2,1)S(1)} %collective-permute-done.12.refs_13_) | copy-start | bytes 1769476
  69.5 15.9 %collective-permute-start.13 = (bf16[4,2,96,384]{3,2,1,0:T(8,128)(2,1)}, bf16[4,2,96,384]{3,2,1,0:T(8,128)(2,1)S(1)}, u32[]{:S(2)}, u32[]{:S(2)}) collective-permute-start(bf16[4,2,96,384]{3,2,1,0:T(8,128)(2,1)} %collective-permute-done.6.refs_7_), channel_id=1, source_target_pairs={{0,64},{64,128},{128,192},{192,0},{1,65},{65,129},{129,193},{193,1... | collective-permute-start | bytes 1769480 | tf_op jit(solution)/shard_map/ppermute | solution.py:493
  69.6 15.8 %collective-permute-start.14 = (bf16[4,2,96,384]{3,2,1,0:T(8,128)(2,1)S(1)}, bf16[4,2,96,384]{3,2,1,0:T(8,128)(2,1)S(1)}, u32[]{:S(2)}, u32[]{:S(2)}) collective-permute-start(bf16[4,2,96,384]{3,2,1,0:T(8,128)(2,1)S(1)} %collective-permute-done.12.refs_13_), channel_id=1, source_target_pairs={{0,24},{8,0},{16,8},{24,16},{1,25},{9,1},{17,9},{25,17},{2,26},{10... | collective-permute-start | bytes 1769480 | tf_op jit(solution)/shard_map/ppermute | solution.py:494
  85.4 3.9 %copy-start.10 = (bf16[4,2,96,384]{3,2,1,0:T(8,128)(2,1)}, bf16[4,2,96,384]{3,2,1,0:T(8,128)(2,1)S(1)}, u32[]{:S(2)}) copy-start(bf16[4,2,96,384]{3,2,1,0:T(8,128)(2,1)S(1)} %collective-permute-done.13.refs_8_) | copy-start | bytes 1769476
  85.4 3.9 %copy-start.11 = (bf16[4,2,96,384]{3,2,1,0:T(8,128)(2,1)}, bf16[4,2,96,384]{3,2,1,0:T(8,128)(2,1)S(1)}, u32[]{:S(2)}) copy-start(bf16[4,2,96,384]{3,2,1,0:T(8,128)(2,1)S(1)} %collective-permute-done.14.refs_12_) | copy-start | bytes 1769476
  85.4 3.8 %collective-permute-start.15 = (bf16[4,256,384]{2,1,0:T(8,128)(2,1)}, bf16[4,256,384]{2,1,0:T(8,128)(2,1)S(1)}, u32[]{:S(2)}, u32[]{:S(2)}) collective-permute-start(bf16[4,256,384]{2,1,0:T(8,128)(2,1)} %all-to-all-done.2.refs_0_), channel_id=1, source_target_pairs={{0,1},{1,0},{2,3},{3,2},{4,5},{5,4},{6,7},{7,6},{8,9},{9,8},{10,11... | collective-permute-start | bytes 2359304 | tf_op jit(solution)/shard_map/ppermute | solution.py:497
  85.5 16.7 %all-to-all-start.3 = ((bf16[4,256,384]{2,1,0:T(8,128)(2,1)}), bf16[4,256,384]{2,1,0:T(8,128)(2,1)S(1)}, u32[]{:S(2)}, u32[]{:S(2)}) async-start(bf16[4,256,384]{2,1,0:T(8,128)(2,1)} %all-to-all-done.2.refs_0_), calls=%async_computation.3 | async-start | bytes 1572864 | tf_op jit(solution)/shard_map/all_to_all | solution.py:498
  89.2 0.9 copy-start.7
  102.2 3.6 %copy-start.2 = (bf16[4,256,384]{2,1,0:T(8,128)(2,1)}, bf16[4,256,384]{2,1,0:T(8,128)(2,1)S(1)}, u32[]{:S(2)}) copy-start(bf16[4,256,384]{2,1,0:T(8,128)(2,1)S(1)} %all-to-all-done.3) | copy-start | bytes 2359300
  102.2 24.5 %all-to-all-start.4 = ((bf16[4,256,768]{2,1,0:T(8,128)(2,1)}), bf16[4,256,768]{2,1,0:T(8,128)(2,1)S(1)}, u32[]{:S(2)}, u32[]{:S(2)}) async-start(bf16[4,256,768]{2,1,0:T(8,128)(2,1)} %get-tuple-element.83), calls=%async_computation.4 | async-start | bytes 3145728 | tf_op jit(solution)/shard_map/all_to_all | solution.py:514
  105.8 2.4 %collective-permute-start.16 = (bf16[1024,384]{1,0:T(8,128)(2,1)S(1)}, bf16[1024,384]{1,0:T(8,128)(2,1)S(1)}, u32[]{:S(2)}, u32[]{:S(2)}) collective-permute-start(bf16[1024,384]{1,0:T(8,128)(2,1)S(1)} %bitcast.27), channel_id=1, source_target_pairs={{0,1},{1,0},{2,3},{3,2},{4,5},{5,4},{6,7},{7,6},{8,9},{9,8},{10,11... | collective-permute-start | bytes 2359304 | tf_op jit(solution)/shard_map/ppermute | solution.py:513
  108.1 1.1 copy-start.3
